TPU v7x, 512 devices: a whole 4x4x16 slice. The times are simulated.
512 devices in a mesh: lat: 32 (over z_lo, x), lon: 8 (over y, z_hi), tp: 2 (over core).
Axes of the slice: x: 4, y: 4, z: 16 (z_hi: 2, z_lo: 8; z = z_hi * 8 + z_lo), core: 2. Of those that a mesh axis runs over, the one named last changes fastest.
Arguments:
- fine_tokens: bfloat16 [2, 384, 192, 512], P(None, 'lat', 'lon'), may hold values from -6 to 6
- attn_gain: float32 [512], replicated, may hold values from 0.1 to 1.9
- fine_qkv: bfloat16 [512, 3, 512], P('lat', None, 'tp'), may hold values from -4 to 4
- fine_proj: bfloat16 [512, 512], P(None, 'lat'), may hold values from -0.25 to 0.25
- merge_gain: float32 [2048], replicated, may hold values from 0.1 to 1.9
- merge_weight: bfloat16 [2048, 1024], P('lat', 'tp'), may hold values from -0.125 to 0.125
- coarse_gain: float32 [1024], replicated, may hold values from 0.1 to 1.9
- coarse_qkv: bfloat16 [1024, 3, 1024], P('lat', None, 'tp'), may hold values from -4 to 4
- coarse_proj: bfloat16 [1024, 1024], P('tp', 'lat'), may hold values from -0.1875 to 0.1875
- split_weight: bfloat16 [1024, 4, 512], P('lat', None, 'tp'), may hold values from -0.1875 to 0.1875
- split_gain: float32 [512], replicated, may hold values from 0.1 to 1.9
Outputs:
- restored: bfloat16 [2, 384, 192, 512], P(None, 'lat', 'lon', 'tp')
All inputs are finite; a program needn't handle non-finite values.
Results may differ from a plain program's by a relative error of at most 0.013.
Values may be sent and summed in bfloat16 or wider, within the bound.
No kernel may reach another device: no remote copies, remote signals or barrier semaphores. Data moves between devices by JAX's collectives and lax.ppermute only.
A program may use at most 64 MiB of HBM per device.

v0:
```python
import jax
import jax.numpy as jnp
from jax import lax
from jax.sharding import PartitionSpec as P

HEAD = 64
WIN_LAT = 6
WIN_LON = 12


EPSILON = 1e-05


def passed_along(value, axis, by):
    peers = lax.axis_size(axis)
    return lax.ppermute(value, axis, [(i, (i + by) % peers) for i in range(peers)])


def layer_norm(values, gain_row):
    average = jnp.mean(values, axis=-1, keepdims=True)
    centred = values - average
    spread = jnp.mean(centred * centred, axis=-1, keepdims=True)
    return centred * lax.rsqrt(spread + EPSILON) * gain_row


def seam_labels(global_rows, lat_total, rim_rows):
    return jnp.where(
        global_rows >= lat_total - rim_rows, 1, jnp.where(global_rows < rim_rows, 2, 0)
    ).astype(jnp.int32)


def window_mix(packed, head_count, row_labels):
    levels, row_count, col_count, channels = packed.shape
    head_size = channels // (3 * head_count)
    window_rows = row_count // WIN_LAT
    window_cols = col_count // WIN_LON
    window_size = levels * WIN_LAT * WIN_LON
    grouped = packed.reshape(
        levels, window_rows, WIN_LAT, window_cols, WIN_LON, 3, head_count, head_size
    )
    grouped = grouped.transpose(1, 3, 0, 2, 4, 5, 6, 7).reshape(
        window_rows * window_cols, window_size, 3, head_count, head_size
    )
    scores = jnp.einsum(
        "wqhd,wkhd->whqk", grouped[:, :, 0], grouped[:, :, 1], preferred_element_type=jnp.float32
    ) * head_size ** (-0.5)
    if row_labels is not None:
        token_labels = jnp.broadcast_to(
            row_labels.reshape(window_rows, 1, 1, WIN_LAT, 1),
            (window_rows, window_cols, levels, WIN_LAT, WIN_LON),
        ).reshape(window_rows * window_cols, window_size)
        allowed = token_labels[:, :, None] == token_labels[:, None, :]
        scores = jnp.where(allowed[:, None], scores, -1e30)
    row_maximum = jnp.max(scores, axis=-1, keepdims=True)
    weights = jnp.exp(scores - row_maximum)
    weights = (weights / jnp.sum(weights, axis=-1, keepdims=True)).astype(jnp.bfloat16)
    window_out = jnp.einsum(
        "whqk,wkhd->wqhd", weights, grouped[:, :, 2], preferred_element_type=jnp.float32
    ).astype(jnp.bfloat16)
    window_out = window_out.reshape(
        window_rows, window_cols, levels, WIN_LAT, WIN_LON, head_count * head_size
    ).transpose(2, 0, 3, 1, 4, 5)
    return window_out.reshape(levels, row_count, col_count, head_count * head_size)


def fold_rows(source, fragment):
    return jnp.dot(
        source, fragment.reshape(fragment.shape[0], -1), preferred_element_type=jnp.float32
    )


def project_with(left_side, fragment):
    return jnp.dot(left_side, fragment, preferred_element_type=jnp.float32)


def body(
    fine_tokens,
    attn_gain,
    fine_qkv,
    fine_proj,
    merge_gain,
    merge_weight,
    coarse_gain,
    coarse_qkv,
    coarse_proj,
    split_weight,
    split_gain,
):
    levels, row_count, col_count, features = fine_tokens.shape
    lat_total = row_count * lax.axis_size("lat")
    row_first = lax.axis_index("lat") * row_count
    rim_rows = WIN_LAT // 2
    rim_cols = WIN_LON // 2
    flat_tokens = fine_tokens.reshape(-1, features)
    normed = layer_norm(flat_tokens.astype(jnp.float32), attn_gain).astype(jnp.bfloat16)
    fine_heads = fine_qkv.shape[2] // HEAD
    packed_width = 3 * fine_qkv.shape[2]
    packed = fold_rows(normed, lax.all_gather(fine_qkv, "lat", axis=0, tiled=True))
    packed = packed.astype(jnp.bfloat16).reshape(levels, row_count, col_count, packed_width)
    arriving = passed_along(packed[:, :, :rim_cols], "lon", -1)
    extended = jnp.concatenate([packed[:, :, rim_cols:], arriving], axis=2)
    arriving = passed_along(extended[:, :rim_rows], "lat", -1)
    extended = jnp.concatenate([extended[:, rim_rows:], arriving], axis=1)
    global_rows = (row_first + rim_rows + jnp.arange(row_count, dtype=jnp.int32)) % lat_total
    window_out = window_mix(extended, fine_heads, seam_labels(global_rows, lat_total, rim_rows))
    returning = passed_along(window_out[:, row_count - rim_rows :], "lat", 1)
    window_out = jnp.concatenate([returning, window_out[:, : row_count - rim_rows]], axis=1)
    returning = passed_along(window_out[:, :, col_count - rim_cols :], "lon", 1)
    window_out = jnp.concatenate([returning, window_out[:, :, : col_count - rim_cols]], axis=2)
    all_heads = lax.all_gather(window_out, "tp", axis=3, tiled=True).reshape(-1, fine_proj.shape[0])
    attended = project_with(all_heads, lax.all_gather(fine_proj, "lat", axis=1, tiled=True))
    residual = (flat_tokens.astype(jnp.float32) + attended).astype(jnp.bfloat16)
    half_rows = row_count // 2
    half_cols = col_count // 2
    quartets = (
        residual.reshape(levels, half_rows, 2, half_cols, 2, features)
        .transpose(0, 1, 3, 2, 4, 5)
        .reshape(-1, 4 * features)
    )
    merged_in = layer_norm(quartets.astype(jnp.float32), merge_gain).astype(jnp.bfloat16)
    coarse_rows = merged_in.shape[0]
    coarse_half = fold_rows(
        merged_in, lax.all_gather(merge_weight, "lat", axis=0, tiled=True)
    ).astype(jnp.bfloat16)
    coarse_full = lax.all_gather(coarse_half, "tp", axis=1, tiled=True)
    coarse_normed = layer_norm(coarse_full.astype(jnp.float32), coarse_gain).astype(jnp.bfloat16)
    coarse_packed = fold_rows(
        coarse_normed, lax.all_gather(coarse_qkv, "lat", axis=0, tiled=True)
    ).astype(jnp.bfloat16)
    heads_here = coarse_qkv.shape[2] // HEAD
    coarse_mixed = window_mix(
        coarse_packed.reshape(levels, half_rows, half_cols, -1), heads_here, None
    ).reshape(coarse_rows, -1)
    partial_value = project_with(
        coarse_mixed, lax.all_gather(coarse_proj, "lat", axis=1, tiled=True)
    )
    own_share = lax.psum_scatter(
        partial_value.astype(jnp.bfloat16), "tp", scatter_dimension=1, tiled=True
    ).astype(jnp.float32)
    coarse_own = (coarse_half.astype(jnp.float32) + own_share).astype(jnp.bfloat16)
    coarse_out = lax.all_gather(coarse_own, "tp", axis=1, tiled=True)
    feature_half = split_weight.shape[2]
    expanded = fold_rows(coarse_out, lax.all_gather(split_weight, "lat", axis=0, tiled=True))
    expanded = expanded.reshape(coarse_rows, 4, feature_half)
    first_sum, second_sum = lax.psum(
        (jnp.sum(expanded, axis=-1), jnp.sum(expanded * expanded, axis=-1)), "tp"
    )
    average = first_sum / features
    spread = second_sum / features - average * average
    feature_start = lax.axis_index("tp") * feature_half
    gain_part = lax.dynamic_slice_in_dim(split_gain, feature_start, feature_half, 0)
    normed_split = (
        (expanded - average[..., None]) * lax.rsqrt(spread[..., None] + EPSILON) * gain_part
    )
    restored = (
        normed_split.reshape(levels, half_rows, half_cols, 2, 2, feature_half)
        .transpose(0, 1, 3, 2, 4, 5)
        .reshape(levels, row_count, col_count, feature_half)
    )
    skip_part = lax.dynamic_slice_in_dim(
        residual.reshape(levels, row_count, col_count, features), feature_start, feature_half, 3
    )
    return (skip_part.astype(jnp.float32) + restored).astype(jnp.bfloat16)


def solution(mesh):
    in_specs = (
        P(None, "lat", "lon", None),
        P(),
        P("lat", None, "tp"),
        P(None, "lat"),
        P(),
        P("lat", "tp"),
        P(),
        P("lat", None, "tp"),
        P("tp", "lat"),
        P("lat", None, "tp"),
        P(),
    )
    out_specs = P(None, "lat", "lon", "tp")
    return jax.shard_map(body, mesh=mesh, in_specs=in_specs, out_specs=out_specs, check_vma=False)
```

profile of v0, /device:TPU:1, one launch (start us, length us, event | category | flops | bytes accessed | tf_op | source)
XLA Modules:
  0.0 953.4 jit_solution(4580351448857460882)
XLA Ops:
  6.5 0.7 all-gather.5.cloned.1.call-update
  7.3 0.7 all-gather.7.cloned.1.call-update
  8.1 0.7 all-gather.9.cloned.1.call-update
  8.8 128.6 %all_gather.27 = bf16[512,3,256]{2,0,1:T(8,128)(2,1)S(1)} all-gather(bf16[16,3,256]{2,0,1:T(8,128)(2,1)} %param.13), channel_id=1, replica_groups=mesh['lat'=32,'lon'=8,'tp'=2] {'lat'}, dimensions={0}, use_global_device_ids=true | all-gather | bytes 811008 | tf_op jit(solution)/shard_map/all_gather | solution.py:98
  138.5 0.7 convolution_convert_fusion.1
  139.2 9.5 collective-permute-start
  149.2 6.6 collective-permute-done
  155.8 1.9 collective-permute-start.1
  158.0 5.0 collective-permute-done.1
  163.1 1.0 reshape.198
  164.1 0.6 copy.56
  164.7 0.8 fusion.52
  165.4 0.5 copy.80
  165.9 0.5 copy.81
  166.4 0.5 copy.79
  166.9 2.5 fusion.53
  169.4 2.0 fusion.8
  171.4 0.6 copy.61
  172.8 1.9 collective-permute-start.2
  174.8 11.7 %collective-permute-done.2 = bf16[2,3,24,256]{3,0,2,1:T(2,128)(2,1)S(1)} collective-permute-done((bf16[2,3,24,256]{3,0,2,1:T(2,128)(2,1)S(1)}, bf16[2,3,24,256]{3,0,2,1:T(2,128)(2,1)S(1)}, u32[]{:S(2)}, u32[]{:S(2)}) %collective-permute-start.2) | collective-permute-done | bytes 73760 | tf_op jit(solution)/shard_map/ppermute | solution.py:16
  186.7 7.6 collective-permute-start.3
  194.3 102.6 %all_gather.29 = bf16[512,512]{0,1:T(8,128)(2,1)S(1)} all-gather(bf16[512,16]{0,1:T(8,128)(2,1)S(1)} %copy-done.5), channel_id=1, replica_groups=mesh['lat'=32,'lon'=8,'tp'=2] {'lat'}, dimensions={1}, use_global_device_ids=true | all-gather | bytes 540672 | tf_op jit(solution)/shard_map/all_gather | solution.py:111
  297.3 34.6 %all_gather.28 = bf16[2,12,24,512]{3,0,2,1:T(2,128)(2,1)S(1)} all-gather(bf16[2,12,24,256]{3,0,2,1:T(2,128)(2,1)S(1)} %fusion.26), channel_id=1, replica_groups=mesh['lat'=32,'lon'=8,'tp'=2] {'tp'}, dimensions={3}, use_global_device_ids=true | all-gather | bytes 884736 | tf_op jit(solution)/shard_map/all_gather | solution.py:110
  331.9 0.5 fusion.7
  332.5 0.8 copy-done.1
  333.3 0.7 reshape.214
  335.0 1.0 multiply_reduce_fusion
  336.0 1.0 reshape.212
  337.1 2.1 convolution_convert_fusion.5
  339.2 2.0 all_gather.31
  341.7 108.9 %all-gather.7.cloned.1.call-done = bf16[1024,3,512]{2,0,1:T(8,128)(2,1)} async-done(((bf16[32,3,512]{2,0,1:T(8,128)(2,1)}), bf16[1024,3,512]{2,0,1:T(8,128)(2,1)}) %all-gather.7.cloned.1.call-update) | async-done | bytes 3145744 | tf_op jit(solution)/shard_map/all_gather | solution.py:128
  450.6 3.2 copy.66
  453.8 2.0 convolution_convert_fusion
  455.8 1.3 copy.78
  457.1 0.6 fusion.58
  457.6 0.7 convolution_convert_fusion.4
  458.4 213.4 %all-gather.9.cloned.1.call-done = bf16[512,1024]{0,1:T(8,128)(2,1)} async-done(((bf16[512,32]{0,1:T(8,128)(2,1)}), bf16[512,1024]{0,1:T(8,128)(2,1)}) %all-gather.9.cloned.1.call-update) | async-done | bytes 1048592 | tf_op jit(solution)/shard_map/all_gather | solution.py:135
  671.8 2.4 convolution_convert_fusion.3
  674.4 222.2 %all-gather.11.cloned.1.call-done = bf16[1024,4,256]{2,1,0:T(4,128)(2,1)} async-done(((bf16[32,4,256]{2,1,0:T(4,128)(2,1)}), bf16[1024,4,256]{2,1,0:T(4,128)(2,1)}) %all-gather.11.cloned.1.call-update) | async-done | bytes 2097168 | tf_op jit(solution)/shard_map/all_gather | solution.py:143
  896.5 3.0 copy.77
  899.5 38.1 %reduce-scatter.2.cloned.1.call-done = bf16[144,512]{1,0:T(8,128)(2,1)} async-done(((bf16[144,1024]{1,0:T(8,128)(2,1)}), bf16[144,512]{1,0:T(8,128)(2,1)}) %reduce-scatter.2.cloned.1.call-update) | async-done | bytes 147472 | tf_op jit(solution)/shard_map/reduce_scatter | solution.py:137
  937.6 0.9 add_convert_fusion.1
  938.6 2.0 all_gather.34
  940.6 1.0 fusion.51
  941.6 2.5 all-reduce
  944.8 0.5 reshape.209
  945.2 0.5 copy.73
  946.1 0.7 copy.74
  (66 shorter events, 6.1 us)
Async XLA Ops:
  6.5 330.5 %all-gather.5.cloned.1.call-start = ((), (), s32[]{:S(2)}) async-start(), calls=%async_computation.1 | async-start | bytes 2162688 | tf_op jit(solution)/shard_map/all_gather | solution.py:123
  7.3 443.3 %all-gather.7.cloned.1.call-start = ((), (), s32[]{:S(2)}) async-start(), calls=%async_computation.2 | async-start | bytes 3244032 | tf_op jit(solution)/shard_map/all_gather | solution.py:128
  8.0 663.8 %all-gather.9.cloned.1.call-start = ((), (), s32[]{:S(2)}) async-start(), calls=%async_computation.3 | async-start | bytes 1081344 | tf_op jit(solution)/shard_map/all_gather | solution.py:135
  8.7 128.9 %copy-start = (bf16[2,12,24,512]{3,2,1,0:T(8,128)(2,1)S(1)}, bf16[2,12,24,512]{3,2,1,0:T(8,128)(2,1)}, u32[]{:S(2)}) copy-start(bf16[2,12,24,512]{3,2,1,0:T(8,128)(2,1)} %param.11) | copy-start | bytes 1769476
  8.8 887.8 %all-gather.11.cloned.1.call-start = ((), (), s32[]{:S(2)}) async-start(), calls=%async_computation.5 | async-start | bytes 2162688 | tf_op jit(solution)/shard_map/all_gather | solution.py:143
  137.4 0.8 copy-start.8
  139.2 16.6 %collective-permute-start = (bf16[2,12,6,768]{3,2,1,0:T(8,128)(2,1)S(1)}, bf16[2,12,6,768]{3,2,1,0:T(8,128)(2,1)S(1)}, u32[]{:S(2)}, u32[]{:S(2)}) collective-permute-start(bf16[2,12,6,768]{3,2,1,0:T(8,128)(2,1)S(1)} %slice.57), channel_id=1, source_target_pairs={{0,14},{2,0},{4,2},{6,4},{8,6},{10,8},{12,10},{14,12},{1,15},{3,1}... | collective-permute-start | bytes 663560 | tf_op jit(solution)/shard_map/ppermute | solution.py:16
  148.7 788.9 %reduce-scatter.2.cloned.1.call-start = ((), (), s32[]{:S(2)}) async-start(), calls=%async_computation.4 | async-start | bytes 442368 | tf_op jit(solution)/shard_map/reduce_scatter | solution.py:137
  155.8 7.2 collective-permute-start.1
  172.0 22.3 %copy-start.5 = (bf16[512,16]{0,1:T(8,128)(2,1)S(1)}, bf16[512,16]{0,1:T(8,128)(2,1)}, u32[]{:S(2)}) copy-start(bf16[512,16]{0,1:T(8,128)(2,1)} %param.14) | copy-start | bytes 49156
  172.8 13.8 %collective-permute-start.2 = (bf16[2,3,24,256]{3,0,2,1:T(2,128)(2,1)S(1)}, bf16[2,3,24,256]{3,0,2,1:T(2,128)(2,1)S(1)}, u32[]{:S(2)}, u32[]{:S(2)}) collective-permute-start(bf16[2,3,24,256]{3,0,2,1:T(2,128)(2,1)S(1)} %slice.63), channel_id=1, source_target_pairs={{0,16},{16,32},{32,48},{48,64},{64,80},{80,96},{96,112},{112,128},... | collective-permute-start | bytes 221192 | tf_op jit(solution)/shard_map/ppermute | solution.py:16
  186.7 110.2 %collective-permute-start.3 = (bf16[2,12,6,256]{3,0,2,1:T(2,128)(2,1)S(1)}, bf16[2,12,6,256]{3,0,2,1:T(2,128)(2,1)S(1)}, u32[]{:S(2)}, u32[]{:S(2)}) collective-permute-start(bf16[2,12,6,256]{3,0,2,1:T(2,128)(2,1)S(1)} %pad_maximum_fusion.3), channel_id=1, source_target_pairs={{0,2},{2,4},{4,6},{6,8},{8,10},{10,12},{12,14},{14,0},{1,3},{3,5},... | collective-permute-start | bytes 221192 | tf_op jit(solution)/shard_map/ppermute | solution.py:16
  332.5 0.8 copy-start.1
  336.0 1.1 copy-start.6
  339.2 2.4 copy-start.3
  341.6 112.1 %copy-start.7 = (f32[1024]{0:T(1024)S(1)}, f32[1024]{0:T(1024)}, u32[]{:S(2)}) copy-start(f32[1024]{0:T(1024)} %param.17) | copy-start | bytes 12292
  458.3 215.9 %copy-start.9 = (f32[512]{0:T(512)S(1)}, f32[512]{0:T(512)}, u32[]{:S(2)}) copy-start(f32[512]{0:T(512)} %param.21) | copy-start | bytes 6148
  458.4 216.0 %copy-start.2 = (bf16[576,512]{1,0:T(8,128)(2,1)S(1)}, bf16[576,512]{1,0:T(8,128)(2,1)}, u32[]{:S(2)}) copy-start(bf16[576,512]{1,0:T(8,128)(2,1)} %copy-done.1) | copy-start | bytes 1769476
  674.4 263.3 %copy-start.4 = (bf16[144,512]{1,0:T(8,128)(2,1)S(1)}, bf16[144,512]{1,0:T(8,128)(2,1)}, u32[]{:S(2)}) copy-start(bf16[144,512]{1,0:T(8,128)(2,1)} %copy-done.3) | copy-start | bytes 442372
Sparse Core Ops, SparseCore 0:
  9.4 213.7 all-gather.4
  225.4 225.1 all-gather.6
  452.7 219.0 all-gather.8
  673.7 222.7 all-gather.10
  899.1 38.4 reduce-scatter.1
where the time goes:
time: 954 us; the launch traced here: 953 us
  waiting for transfers between devices  608 us (64%)
  blocking collectives  272 us (29%)
  starting transfers between devices  21.1 us (2%)
  local copies, waits for them, and re-layouts  18.8 us (2%)
  matrix products  14.5 us (2%)
  between operations  13.7 us (1%)
    all_gather x1, waiting for transfers between devices, body(): lax.all_gather(split_weight, 'lat', axis=0, tiled=True)  222 us
    all_gather x1, waiting for transfers between devices, body(): lax.all_gather(coarse_proj, 'lat', axis=1, tiled=True)  213 us
    all_gather x1, blocking collectives, body(): lax.all_gather(fine_qkv, 'lat', axis=0, tiled=True)  129 us
    all_gather x1, waiting for transfers between devices, body(): lax.all_gather(coarse_qkv, 'lat', axis=0, tiled=True)  109 us
    all_gather x1, blocking collectives, body(): lax.all_gather(fine_proj, 'lat', axis=1, tiled=True)  103 us
    reduce_scatter x1, waiting for transfers between devices, body(): lax.psum_scatter(partial_value.astype(jnp.bfloat16), 'tp', scatter_dimens...  38.1 us
    all_gather x1, blocking collectives, body(): lax.all_gather(window_out, 'tp', axis=3, tiled=True)  34.6 us
    ppermute x4, waiting for transfers between devices, passed_along(): lax.ppermute(value, axis, [(i, (i + by) % peers) for i in range(peers)])  23.3 us
  transfers between devices with their start and end apart: 9, of which 7 were waited for; matrix products, arithmetic and copies ran while one was open for 3% of the time, Pallas kernels for 0%

commit v1 on v0

v1 whole, which is shorter than its diff:
```python
import jax
import jax.numpy as jnp
from jax import lax
from jax.sharding import Mesh, PartitionSpec as P

HEAD = 64
WIN_LAT = 6
WIN_LON = 12


EPSILON = 1e-05


def layer_norm(values, gain_row):
    average = jnp.mean(values, axis=-1, keepdims=True)
    centred = values - average
    spread = jnp.mean(centred * centred, axis=-1, keepdims=True)
    return centred * lax.rsqrt(spread + EPSILON) * gain_row


def seam_labels(global_rows, lat_total, rim_rows):
    return jnp.where(
        global_rows >= lat_total - rim_rows, 1, jnp.where(global_rows < rim_rows, 2, 0)
    ).astype(jnp.int32)


def window_mix(packed, head_count, row_labels):
    levels, row_count, col_count, channels = packed.shape
    head_size = channels // (3 * head_count)
    window_rows = row_count // WIN_LAT
    window_cols = col_count // WIN_LON
    window_size = levels * WIN_LAT * WIN_LON
    grouped = packed.reshape(
        levels, window_rows, WIN_LAT, window_cols, WIN_LON, 3, head_count, head_size
    )
    grouped = grouped.transpose(1, 3, 0, 2, 4, 5, 6, 7).reshape(
        window_rows * window_cols, window_size, 3, head_count, head_size
    )
    scores = jnp.einsum(
        "wqhd,wkhd->whqk", grouped[:, :, 0], grouped[:, :, 1], preferred_element_type=jnp.float32
    ) * head_size ** (-0.5)
    if row_labels is not None:
        token_labels = jnp.broadcast_to(
            row_labels.reshape(window_rows, 1, 1, WIN_LAT, 1),
            (window_rows, window_cols, levels, WIN_LAT, WIN_LON),
        ).reshape(window_rows * window_cols, window_size)
        allowed = token_labels[:, :, None] == token_labels[:, None, :]
        scores = jnp.where(allowed[:, None], scores, -1e30)
    row_maximum = jnp.max(scores, axis=-1, keepdims=True)
    weights = jnp.exp(scores - row_maximum)
    weights = (weights / jnp.sum(weights, axis=-1, keepdims=True)).astype(jnp.bfloat16)
    window_out = jnp.einsum(
        "whqk,wkhd->wqhd", weights, grouped[:, :, 2], preferred_element_type=jnp.float32
    ).astype(jnp.bfloat16)
    window_out = window_out.reshape(
        window_rows, window_cols, levels, WIN_LAT, WIN_LON, head_count * head_size
    ).transpose(2, 0, 3, 1, 4, 5)
    return window_out.reshape(levels, row_count, col_count, head_count * head_size)


def project_with(left_side, fragment):
    return jnp.dot(left_side, fragment, preferred_element_type=jnp.float32)


def project_with_transposed(left_side, fragment):
    return lax.dot_general(
        left_side, fragment, (((1,), (1,)), ((), ())), preferred_element_type=jnp.float32
    )


def quartered(shard, row_parts, col_parts):
    rows, cols = shard.shape[0] // row_parts, shard.shape[1] // col_parts
    place = lax.axis_index("y")
    return lax.dynamic_slice(
        shard, (place // col_parts * rows, place % col_parts * cols), (rows, cols)
    )


def sent_to_all(block, axes):
    peers = lax.axis_size(axes)
    copies = jnp.broadcast_to(block[None], (peers,) + block.shape)
    return lax.all_to_all(copies, axes, split_axis=0, concat_axis=0, tiled=True)


def over_depth(block):
    other = lax.ppermute(block, "za", [(0, 1), (1, 0)])
    upper = lax.axis_index("za") == 1
    pair = jnp.stack([jnp.where(upper, other, block), jnp.where(upper, block, other)])
    return sent_to_all(pair, "zq")


def over_plane(block, row_parts, col_parts):
    quads, pairs, rows, cols = block.shape
    whole = sent_to_all(block, ("x", "y"))
    whole = whole.reshape(4, row_parts, col_parts, quads, pairs, rows, cols)
    whole = whole.transpose(4, 3, 0, 1, 5, 2, 6)
    return whole.reshape(-1, col_parts * cols)


def after(value, earlier):
    return lax.optimization_barrier((value, earlier))[0]


def lat_shift(value, by):
    perm = [(i, (i + by) % 32) for i in range(32)]
    return lax.ppermute(value, ("za", "zq", "x"), perm)


def lon_shift(value, by):
    perm = [(i, (i + by) % 8) for i in range(8)]
    return lax.ppermute(value, ("y", "zh"), perm)


def body(
    fine_tokens,
    attn_gain,
    fine_qkv,
    fine_proj,
    merge_gain,
    merge_weight,
    coarse_gain,
    coarse_qkv,
    coarse_proj,
    split_weight,
    split_gain,
):
    levels, row_count, col_count, features = fine_tokens.shape
    lat_total = row_count * 32
    row_first = lax.axis_index(("za", "zq", "x")) * row_count
    rim_rows = WIN_LAT // 2
    rim_cols = WIN_LON // 2

    late_shard = jnp.concatenate([split_weight.reshape(32, -1), coarse_proj.T], axis=1)
    late = lax.all_gather(late_shard, "x", axis=0, tiled=True)
    late = lax.all_gather(late, ("za", "zq"), axis=0, tiled=True)
    packed_width = 3 * fine_qkv.shape[2]
    first_shard = jnp.concatenate([fine_qkv.reshape(16, packed_width), fine_proj.T], axis=1)
    first = over_depth(quartered(first_shard, 2, 2))
    first_all = over_plane(first, 2, 2)
    merge_depth = over_depth(after(quartered(merge_weight, 4, 1), first_all))
    qkv_depth = over_depth(after(quartered(coarse_qkv.reshape(32, -1), 4, 1), merge_depth))
    merge_all = over_plane(after(merge_depth, qkv_depth), 4, 1)
    qkv_all = over_plane(after(qkv_depth, merge_all), 4, 1)

    arriving = lon_shift(fine_tokens[:, :, :rim_cols], -1)
    extended = jnp.concatenate([fine_tokens[:, :, rim_cols:], arriving], axis=2)
    arriving = lat_shift(extended[:, :rim_rows], -1)
    extended = jnp.concatenate([extended[:, rim_rows:], arriving], axis=1)
    normed = layer_norm(extended.reshape(-1, features).astype(jnp.float32), attn_gain).astype(
        jnp.bfloat16
    )
    fine_heads = fine_qkv.shape[2] // HEAD
    packed = project_with(normed, first_all[:, :packed_width])
    packed = packed.astype(jnp.bfloat16).reshape(levels, row_count, col_count, packed_width)
    global_rows = (row_first + rim_rows + jnp.arange(row_count, dtype=jnp.int32)) % lat_total
    window_out = window_mix(packed, fine_heads, seam_labels(global_rows, lat_total, rim_rows))
    returning = lat_shift(window_out[:, row_count - rim_rows :], 1)
    window_out = jnp.concatenate([returning, window_out[:, : row_count - rim_rows]], axis=1)
    returning = lon_shift(window_out[:, :, col_count - rim_cols :], 1)
    window_out = jnp.concatenate([returning, window_out[:, :, : col_count - rim_cols]], axis=2)
    all_heads = lax.all_gather(window_out, "core", axis=3, tiled=True).reshape(-1, features)
    attended = project_with_transposed(all_heads, first_all[:, packed_width:])
    flat_tokens = fine_tokens.reshape(-1, features)
    residual = (flat_tokens.astype(jnp.float32) + attended).astype(jnp.bfloat16)
    half_rows = row_count // 2
    half_cols = col_count // 2
    quartets = (
        residual.reshape(levels, half_rows, 2, half_cols, 2, features)
        .transpose(0, 1, 3, 2, 4, 5)
        .reshape(-1, 4 * features)
    )
    merged_in = layer_norm(quartets.astype(jnp.float32), merge_gain).astype(jnp.bfloat16)
    coarse_rows = merged_in.shape[0]
    coarse_half = project_with(merged_in, merge_all).astype(jnp.bfloat16)
    coarse_full = lax.all_gather(coarse_half, "core", axis=1, tiled=True)
    coarse_normed = layer_norm(coarse_full.astype(jnp.float32), coarse_gain).astype(jnp.bfloat16)
    coarse_packed = project_with(coarse_normed, qkv_all).astype(jnp.bfloat16)
    heads_here = coarse_qkv.shape[2] // HEAD
    coarse_mixed = window_mix(
        coarse_packed.reshape(levels, half_rows, half_cols, -1), heads_here, None
    ).reshape(coarse_rows, -1)
    partial_value = project_with_transposed(coarse_mixed, late[:, 1024:]).astype(jnp.bfloat16)
    both = lax.all_gather(partial_value, "core", axis=0, tiled=False).astype(jnp.float32)
    coarse_out = (coarse_full.astype(jnp.float32) + (both[0] + both[1])).astype(jnp.bfloat16)
    feature_half = split_weight.shape[2]
    expanded = project_with(coarse_out, late[:, :1024])
    expanded = expanded.reshape(coarse_rows, 4, feature_half)
    first_sum, second_sum = lax.psum(
        (jnp.sum(expanded, axis=-1), jnp.sum(expanded * expanded, axis=-1)), "core"
    )
    average = first_sum / features
    spread = second_sum / features - average * average
    feature_start = lax.axis_index("core") * feature_half
    gain_part = lax.dynamic_slice_in_dim(split_gain, feature_start, feature_half, 0)
    normed_split = (
        (expanded - average[..., None]) * lax.rsqrt(spread[..., None] + EPSILON) * gain_part
    )
    restored = (
        normed_split.reshape(levels, half_rows, half_cols, 2, 2, feature_half)
        .transpose(0, 1, 3, 2, 4, 5)
        .reshape(levels, row_count, col_count, feature_half)
    )
    skip_part = lax.dynamic_slice_in_dim(
        residual.reshape(levels, row_count, col_count, features), feature_start, feature_half, 3
    )
    return (skip_part.astype(jnp.float32) + restored).astype(jnp.bfloat16)


def solution(mesh):
    finer = Mesh(
        mesh.devices.reshape(2, 4, 4, 4, 2, 2), ("za", "zq", "x", "y", "zh", "core")
    )
    lat, lon, tp = ("za", "zq", "x"), ("y", "zh"), "core"
    in_specs = (
        P(None, lat, lon, None),
        P(),
        P(lat, None, tp),
        P(None, lat),
        P(),
        P(lat, tp),
        P(),
        P(lat, None, tp),
        P(tp, lat),
        P(lat, None, tp),
        P(),
    )
    out_specs = P(None, lat, lon, tp)
    return jax.shard_map(body, mesh=finer, in_specs=in_specs, out_specs=out_specs, check_vma=False)
```

time: 954 us -> 225 us (0.24)
  the two profiles are of different devices: /device:TPU:1 before, /device:TPU:57 now
where the time goes in v1:
time: 225 us; the launch traced here: 224 us
  starting transfers between devices  79.8 us (35%)
  waiting for transfers between devices  39.9 us (18%)
  blocking collectives  39.1 us (17%)
  local copies, waits for them, and re-layouts  28.7 us (13%)
  between operations  14.1 us (6%)
  matrix products  13.2 us (6%)
  other arithmetic  9.14 us (4%)
    all_to_all x5, starting transfers between devices, sent_to_all(): return lax.all_to_all(copies, axes, split_axis=0, concat_axis=0, tiled=True)  38.4 us
    ppermute x3, starting transfers between devices, over_depth(): other = lax.ppermute(block, 'za', [(0, 1), (1, 0)])  21.6 us
    all_to_all x5, waiting for transfers between devices, sent_to_all(): return lax.all_to_all(copies, axes, split_axis=0, concat_axis=0, tiled=True)  15.3 us
    ppermute x2, waiting for transfers between devices, lon_shift(): return lax.ppermute(value, ('y', 'zh'), perm)  15.1 us
    ppermute x2, starting transfers between devices, lon_shift(): return lax.ppermute(value, ('y', 'zh'), perm)  13.6 us
    all_gather x1, blocking collectives, body(): late = lax.all_gather(late_shard, 'x', axis=0, tiled=True)  11.3 us
    ppermute x3, waiting for transfers between devices, over_depth(): other = lax.ppermute(block, 'za', [(0, 1), (1, 0)])  9.44 us
    all_to_all x1, blocking collectives, sent_to_all(): return lax.all_to_all(copies, axes, split_axis=0, concat_axis=0, tiled=True)  9.14 us
  transfers between devices with their start and end apart: 13, of which 7 were waited for; matrix products, arithmetic and copies ran while one was open for 18% of the time, Pallas kernels for 0%

profile of v1, /device:TPU:57, one launch (start us, length us, event | category | flops | bytes accessed | tf_op | source)
XLA Modules:
  0.0 224.0 jit_solution(10463762311979680166)
XLA Ops:
  6.5 0.8 copy.111
  7.3 0.7 fusion.44
  8.0 8.8 %collective-permute-start.2 = (bf16[8,640]{1,0:T(8,128)(2,1)S(1)}, bf16[8,640]{1,0:T(8,128)(2,1)S(1)}, u32[]{:S(2)}, u32[]{:S(2)}) collective-permute-start(bf16[8,640]{1,0:T(8,128)(2,1)S(1)} %fusion.44), channel_id=1, source_target_pairs={{0,256},{256,0},{1,257},{257,1},{2,258},{258,2},{3,259},{259,3},{4... | collective-permute-start | bytes 30728 | tf_op jit(solution)/shard_map/ppermute | solution.py:86
  16.9 1.0 collective-permute-done.2
  17.9 9.1 %all_to_all.30 = bf16[4,2,8,640]{3,2,1,0:T(8,128)(2,1)S(1)} all-to-all(bf16[4,2,8,640]{3,2,1,0:T(8,128)(2,1)S(1)} %broadcast_in_dim.31), channel_id=1, replica_groups=mesh['za'=2,'zq'=4,'x'=4,'y'=4,'zh'=2,'core'=2] {'zq'}, dimensions={0} | all-to-all | bytes 163840 | tf_op jit(solution)/shard_map/all_to_all | solution.py:82
  27.1 1.2 broadcast_in_dim.33
  28.3 6.6 %all-to-all-start.1 = ((bf16[16,4,2,8,640]{4,3,2,1,0:T(8,128)(2,1)}), bf16[16,4,2,8,640]{4,3,2,1,0:T(8,128)(2,1)S(1)}, u32[]{:S(2)}, u32[]{:S(2)}) async-start(bf16[16,4,2,8,640]{4,3,2,1,0:T(8,128)(2,1)} %broadcast_in_dim.33), calls=%async_computation.1 | async-start | bytes 2621440 | tf_op jit(solution)/shard_map/all_to_all | solution.py:82
  35.6 11.5 %collective-permute-start = (bf16[2,12,6,512]{3,2,1,0:T(8,128)(2,1)}, bf16[2,12,6,512]{3,2,1,0:T(8,128)(2,1)S(1)}, u32[]{:S(2)}, u32[]{:S(2)}) collective-permute-start(bf16[2,12,6,512]{3,2,1,0:T(8,128)(2,1)} %slice.61), channel_id=1, source_target_pairs={{0,14},{2,0},{4,2},{6,4},{8,6},{10,8},{12,10},{14,12},{1,15},{3,1}... | collective-permute-start | bytes 442376 | tf_op jit(solution)/shard_map/ppermute | solution.py:111
  47.1 2.3 %all-to-all-done.1 = bf16[16,4,2,8,640]{4,3,2,1,0:T(8,128)(2,1)S(1)} async-done(((bf16[16,4,2,8,640]{4,3,2,1,0:T(8,128)(2,1)}), bf16[16,4,2,8,640]{4,3,2,1,0:T(8,128)(2,1)S(1)}, u32[]{:S(2)}, u32[]{:S(2)}) %all-to-all-start.1) | async-done | bytes 1310752 | tf_op jit(solution)/shard_map/all_to_all | solution.py:82
  49.5 1.3 copy.81
  51.0 7.1 %collective-permute-start.5 = (bf16[16,512]{1,0:T(8,128)(2,1)S(1)}, bf16[16,512]{1,0:T(8,128)(2,1)S(1)}, u32[]{:S(2)}, u32[]{:S(2)}) collective-permute-start(bf16[16,512]{1,0:T(8,128)(2,1)S(1)} %constant_dynamic-slice_fusion.1), channel_id=1, source_target_pairs={{0,256},{256,0},{1,257},{257,1},{2,258},{258,2},{3,259},{259,3},{4... | collective-permute-start | bytes 49160 | tf_op jit(solution)/shard_map/ppermute | solution.py:86
  58.1 8.4 %collective-permute-done.5 = bf16[16,512]{1,0:T(8,128)(2,1)S(1)} collective-permute-done((bf16[16,512]{1,0:T(8,128)(2,1)S(1)}, bf16[16,512]{1,0:T(8,128)(2,1)S(1)}, u32[]{:S(2)}, u32[]{:S(2)}) %collective-permute-start.5) | collective-permute-done | bytes 16416 | tf_op jit(solution)/shard_map/ppermute | solution.py:86
  67.2 5.4 %all-to-all-start.2 = ((bf16[4,2,16,512]{3,2,1,0:T(8,128)(2,1)}), bf16[4,2,16,512]{3,2,1,0:T(8,128)(2,1)S(1)}, u32[]{:S(2)}, u32[]{:S(2)}) async-start(bf16[4,2,16,512]{3,2,1,0:T(8,128)(2,1)} %broadcast_in_dim.39), calls=%async_computation.2 | async-start | bytes 262144 | tf_op jit(solution)/shard_map/all_to_all | solution.py:82
  72.6 11.3 %all_gather.20 = bf16[128,1536]{1,0:T(8,128)(2,1)} all-gather(bf16[32,1536]{1,0:T(8,128)(2,1)S(1)} %pad_maximum_fusion.2), channel_id=1, replica_groups=mesh['za'=2,'zq'=4,'x'=4,'y'=4,'zh'=2,'core'=2] {'x'}, dimensions={0}, use_global_device_ids=true | all-gather | bytes 491520 | tf_op jit(solution)/shard_map/all_gather | solution.py:134
  84.4 5.7 %collective-permute-start.6 = (bf16[8,1536]{1,0:T(8,128)(2,1)S(1)}, bf16[8,1536]{1,0:T(8,128)(2,1)S(1)}, u32[]{:S(2)}, u32[]{:S(2)}) collective-permute-start(bf16[8,1536]{1,0:T(8,128)(2,1)S(1)} %constant_dynamic-slice_fusion), channel_id=1, source_target_pairs={{0,256},{256,0},{1,257},{257,1},{2,258},{258,2},{3,259},{259,3},{4... | collective-permute-start | bytes 73736 | tf_op jit(solution)/shard_map/ppermute | solution.py:86
  90.8 3.1 %collective-permute-start.1 = (bf16[2,3,24,512]{3,2,1,0:T(8,128)(2,1)}, bf16[2,3,24,512]{3,2,1,0:T(8,128)(2,1)S(1)}, u32[]{:S(2)}, u32[]{:S(2)}) collective-permute-start(bf16[2,3,24,512]{3,2,1,0:T(8,128)(2,1)} %pad_maximum_fusion.1), channel_id=1, source_target_pairs={{0,496},{16,0},{32,16},{48,32},{64,48},{80,64},{96,80},{112,96},{1... | collective-permute-start | bytes 442376 | tf_op jit(solution)/shard_map/ppermute | solution.py:106
  94.7 7.8 %all-to-all-start.3 = ((bf16[4,2,8,1536]{3,2,1,0:T(8,128)(2,1)}), bf16[4,2,8,1536]{3,2,1,0:T(8,128)(2,1)S(1)}, u32[]{:S(2)}, u32[]{:S(2)}) async-start(bf16[4,2,8,1536]{3,2,1,0:T(8,128)(2,1)} %broadcast_in_dim.40), calls=%async_computation.3 | async-start | bytes 393216 | tf_op jit(solution)/shard_map/all_to_all | solution.py:82
  102.5 0.8 broadcast_compare_fusion
  103.9 9.0 %all-to-all-done.3 = bf16[4,2,8,1536]{3,2,1,0:T(8,128)(2,1)S(1)} async-done(((bf16[4,2,8,1536]{3,2,1,0:T(8,128)(2,1)}), bf16[4,2,8,1536]{3,2,1,0:T(8,128)(2,1)S(1)}, u32[]{:S(2)}, u32[]{:S(2)}) %all-to-all-start.3) | async-done | bytes 196640 | tf_op jit(solution)/shard_map/all_to_all | solution.py:82
  112.9 1.7 broadcast_in_dim.45
  114.6 7.9 %all-to-all-start.4 = ((bf16[16,4,2,16,512]{4,3,1,2,0:T(8,128)(2,1)}), bf16[16,4,2,16,512]{4,3,1,2,0:T(8,128)(2,1)}, u32[]{:S(2)}, u32[]{:S(2)}) async-start(bf16[16,4,2,16,512]{4,3,1,2,0:T(8,128)(2,1)} %broadcast_in_dim.45), calls=%async_computation.4 | async-start | bytes 4194304 | tf_op jit(solution)/shard_map/all_to_all | solution.py:82
  123.4 1.5 convolution_convert_fusion.1
  125.0 3.0 %reshape_reshape.3 = bf16[2,2,6,2,12,3,4,64]{7,6,5,4,3,2,1,0:T(4,128)(2,1)S(1)} reshape(bf16[576,768]{1,0:T(8,128)(2,1)} %convolution_convert_fusion.1) | data formatting | bytes 1769472 | tf_op jit(solution)/shard_map/reshape;reshape | solution.py:33
  128.6 0.8 fusion.57
  130.8 2.5 %fusion.58 = (f32[4,4,144]{2,1,0:T(4,128)S(1)}, f32[4,4,144,144]{2,3,1,0:T(8,128)}) fusion(pred[4,144,144]{1,2,0:T(8,128)(4,1)S(1)} %copy-done.6, bf16[4,144,1,4,64]{1,4,3,0,2:T(8,128)(2,1)S(1)} %copy.110, bf16[4,144,1,4,64]{1,4,3,0,2:T(8,128)(2,1)S(1)} %copy.109), kind=kOutput, calls=%fused_computation.103 | convolution fusion | flops 43794576 | bytes 2009088 | tf_op jit(solution)/shard_map/sub | solution.py:50
  133.3 2.0 fusion.8
  136.6 3.1 %collective-permute-start.3 = (bf16[2,3,24,256]{3,0,2,1:T(2,128)(2,1)S(1)}, bf16[2,3,24,256]{3,0,2,1:T(2,128)(2,1)S(1)}, u32[]{:S(2)}, u32[]{:S(2)}) collective-permute-start(bf16[2,3,24,256]{3,0,2,1:T(2,128)(2,1)S(1)} %slice.88), channel_id=1, source_target_pairs={{0,16},{16,32},{32,48},{48,64},{64,80},{80,96},{96,112},{112,128},... | collective-permute-start | bytes 221192 | tf_op jit(solution)/shard_map/ppermute | solution.py:106
  139.9 3.8 %all-to-all-done.4 = bf16[16,4,2,16,512]{4,3,1,2,0:T(8,128)(2,1)} async-done(((bf16[16,4,2,16,512]{4,3,1,2,0:T(8,128)(2,1)}), bf16[16,4,2,16,512]{4,3,1,2,0:T(8,128)(2,1)}, u32[]{:S(2)}, u32[]{:S(2)}) %all-to-all-start.4) | async-done | bytes 2097184 | tf_op jit(solution)/shard_map/all_to_all | solution.py:82
  143.8 1.8 copy.93
  145.6 2.1 broadcast_in_dim.46
  147.7 10.8 %all-to-all-start.5 = ((bf16[16,4,2,8,1536]{4,3,1,2,0:T(8,128)(2,1)}), bf16[16,4,2,8,1536]{4,3,1,2,0:T(8,128)(2,1)}, u32[]{:S(2)}, u32[]{:S(2)}) async-start(bf16[16,4,2,8,1536]{4,3,1,2,0:T(8,128)(2,1)} %broadcast_in_dim.46), calls=%async_computation.5 | async-start | bytes 6291456 | tf_op jit(solution)/shard_map/all_to_all | solution.py:82
  158.6 2.1 collective-permute-start.4
  160.8 15.1 %collective-permute-done.4 = bf16[2,12,6,256]{3,0,2,1:T(2,128)(2,1)S(1)} collective-permute-done((bf16[2,12,6,256]{3,0,2,1:T(2,128)(2,1)S(1)}, bf16[2,12,6,256]{3,0,2,1:T(2,128)(2,1)S(1)}, u32[]{:S(2)}, u32[]{:S(2)}) %collective-permute-start.4) | collective-permute-done | bytes 73760 | tf_op jit(solution)/shard_map/ppermute | solution.py:111
  176.3 6.3 %all_gather.18 = bf16[2,12,24,512]{3,0,2,1:T(2,128)(2,1)S(1)} all-gather(bf16[2,12,24,256]{3,0,2,1:T(2,128)(2,1)S(1)} %fusion.31), channel_id=1, replica_groups=mesh['za'=2,'zq'=4,'x'=4,'y'=4,'zh'=2,'core'=2] {'core'}, dimensions={3}, use_global_device_ids=true | all-gather | bytes 884736 | tf_op jit(solution)/shard_map/all_gather | solution.py:161
  182.6 2.4 %fusion.7 = bf16[576,512]{1,0:T(8,128)(2,1)} fusion(bf16[576,512]{1,0:T(8,128)(2,1)S(1)} %bitcast.150, bf16[576,512]{1,0:T(8,128)(2,1)S(1)} %bitcast.147, bf16[512,1280]{1,0:T(8,128)(2,1)} %bitcast.143), kind=kOutput, calls=%fused_computation.14 | convolution fusion | flops 302874624 | bytes 2293760 | tf_op jit(solution)/shard_map/dot_general | solution.py:66
  185.0 1.9 reshape.242
  187.4 1.0 multiply_reduce_fusion
  188.3 1.6 multiply_convert_fusion
  189.9 2.2 convert_element_type.109
  192.6 2.0 all_gather.19
  195.1 2.2 copy.95
  197.3 0.7 convolution_convert_fusion
  198.9 0.7 convolution_convert_fusion.4
  199.6 1.9 convolution_convert_fusion.3
  201.5 7.8 %all-gather = bf16[288,1024]{1,0:T(8,128)(2,1)S(1)} all-gather(bf16[144,1024]{1,0:T(8,128)(2,1)S(1)} %convolution_convert_fusion.3), channel_id=2, replica_groups=mesh['za'=2,'zq'=4,'x'=4,'y'=4,'zh'=2,'core'=2] {'core'}, dimensions={0}, use_global_device_ids=true | all-gather | bytes 884736 | tf_op jit(solution)/shard_map/all_gather | solution.py:183
  211.3 2.5 %all-reduce = (f32[144,4]{0,1:T(4,128)S(1)}, f32[144,4]{0,1:T(4,128)S(1)}) all-reduce(f32[144,4]{0,1:T(4,128)S(1)} %copy.102, f32[144,4]{0,1:T(4,128)S(1)} %copy.100), channel_id=1, replica_groups=mesh['za'=2,'zq'=4,'x'=4,'y'=4,'zh'=2,'core'=2] {'core'}, use_global_device_ids=true, to_apply=%region_13.14 | all-reduce | flops 1152 | bytes 9216 | tf_op jit(solution)/shard_map/psum | solution.py:188
  214.5 0.8 multiply_bitcast_fusion
  216.3 0.8 add_convert_fusion
  (109 shorter events, 15.1 us)
Async XLA Ops:
  6.5 40.5 %copy-start = (bf16[64,512]{1,0:T(8,128)(2,1)S(1)}, bf16[64,512]{1,0:T(8,128)(2,1)}, u32[]{:S(2)}) copy-start(bf16[64,512]{1,0:T(8,128)(2,1)} %param.16) | copy-start | bytes 196612
  8.0 9.9 %collective-permute-start.2 = (bf16[8,640]{1,0:T(8,128)(2,1)S(1)}, bf16[8,640]{1,0:T(8,128)(2,1)S(1)}, u32[]{:S(2)}, u32[]{:S(2)}) collective-permute-start(bf16[8,640]{1,0:T(8,128)(2,1)S(1)} %fusion.44), channel_id=1, source_target_pairs={{0,256},{256,0},{1,257},{257,1},{2,258},{258,2},{3,259},{259,3},{4... | collective-permute-start | bytes 30728 | tf_op jit(solution)/shard_map/ppermute | solution.py:86
  28.3 6.6 %copy-start.3 = (bf16[2,12,24,512]{3,2,1,0:T(8,128)(2,1)S(1)}, bf16[2,12,24,512]{3,2,1,0:T(8,128)(2,1)}, u32[]{:S(2)}) copy-start(bf16[2,12,24,512]{3,2,1,0:T(8,128)(2,1)} %param.11) | copy-start | bytes 1769476
  28.3 18.7 %copy-start.8 = (bf16[32,4,256]{2,1,0:T(4,128)(2,1)S(1)}, bf16[32,4,256]{2,1,0:T(4,128)(2,1)}, u32[]{:S(2)}) copy-start(bf16[32,4,256]{2,1,0:T(4,128)(2,1)} %param.20) | copy-start | bytes 196612
  28.3 21.1 %all-to-all-start.1 = ((bf16[16,4,2,8,640]{4,3,2,1,0:T(8,128)(2,1)}), bf16[16,4,2,8,640]{4,3,2,1,0:T(8,128)(2,1)S(1)}, u32[]{:S(2)}, u32[]{:S(2)}) async-start(bf16[16,4,2,8,640]{4,3,2,1,0:T(8,128)(2,1)} %broadcast_in_dim.33), calls=%async_computation.1 | async-start | bytes 2621440 | tf_op jit(solution)/shard_map/all_to_all | solution.py:82
  35.6 54.5 %collective-permute-start = (bf16[2,12,6,512]{3,2,1,0:T(8,128)(2,1)}, bf16[2,12,6,512]{3,2,1,0:T(8,128)(2,1)S(1)}, u32[]{:S(2)}, u32[]{:S(2)}) collective-permute-start(bf16[2,12,6,512]{3,2,1,0:T(8,128)(2,1)} %slice.61), channel_id=1, source_target_pairs={{0,14},{2,0},{4,2},{6,4},{8,6},{10,8},{12,10},{14,12},{1,15},{3,1}... | collective-permute-start | bytes 442376 | tf_op jit(solution)/shard_map/ppermute | solution.py:111
  50.8 7.3 %copy-start.9 = (bf16[512,32]{0,1:T(8,128)(2,1)S(1)}, bf16[512,32]{0,1:T(8,128)(2,1)}, u32[]{:S(2)}) copy-start(bf16[512,32]{0,1:T(8,128)(2,1)} %param.19) | copy-start | bytes 98308
  51.0 72.4 %copy-start.2 = (bf16[64,8,2,640]{3,1,2,0:T(8,128)(2,1)}, bf16[64,8,2,640]{3,1,2,0:T(8,128)(2,1)S(1)}, u32[]{:S(2)}) copy-start(bf16[64,8,2,640]{3,1,2,0:T(8,128)(2,1)S(1)} %copy.113) | copy-start | bytes 3932164
  51.0 15.5 %collective-permute-start.5 = (bf16[16,512]{1,0:T(8,128)(2,1)S(1)}, bf16[16,512]{1,0:T(8,128)(2,1)S(1)}, u32[]{:S(2)}, u32[]{:S(2)}) collective-permute-start(bf16[16,512]{1,0:T(8,128)(2,1)S(1)} %constant_dynamic-slice_fusion.1), channel_id=1, source_target_pairs={{0,256},{256,0},{1,257},{257,1},{2,258},{258,2},{3,259},{259,3},{4... | collective-permute-start | bytes 49160 | tf_op jit(solution)/shard_map/ppermute | solution.py:86
  67.2 16.9 %copy-start.7 = (bf16[32,3,512]{2,0,1:T(8,128)(2,1)S(1)}, bf16[32,3,512]{2,0,1:T(8,128)(2,1)}, u32[]{:S(2)}) copy-start(bf16[32,3,512]{2,0,1:T(8,128)(2,1)} %param.18) | copy-start | bytes 294916
  67.2 17.1 %all-to-all-start.2 = ((bf16[4,2,16,512]{3,2,1,0:T(8,128)(2,1)}), bf16[4,2,16,512]{3,2,1,0:T(8,128)(2,1)S(1)}, u32[]{:S(2)}, u32[]{:S(2)}) async-start(bf16[4,2,16,512]{3,2,1,0:T(8,128)(2,1)} %broadcast_in_dim.39), calls=%async_computation.2 | async-start | bytes 262144 | tf_op jit(solution)/shard_map/all_to_all | solution.py:82
  72.6 127.0 %all-gather.3.cloned.1.call-start = ((), (), s32[]{:S(2)}) async-start(), calls=%async_computation.6 | async-start | bytes 3538944 | tf_op jit(solution)/shard_map/all_gather | solution.py:135
  84.3 5.7 %copy-start.4 = (bf16[4,2,16,512]{3,2,1,0:T(8,128)(2,1)}, bf16[4,2,16,512]{3,2,1,0:T(8,128)(2,1)S(1)}, u32[]{:S(2)}) copy-start(bf16[4,2,16,512]{3,2,1,0:T(8,128)(2,1)S(1)} %all-to-all-done.2) | copy-start | bytes 393220
  84.4 9.6 %collective-permute-start.6 = (bf16[8,1536]{1,0:T(8,128)(2,1)S(1)}, bf16[8,1536]{1,0:T(8,128)(2,1)S(1)}, u32[]{:S(2)}, u32[]{:S(2)}) collective-permute-start(bf16[8,1536]{1,0:T(8,128)(2,1)S(1)} %constant_dynamic-slice_fusion), channel_id=1, source_target_pairs={{0,256},{256,0},{1,257},{257,1},{2,258},{258,2},{3,259},{259,3},{4... | collective-permute-start | bytes 73736 | tf_op jit(solution)/shard_map/ppermute | solution.py:86
  90.8 12.6 %collective-permute-start.1 = (bf16[2,3,24,512]{3,2,1,0:T(8,128)(2,1)}, bf16[2,3,24,512]{3,2,1,0:T(8,128)(2,1)S(1)}, u32[]{:S(2)}, u32[]{:S(2)}) collective-permute-start(bf16[2,3,24,512]{3,2,1,0:T(8,128)(2,1)} %pad_maximum_fusion.1), channel_id=1, source_target_pairs={{0,496},{16,0},{32,16},{48,32},{64,48},{80,64},{96,80},{112,96},{1... | collective-permute-start | bytes 442376 | tf_op jit(solution)/shard_map/ppermute | solution.py:106
  94.7 18.3 %all-to-all-start.3 = ((bf16[4,2,8,1536]{3,2,1,0:T(8,128)(2,1)}), bf16[4,2,8,1536]{3,2,1,0:T(8,128)(2,1)S(1)}, u32[]{:S(2)}, u32[]{:S(2)}) async-start(bf16[4,2,8,1536]{3,2,1,0:T(8,128)(2,1)} %broadcast_in_dim.40), calls=%async_computation.3 | async-start | bytes 393216 | tf_op jit(solution)/shard_map/all_to_all | solution.py:82
  103.4 9.5 %copy-start.5 = (bf16[4,2,16,512]{3,2,1,0:T(8,128)(2,1)S(1)}, bf16[4,2,16,512]{3,2,1,0:T(8,128)(2,1)}, u32[]{:S(2)}) copy-start(bf16[4,2,16,512]{3,2,1,0:T(8,128)(2,1)} %copy-done.4) | copy-start | bytes 393220
  114.6 29.1 %all-to-all-start.4 = ((bf16[16,4,2,16,512]{4,3,1,2,0:T(8,128)(2,1)}), bf16[16,4,2,16,512]{4,3,1,2,0:T(8,128)(2,1)}, u32[]{:S(2)}, u32[]{:S(2)}) async-start(bf16[16,4,2,16,512]{4,3,1,2,0:T(8,128)(2,1)} %broadcast_in_dim.45), calls=%async_computation.4 | async-start | bytes 4194304 | tf_op jit(solution)/shard_map/all_to_all | solution.py:82
  122.5 0.7 copy-start.12
  129.8 1.0 copy-start.6
  136.6 21.8 %collective-permute-start.3 = (bf16[2,3,24,256]{3,0,2,1:T(2,128)(2,1)S(1)}, bf16[2,3,24,256]{3,0,2,1:T(2,128)(2,1)S(1)}, u32[]{:S(2)}, u32[]{:S(2)}) collective-permute-start(bf16[2,3,24,256]{3,0,2,1:T(2,128)(2,1)S(1)} %slice.88), channel_id=1, source_target_pairs={{0,16},{16,32},{32,48},{48,64},{64,80},{80,96},{96,112},{112,128},... | collective-permute-start | bytes 221192 | tf_op jit(solution)/shard_map/ppermute | solution.py:106
  147.7 13.0 %copy-start.10 = (f32[2048]{0:T(1024)S(1)}, f32[2048]{0:T(1024)}, u32[]{:S(2)}) copy-start(f32[2048]{0:T(1024)} %param.15) | copy-start | bytes 24580
  147.7 13.0 %copy-start.13 = (f32[512]{0:T(512)S(1)}, f32[512]{0:T(512)}, u32[]{:S(2)}) copy-start(f32[512]{0:T(512)} %param.21) | copy-start | bytes 6148
  147.7 47.4 %all-to-all-start.5 = ((bf16[16,4,2,8,1536]{4,3,1,2,0:T(8,128)(2,1)}), bf16[16,4,2,8,1536]{4,3,1,2,0:T(8,128)(2,1)}, u32[]{:S(2)}, u32[]{:S(2)}) async-start(bf16[16,4,2,8,1536]{4,3,1,2,0:T(8,128)(2,1)} %broadcast_in_dim.46), calls=%async_computation.5 | async-start | bytes 6291456 | tf_op jit(solution)/shard_map/all_to_all | solution.py:82
  158.6 17.3 %collective-permute-start.4 = (bf16[2,12,6,256]{3,0,2,1:T(2,128)(2,1)S(1)}, bf16[2,12,6,256]{3,0,2,1:T(2,128)(2,1)S(1)}, u32[]{:S(2)}, u32[]{:S(2)}) collective-permute-start(bf16[2,12,6,256]{3,0,2,1:T(2,128)(2,1)S(1)} %pad_maximum_fusion.3), channel_id=1, source_target_pairs={{0,2},{2,4},{4,6},{6,8},{8,10},{10,12},{12,14},{14,0},{1,3},{3,5},... | collective-permute-start | bytes 221192 | tf_op jit(solution)/shard_map/ppermute | solution.py:111
  195.0 2.3 %copy-start.11 = (f32[1024]{0:T(1024)S(1)}, f32[1024]{0:T(1024)}, u32[]{:S(2)}) copy-start(f32[1024]{0:T(1024)} %param.17) | copy-start | bytes 12292
  199.6 9.8 %copy-start.14 = (bf16[1024,1536]{1,0:T(8,128)(2,1)S(1)}, bf16[1024,1536]{1,0:T(8,128)(2,1)}, u32[]{:S(2)}) copy-start(bf16[1024,1536]{1,0:T(8,128)(2,1)} %all-gather.3.cloned.1.call-done) | copy-start | bytes 9437188
  215.3 1.1 copy-start.1
Sparse Core Ops, SparseCore 0:
  84.1 84.2 all-gather.2

commit v2 on v1

--- a/solution.py
+++ b/solution.py
@@ -89,12 +89,8 @@
     return sent_to_all(pair, "zq")
 
 
-def over_plane(block, row_parts, col_parts):
-    quads, pairs, rows, cols = block.shape
-    whole = sent_to_all(block, ("x", "y"))
-    whole = whole.reshape(4, row_parts, col_parts, quads, pairs, rows, cols)
-    whole = whole.transpose(4, 3, 0, 1, 5, 2, 6)
-    return whole.reshape(-1, col_parts * cols)
+def over_plane(block):
+    return sent_to_all(block, ("x", "y")).reshape((4,) * 3 + block.shape[1:])
 
 
 def after(value, earlier):
@@ -130,34 +126,72 @@
     rim_rows = WIN_LAT // 2
     rim_cols = WIN_LON // 2
 
-    late_shard = jnp.concatenate([split_weight.reshape(32, -1), coarse_proj.T], axis=1)
-    late = lax.all_gather(late_shard, "x", axis=0, tiled=True)
-    late = lax.all_gather(late, ("za", "zq"), axis=0, tiled=True)
+    core = lax.axis_index("core")
     packed_width = 3 * fine_qkv.shape[2]
     first_shard = jnp.concatenate([fine_qkv.reshape(16, packed_width), fine_proj.T], axis=1)
-    first = over_depth(quartered(first_shard, 2, 2))
-    first_all = over_plane(first, 2, 2)
-    merge_depth = over_depth(after(quartered(merge_weight, 4, 1), first_all))
-    qkv_depth = over_depth(after(quartered(coarse_qkv.reshape(32, -1), 4, 1), merge_depth))
-    merge_all = over_plane(after(merge_depth, qkv_depth), 4, 1)
-    qkv_all = over_plane(after(qkv_depth, merge_all), 4, 1)
-
-    arriving = lon_shift(fine_tokens[:, :, :rim_cols], -1)
-    extended = jnp.concatenate([fine_tokens[:, :, rim_cols:], arriving], axis=2)
-    arriving = lat_shift(extended[:, :rim_rows], -1)
-    extended = jnp.concatenate([extended[:, rim_rows:], arriving], axis=1)
+    merge_part = quartered(merge_weight, 4, 1)
+    depth = over_depth(
+        jnp.concatenate(
+            [
+                quartered(first_shard, 2, 2),
+                merge_part[:8],
+                merge_part[8:],
+                quartered(coarse_qkv.reshape(32, -1), 4, 1),
+            ],
+            axis=1,
+        )
+    )
+    first_all = over_plane(depth[..., :640])
+    merge_all = over_plane(after(depth[..., 640:1664], first_all))
+    qkv_all = over_plane(after(depth[..., 1664:], merge_all))
+    first_all = first_all.reshape(4, 2, 2, 4, 2, 8, 640)
+    first_all = first_all.transpose(4, 3, 0, 1, 5, 2, 6).reshape(512, 1280)
+    merge_all = merge_all.reshape(4, 4, 4, 2, 8, 2, 512)
+    merge_all = merge_all.transpose(3, 2, 0, 1, 5, 4, 6).reshape(2048, 512)
+    qkv_all = qkv_all.transpose(3, 2, 0, 1, 4, 5).reshape(1024, 1536)
+
+    late_shard = jnp.concatenate([split_weight.reshape(32, -1), coarse_proj.T], axis=1)
+    late = lax.all_gather(jnp.pad(late_shard, ((0, 56), (0, 0))), "x", axis=0, tiled=False)
+    late = late[:, :32].reshape(128, 1536)
+    late = lax.all_gather(late, ("za", "zq"), axis=0, tiled=True)
+
+    own_half = lax.dynamic_slice_in_dim(
+        after(fine_tokens, depth), core * (features // 2), features // 2, 3
+    )
+    east = lon_shift(own_half[:, :, :rim_cols], -1)
+    west = lon_shift(own_half[:, :, col_count - rim_cols :], 1)
+    strip = jnp.concatenate([west, own_half, east], axis=2)
+    below = lat_shift(strip[:, :rim_rows], -1)
+    above = lat_shift(strip[:, row_count - rim_rows :], 1)
+    rims = [above, below, west, east]
+    flat_rims = lax.all_gather(
+        jnp.concatenate([rim.reshape(-1, features // 2) for rim in rims], axis=0),
+        "core",
+        axis=1,
+        tiled=True,
+    )
+    whole, place = [], 0
+    for rim in rims:
+        rows = rim.size // (features // 2)
+        whole.append(flat_rims[place : place + rows].reshape(rim.shape[:3] + (features,)))
+        place += rows
+    above, below, west, east = whole
+    extended = jnp.concatenate(
+        [above, jnp.concatenate([west, fine_tokens, east], axis=2), below], axis=1
+    )
+    wide_rows, wide_cols = extended.shape[1:3]
     normed = layer_norm(extended.reshape(-1, features).astype(jnp.float32), attn_gain).astype(
         jnp.bfloat16
     )
     fine_heads = fine_qkv.shape[2] // HEAD
     packed = project_with(normed, first_all[:, :packed_width])
-    packed = packed.astype(jnp.bfloat16).reshape(levels, row_count, col_count, packed_width)
-    global_rows = (row_first + rim_rows + jnp.arange(row_count, dtype=jnp.int32)) % lat_total
+    packed = packed.astype(jnp.bfloat16).reshape(levels, wide_rows, wide_cols, packed_width)
+    global_rows = row_first - rim_rows + jnp.arange(wide_rows, dtype=jnp.int32)
+    global_rows = (global_rows + lat_total) % lat_total
     window_out = window_mix(packed, fine_heads, seam_labels(global_rows, lat_total, rim_rows))
-    returning = lat_shift(window_out[:, row_count - rim_rows :], 1)
-    window_out = jnp.concatenate([returning, window_out[:, : row_count - rim_rows]], axis=1)
-    returning = lon_shift(window_out[:, :, col_count - rim_cols :], 1)
-    window_out = jnp.concatenate([returning, window_out[:, :, : col_count - rim_cols]], axis=2)
+    window_out = window_out[
+        :, rim_rows : rim_rows + row_count, rim_cols : rim_cols + col_count
+    ]
     all_heads = lax.all_gather(window_out, "core", axis=3, tiled=True).reshape(-1, features)
     attended = project_with_transposed(all_heads, first_all[:, packed_width:])
     flat_tokens = fine_tokens.reshape(-1, features)
@@ -190,7 +224,7 @@
     )
     average = first_sum / features
     spread = second_sum / features - average * average
-    feature_start = lax.axis_index("core") * feature_half
+    feature_start = core * feature_half
     gain_part = lax.dynamic_slice_in_dim(split_gain, feature_start, feature_half, 0)
     normed_split = (
         (expanded - average[..., None]) * lax.rsqrt(spread[..., None] + EPSILON) * gain_part

time: 225 us -> 223 us (level)
  the two profiles are of different devices: /device:TPU:57 before, /device:TPU:1 now
where the time goes in v2:
time: 223 us; the launch traced here: 222 us
  starting transfers between devices  67.4 us (30%)
  local copies, waits for them, and re-layouts  49 us (22%)
  waiting for transfers between devices  46.4 us (21%)
  blocking collectives  18.5 us (8%)
  between operations  14.2 us (6%)
  other arithmetic  13.7 us (6%)
  matrix products  13 us (6%)
    all_to_all x4, waiting for transfers between devices, sent_to_all(): return lax.all_to_all(copies, axes, split_axis=0, concat_axis=0, tiled=True)  31.2 us
    all_to_all x4, starting transfers between devices, sent_to_all(): return lax.all_to_all(copies, axes, split_axis=0, concat_axis=0, tiled=True)  23 us
    ppermute x2, starting transfers between devices, lat_shift(): return lax.ppermute(value, ('za', 'zq', 'x'), perm)  18.4 us
    ppermute x2, starting transfers between devices, lon_shift(): return lax.ppermute(value, ('y', 'zh'), perm)  16.1 us
    ppermute x1, starting transfers between devices, over_depth(): other = lax.ppermute(block, 'za', [(0, 1), (1, 0)])  9.65 us
    ppermute x2, waiting for transfers between devices, lon_shift(): return lax.ppermute(value, ('y', 'zh'), perm)  9.39 us
    unnamed x53, local copies, waits for them, and re-layouts  9.12 us
    another operation x2, local copies, waits for them, and re-layouts, window_mix(): packed.reshape(levels, window_rows, WIN_LAT, window_cols, WIN_LON, 3, hea...  7.28 us
  transfers between devices with their start and end apart: 11, of which 7 were waited for; matrix products, arithmetic and copies ran while one was open for 29% of the time, Pallas kernels for 0%

profile of v2, /device:TPU:1, one launch (start us, length us, event | category | flops | bytes accessed | tf_op | source)
XLA Modules:
  0.0 222.1 jit_solution(108275229791739605)
XLA Ops:
  7.3 0.9 copy.114
  9.0 9.6 %collective-permute-start = (bf16[8,3200]{1,0:T(8,128)(2,1)S(1)}, bf16[8,3200]{1,0:T(8,128)(2,1)S(1)}, u32[]{:S(2)}, u32[]{:S(2)}) collective-permute-start(bf16[8,3200]{1,0:T(8,128)(2,1)S(1)} %pad_maximum_fusion.5), channel_id=1, source_target_pairs={{0,256},{256,0},{1,257},{257,1},{2,258},{258,2},{3,259},{259,3},{4... | collective-permute-start | bytes 153608 | tf_op jit(solution)/shard_map/ppermute | solution.py:86
  18.7 1.5 collective-permute-done
  21.0 7.4 %all-to-all-start = ((bf16[4,2,8,3200]{3,2,1,0:T(8,128)(2,1)}), bf16[4,2,8,3200]{3,2,1,0:T(8,128)(2,1)S(1)}, u32[]{:S(2)}, u32[]{:S(2)}) async-start(bf16[4,2,8,3200]{3,2,1,0:T(8,128)(2,1)} %broadcast_in_dim.28), calls=%async_computation | async-start | bytes 819200 | tf_op jit(solution)/shard_map/all_to_all | solution.py:82
  29.4 8.6 %all-to-all-done = bf16[4,2,8,3200]{3,2,1,0:T(8,128)(2,1)S(1)} async-done(((bf16[4,2,8,3200]{3,2,1,0:T(8,128)(2,1)}), bf16[4,2,8,3200]{3,2,1,0:T(8,128)(2,1)S(1)}, u32[]{:S(2)}, u32[]{:S(2)}) %all-to-all-start) | async-done | bytes 409632 | tf_op jit(solution)/shard_map/all_to_all | solution.py:82
  38.1 8.4 %collective-permute-start.1 = (bf16[2,12,6,256]{3,2,1,0:T(8,128)(2,1)S(1)}, bf16[2,12,6,256]{3,2,1,0:T(8,128)(2,1)S(1)}, u32[]{:S(2)}, u32[]{:S(2)}) collective-permute-start(bf16[2,12,6,256]{3,2,1,0:T(8,128)(2,1)S(1)} %get-tuple-element.18), channel_id=1, source_target_pairs={{0,2},{2,4},{4,6},{6,8},{8,10},{10,12},{12,14},{14,0},{1,3},{3,5},... | collective-permute-start | bytes 221192 | tf_op jit(solution)/shard_map/ppermute | solution.py:107
  46.5 7.7 %collective-permute-start.2 = (bf16[2,12,6,256]{3,2,1,0:T(8,128)(2,1)S(1)}, bf16[2,12,6,256]{3,2,1,0:T(8,128)(2,1)S(1)}, u32[]{:S(2)}, u32[]{:S(2)}) collective-permute-start(bf16[2,12,6,256]{3,2,1,0:T(8,128)(2,1)S(1)} %get-tuple-element.19), channel_id=1, source_target_pairs={{0,14},{2,0},{4,2},{6,4},{8,6},{10,8},{12,10},{14,12},{1,15},{3,1}... | collective-permute-start | bytes 221192 | tf_op jit(solution)/shard_map/ppermute | solution.py:107
  54.4 9.3 %collective-permute-done.2 = bf16[2,12,6,256]{3,2,1,0:T(8,128)(2,1)S(1)} collective-permute-done((bf16[2,12,6,256]{3,2,1,0:T(8,128)(2,1)S(1)}, bf16[2,12,6,256]{3,2,1,0:T(8,128)(2,1)S(1)}, u32[]{:S(2)}, u32[]{:S(2)}) %collective-permute-start.2) | collective-permute-done | bytes 73760 | tf_op jit(solution)/shard_map/ppermute | solution.py:107
  63.7 2.5 %collective-permute-start.3 = (bf16[2,3,36,256]{3,2,1,0:T(8,128)(2,1)S(1)}, bf16[2,3,36,256]{3,2,1,0:T(8,128)(2,1)S(1)}, u32[]{:S(2)}, u32[]{:S(2)}) collective-permute-start(bf16[2,3,36,256]{3,2,1,0:T(8,128)(2,1)S(1)} %get-tuple-element.20), channel_id=1, source_target_pairs={{0,16},{16,32},{32,48},{48,64},{64,80},{80,96},{96,112},{112,128},... | collective-permute-start | bytes 331784 | tf_op jit(solution)/shard_map/ppermute | solution.py:102
  66.2 15.9 %collective-permute-start.4 = (bf16[2,3,36,256]{3,2,1,0:T(8,128)(2,1)S(1)}, bf16[2,3,36,256]{3,2,1,0:T(8,128)(2,1)S(1)}, u32[]{:S(2)}, u32[]{:S(2)}) collective-permute-start(bf16[2,3,36,256]{3,2,1,0:T(8,128)(2,1)S(1)} %get-tuple-element.21), channel_id=1, source_target_pairs={{0,496},{16,0},{32,16},{48,32},{64,48},{80,64},{96,80},{112,96},{1... | collective-permute-start | bytes 331784 | tf_op jit(solution)/shard_map/ppermute | solution.py:102
  82.1 1.0 broadcast_compare_fusion
  84.4 1.2 broadcast_in_dim.29
  85.6 4.3 %all-to-all-start.1 = ((bf16[16,4,2,8,640]{4,3,2,1,0:T(8,128)(2,1)}), bf16[16,4,2,8,640]{4,3,2,1,0:T(8,128)(2,1)S(1)}, u32[]{:S(2)}, u32[]{:S(2)}) async-start(bf16[16,4,2,8,640]{4,3,2,1,0:T(8,128)(2,1)} %broadcast_in_dim.29), calls=%async_computation.1 | async-start | bytes 2621440 | tf_op jit(solution)/shard_map/all_to_all | solution.py:82
  90.8 4.3 %all_gather.24 = bf16[720,512]{1,0:T(8,128)(2,1)S(1)} all-gather(bf16[720,256]{1,0:T(8,128)(2,1)S(1)} %pad_maximum_fusion), channel_id=1, replica_groups=mesh['za'=2,'zq'=4,'x'=4,'y'=4,'zh'=2,'core'=2] {'core'}, dimensions={1}, use_global_device_ids=true | all-gather | bytes 1105920 | tf_op jit(solution)/shard_map/all_gather | solution.py:167
  96.0 0.9 multiply_reduce_fusion
  96.9 10.4 %all-to-all-done.1 = bf16[16,4,2,8,640]{4,3,2,1,0:T(8,128)(2,1)S(1)} async-done(((bf16[16,4,2,8,640]{4,3,2,1,0:T(8,128)(2,1)}), bf16[16,4,2,8,640]{4,3,2,1,0:T(8,128)(2,1)S(1)}, u32[]{:S(2)}, u32[]{:S(2)}) %all-to-all-start.1) | async-done | bytes 1310752 | tf_op jit(solution)/shard_map/all_to_all | solution.py:82
  107.4 1.9 broadcast_in_dim.39
  109.3 4.5 %all-to-all-start.2 = ((bf16[16,4,2,8,1024]{4,3,2,1,0:T(8,128)(2,1)}), bf16[16,4,2,8,1024]{4,3,2,1,0:T(8,128)(2,1)}, u32[]{:S(2)}, u32[]{:S(2)}) async-start(bf16[16,4,2,8,1024]{4,3,2,1,0:T(8,128)(2,1)} %broadcast_in_dim.39), calls=%async_computation.2 | async-start | bytes 4194304 | tf_op jit(solution)/shard_map/all_to_all | solution.py:82
  114.2 1.7 maximum_convert_fusion
  115.9 1.7 reshape.270
  117.6 1.8 slice.126
  119.4 2.8 %copy.85 = bf16[2,4,4,2,8,2,640]{6,5,4,3,2,1,0:T(2,128)(2,1)S(1)} copy(bf16[2,4,4,2,8,2,640]{6,4,0,1,5,3,2:T(8,128)(2,1)} %bitcast.107) | data formatting | bytes 2621440 | tf_op jit(solution)/shard_map/transpose | solution.py:148
  122.5 1.1 copy-done.11
  123.5 1.3 convolution_convert_fusion
  124.9 3.6 %reshape_reshape.10 = bf16[2,3,6,3,12,3,4,64]{7,6,5,4,3,2,1,0:T(4,128)(2,1)} reshape(bf16[1296,768]{1,0:T(8,128)(2,1)S(1)} %convolution_convert_fusion) | data formatting | bytes 3981312 | tf_op jit(solution)/shard_map/reshape;reshape | solution.py:33
  128.4 3.7 %copy.86 = bf16[2,3,6,3,12,3,4,64]{7,6,5,4,2,0,3,1:T(4,128)(2,1)S(1)} copy(bf16[2,3,6,3,12,3,4,64]{7,6,5,4,3,2,1,0:T(4,128)(2,1)} %reshape_reshape.10) | data formatting | bytes 3981312 | tf_op jit(solution)/shard_map/reshape;reshape | solution.py:33
  132.1 2.5 %fusion.48 = (bf16[9,144,1,4,64]{4,3,2,1,0:T(4,128)(2,1)S(1)}, bf16[9,144,1,4,64]{4,3,2,1,0:T(4,128)(2,1)}, bf16[9,144,1,4,64]{4,3,2,1,0:T(4,128)(2,1)S(1)}) fusion(bf16[9,144,3,4,64]{4,3,2,1,0:T(4,128)(2,1)S(1)} %bitcast.102), kind=kLoop, calls=%fused_computation.102 | loop fusion | bytes 3981312 | tf_op jit(solution)/shard_map/slice | solution.py:53
  134.6 3.5 %copy.111 = bf16[9,144,1,4,64]{1,4,3,0,2:T(8,128)(2,1)} copy(bf16[9,144,1,4,64]{4,3,2,1,0:T(4,128)(2,1)} %get-tuple-element.12) | data formatting | bytes 1327104
  138.1 2.1 copy.112
  140.2 2.1 copy.110
  142.4 2.2 %fusion.17 = f32[9,4,144,144]{2,3,1,0:T(8,128)S(1)} fusion(bf16[9,144,1,4,64]{1,4,3,0,2:T(8,128)(2,1)} %copy.112, bf16[9,144,1,4,64]{1,4,3,0,2:T(8,128)(2,1)S(1)} %copy-done.2), kind=kOutput, calls=%fused_computation.31 | convolution fusion | flops 95551488 | bytes 4313088 | tf_op jit(solution)/shard_map/wqhd,wkhd->whqk/dot_general | solution.py:39
  144.6 4.0 %fusion.51 = (f32[9,4,144]{2,1,0:T(4,128)S(1)}, f32[9,4,144,144]{2,3,1,0:T(8,128)}) fusion(f32[9,4,144,144]{2,3,1,0:T(8,128)S(1)} %fusion.17, pred[9,144,144]{1,2,0:T(8,128)(4,1)S(1)} %copy-done.14), kind=kOutput, calls=%fused_computation.105 | output fusion | flops 4479119 | bytes 6179328 | tf_op jit(solution)/shard_map/sub | solution.py:50
  148.6 2.1 broadcast_in_dim.40
  150.7 6.8 %all-to-all-start.3 = ((bf16[16,4,2,8,1536]{4,3,1,2,0:T(8,128)(2,1)}), bf16[16,4,2,8,1536]{4,3,1,2,0:T(8,128)(2,1)}, u32[]{:S(2)}, u32[]{:S(2)}) async-start(bf16[16,4,2,8,1536]{4,3,1,2,0:T(8,128)(2,1)} %broadcast_in_dim.40), calls=%async_computation.3 | async-start | bytes 6291456 | tf_op jit(solution)/shard_map/all_to_all | solution.py:82
  157.5 3.1 %fusion.12 = bf16[9,144,4,64]{1,3,2,0:T(8,128)(2,1)S(1)} fusion(f32[9,4,144,144]{2,3,1,0:T(8,128)} %get-tuple-element.29, f32[9,4,144]{2,1,0:T(4,128)S(1)} %get-tuple-element.28, bf16[9,144,1,4,64]{1,4,3,0,2:T(8,128)(2,1)S(1)} %copy-done.12), kind=kOutput, calls=%fused_computation.22 | convolution fusion | flops 97376256 | bytes 4333824 | tf_op jit(solution)/shard_map/whqk,wkhd->wqhd/dot_general | solution.py:52
  160.6 1.0 copy.91
  161.6 0.9 reshape.254
  163.4 6.0 %all_gather.25 = bf16[2,12,24,512]{3,0,2,1:T(2,128)(2,1)S(1)} all-gather(bf16[2,12,24,256]{3,0,2,1:T(2,128)(2,1)S(1)} %slice.119), channel_id=1, replica_groups=mesh['za'=2,'zq'=4,'x'=4,'y'=4,'zh'=2,'core'=2] {'core'}, dimensions={3}, use_global_device_ids=true | all-gather | bytes 884736 | tf_op jit(solution)/shard_map/all_gather | solution.py:195
  169.5 1.5 fusion.16
  172.3 1.0 multiply_reduce_fusion.1
  174.5 3.3 %reshape_reshape.11 = bf16[4,4,4,2,8,2,512]{6,5,4,3,2,1,0:T(2,128)(2,1)S(1)} reshape(bf16[16,4,2,8,1024]{4,3,2,1,0:T(8,128)(2,1)} %all-to-all-done.2) | data formatting | bytes 4194304 | tf_op jit(solution)/shard_map/reshape;reshape | solution.py:149
  178.8 2.0 all_gather.26
  181.3 12.1 %all-to-all-done.3 = bf16[16,4,2,8,1536]{4,3,1,2,0:T(8,128)(2,1)} async-done(((bf16[16,4,2,8,1536]{4,3,1,2,0:T(8,128)(2,1)}), bf16[16,4,2,8,1536]{4,3,1,2,0:T(8,128)(2,1)}, u32[]{:S(2)}, u32[]{:S(2)}) %all-to-all-start.3) | async-done | bytes 3145760 | tf_op jit(solution)/shard_map/all_to_all | solution.py:82
  193.4 2.2 copy.97
  197.9 4.4 %all-gather.5.cloned.1.call-done = bf16[1024,1536]{1,0:T(8,128)(2,1)} async-done(((bf16[128,1536]{1,0:T(8,128)(2,1)}), bf16[1024,1536]{1,0:T(8,128)(2,1)}) %all-gather.5.cloned.1.call-update) | async-done | bytes 3145744 | tf_op jit(solution)/shard_map/all_gather | solution.py:156
  202.3 1.9 convolution_convert_fusion.2
  204.1 3.7 %all-gather.1 = bf16[288,1024]{1,0:T(8,128)(2,1)S(1)} all-gather(bf16[144,1024]{1,0:T(8,128)(2,1)S(1)} %convolution_convert_fusion.2), channel_id=3, replica_groups=mesh['za'=2,'zq'=4,'x'=4,'y'=4,'zh'=2,'core'=2] {'core'}, dimensions={0}, use_global_device_ids=true | all-gather | bytes 884736 | tf_op jit(solution)/shard_map/all_gather | solution.py:217
  209.8 2.5 %all-reduce.1 = (f32[144,4]{0,1:T(4,128)S(1)}, f32[144,4]{0,1:T(4,128)S(1)}) all-reduce(f32[144,4]{0,1:T(4,128)S(1)} %copy.104, f32[144,4]{0,1:T(4,128)S(1)} %copy.102), channel_id=1, replica_groups=mesh['za'=2,'zq'=4,'x'=4,'y'=4,'zh'=2,'core'=2] {'core'}, use_global_device_ids=true, to_apply=%region_13.14 | all-reduce | flops 1152 | bytes 9216 | tf_op jit(solution)/shard_map/psum | solution.py:222
  (131 shorter events, 19.1 us)
Async XLA Ops:
  6.5 21.9 %copy-start.15 = (bf16[32,4,256]{2,1,0:T(4,128)(2,1)S(1)}, bf16[32,4,256]{2,1,0:T(4,128)(2,1)}, u32[]{:S(2)}) copy-start(bf16[32,4,256]{2,1,0:T(4,128)(2,1)} %param.20) | copy-start | bytes 196612
  6.5 21.9 %copy-start.17 = (bf16[512,32]{0,1:T(8,128)(2,1)S(1)}, bf16[512,32]{0,1:T(8,128)(2,1)}, u32[]{:S(2)}) copy-start(bf16[512,32]{0,1:T(8,128)(2,1)} %param.19) | copy-start | bytes 98308
  6.5 31.4 %copy-start = (bf16[2,12,24,512]{3,2,1,0:T(8,128)(2,1)S(1)}, bf16[2,12,24,512]{3,2,1,0:T(8,128)(2,1)}, u32[]{:S(2)}) copy-start(bf16[2,12,24,512]{3,2,1,0:T(8,128)(2,1)} %param.11) | copy-start | bytes 1769476
  9.0 11.1 %collective-permute-start = (bf16[8,3200]{1,0:T(8,128)(2,1)S(1)}, bf16[8,3200]{1,0:T(8,128)(2,1)S(1)}, u32[]{:S(2)}, u32[]{:S(2)}) collective-permute-start(bf16[8,3200]{1,0:T(8,128)(2,1)S(1)} %pad_maximum_fusion.5), channel_id=1, source_target_pairs={{0,256},{256,0},{1,257},{257,1},{2,258},{258,2},{3,259},{259,3},{4... | collective-permute-start | bytes 153608 | tf_op jit(solution)/shard_map/ppermute | solution.py:86
  20.2 62.9 %copy-start.18 = (f32[2048]{0:T(1024)S(1)}, f32[2048]{0:T(1024)}, u32[]{:S(2)}) copy-start(f32[2048]{0:T(1024)} %param.15) | copy-start | bytes 24580
  20.2 63.5 %copy-start.21 = (f32[512]{0:T(512)S(1)}, f32[512]{0:T(512)}, u32[]{:S(2)}) copy-start(f32[512]{0:T(512)} %param.21) | copy-start | bytes 6148
  21.0 17.0 %all-to-all-start = ((bf16[4,2,8,3200]{3,2,1,0:T(8,128)(2,1)}), bf16[4,2,8,3200]{3,2,1,0:T(8,128)(2,1)S(1)}, u32[]{:S(2)}, u32[]{:S(2)}) async-start(bf16[4,2,8,3200]{3,2,1,0:T(8,128)(2,1)} %broadcast_in_dim.28), calls=%async_computation | async-start | bytes 819200 | tf_op jit(solution)/shard_map/all_to_all | solution.py:82
  28.4 89.2 %all-gather.7.cloned.1.call-start = ((), (), s32[]{:S(2)}) async-start(), calls=%async_computation.5 | async-start | bytes 1351680 | tf_op jit(solution)/shard_map/all_gather | solution.py:154
  38.0 51.9 %copy-start.8 = (bf16[4,2,8,3200]{3,2,1,0:T(8,128)(2,1)}, bf16[4,2,8,3200]{3,2,1,0:T(8,128)(2,1)S(1)}, u32[]{:S(2)}) copy-start(bf16[4,2,8,3200]{3,2,1,0:T(8,128)(2,1)S(1)} %all-to-all-done) | copy-start | bytes 1228804
  38.1 16.3 %collective-permute-start.1 = (bf16[2,12,6,256]{3,2,1,0:T(8,128)(2,1)S(1)}, bf16[2,12,6,256]{3,2,1,0:T(8,128)(2,1)S(1)}, u32[]{:S(2)}, u32[]{:S(2)}) collective-permute-start(bf16[2,12,6,256]{3,2,1,0:T(8,128)(2,1)S(1)} %get-tuple-element.18), channel_id=1, source_target_pairs={{0,2},{2,4},{4,6},{6,8},{8,10},{10,12},{12,14},{14,0},{1,3},{3,5},... | collective-permute-start | bytes 221192 | tf_op jit(solution)/shard_map/ppermute | solution.py:107
  46.5 17.2 %collective-permute-start.2 = (bf16[2,12,6,256]{3,2,1,0:T(8,128)(2,1)S(1)}, bf16[2,12,6,256]{3,2,1,0:T(8,128)(2,1)S(1)}, u32[]{:S(2)}, u32[]{:S(2)}) collective-permute-start(bf16[2,12,6,256]{3,2,1,0:T(8,128)(2,1)S(1)} %get-tuple-element.19), channel_id=1, source_target_pairs={{0,14},{2,0},{4,2},{6,4},{8,6},{10,8},{12,10},{14,12},{1,15},{3,1}... | collective-permute-start | bytes 221192 | tf_op jit(solution)/shard_map/ppermute | solution.py:107
  63.7 27.0 %collective-permute-start.3 = (bf16[2,3,36,256]{3,2,1,0:T(8,128)(2,1)S(1)}, bf16[2,3,36,256]{3,2,1,0:T(8,128)(2,1)S(1)}, u32[]{:S(2)}, u32[]{:S(2)}) collective-permute-start(bf16[2,3,36,256]{3,2,1,0:T(8,128)(2,1)S(1)} %get-tuple-element.20), channel_id=1, source_target_pairs={{0,16},{16,32},{32,48},{48,64},{64,80},{80,96},{96,112},{112,128},... | collective-permute-start | bytes 331784 | tf_op jit(solution)/shard_map/ppermute | solution.py:102
  66.2 24.6 %collective-permute-start.4 = (bf16[2,3,36,256]{3,2,1,0:T(8,128)(2,1)S(1)}, bf16[2,3,36,256]{3,2,1,0:T(8,128)(2,1)S(1)}, u32[]{:S(2)}, u32[]{:S(2)}) collective-permute-start(bf16[2,3,36,256]{3,2,1,0:T(8,128)(2,1)S(1)} %get-tuple-element.21), channel_id=1, source_target_pairs={{0,496},{16,0},{32,16},{48,32},{64,48},{80,64},{96,80},{112,96},{1... | collective-permute-start | bytes 331784 | tf_op jit(solution)/shard_map/ppermute | solution.py:102
  85.6 21.8 %all-to-all-start.1 = ((bf16[16,4,2,8,640]{4,3,2,1,0:T(8,128)(2,1)}), bf16[16,4,2,8,640]{4,3,2,1,0:T(8,128)(2,1)S(1)}, u32[]{:S(2)}, u32[]{:S(2)}) async-start(bf16[16,4,2,8,640]{4,3,2,1,0:T(8,128)(2,1)} %broadcast_in_dim.29), calls=%async_computation.1 | async-start | bytes 2621440 | tf_op jit(solution)/shard_map/all_to_all | solution.py:82
  95.2 1.7 copy-start.3
  95.3 1.7 copy-start.4
  95.3 12.1 %slice-start = ((bf16[4,2,8,3200]{3,2,1,0:T(8,128)(2,1)}), bf16[4,2,8,1024]{3,2,1,0:T(8,128)(2,1)S(1)}, s32[]{:S(2)}) async-start(bf16[4,2,8,3200]{3,2,1,0:T(8,128)(2,1)} %copy-done.8), calls=%async_computation.6 | async-start | bytes 262144 | tf_op jit(solution)/shard_map/slice | solution.py:145
  95.4 13.9 %copy-start.5 = (bf16[2,12,6,512]{3,2,1,0:T(8,128)(2,1)}, bf16[2,12,6,512]{3,2,1,0:T(8,128)(2,1)S(1)}, u32[]{:S(2)}) copy-start(bf16[2,12,6,512]{3,2,1,0:T(8,128)(2,1)S(1)} %reshape.249) | copy-start | bytes 442372
  95.4 13.8 %copy-start.6 = (bf16[2,12,6,512]{3,2,1,0:T(8,128)(2,1)}, bf16[2,12,6,512]{3,2,1,0:T(8,128)(2,1)S(1)}, u32[]{:S(2)}) copy-start(bf16[2,12,6,512]{3,2,1,0:T(8,128)(2,1)S(1)} %reshape.250) | copy-start | bytes 442372
  107.4 1.9 copy-start.1
  109.3 39.3 %all-to-all-start.2 = ((bf16[16,4,2,8,1024]{4,3,2,1,0:T(8,128)(2,1)}), bf16[16,4,2,8,1024]{4,3,2,1,0:T(8,128)(2,1)}, u32[]{:S(2)}, u32[]{:S(2)}) async-start(bf16[16,4,2,8,1024]{4,3,2,1,0:T(8,128)(2,1)} %broadcast_in_dim.39), calls=%async_computation.2 | async-start | bytes 4194304 | tf_op jit(solution)/shard_map/all_to_all | solution.py:82
  113.8 88.5 %all-gather.5.cloned.1.call-start = ((), (), s32[]{:S(2)}) async-start(), calls=%async_computation.4 | async-start | bytes 3538944 | tf_op jit(solution)/shard_map/all_gather | solution.py:156
  119.4 4.1 %copy-start.7 = (f32[1296,512]{1,0:T(8,128)S(1)}, f32[1296,512]{1,0:T(8,128)}, u32[]{:S(2)}) copy-start(f32[1296,512]{1,0:T(8,128)} %reshape.270) | copy-start | bytes 7962628
  119.4 4.1 %copy-start.23 = (f32[512]{0:T(512)S(1)}, f32[512]{0:T(512)}, u32[]{:S(2)}) copy-start(f32[512]{0:T(512)} %param.12) | copy-start | bytes 6148
  122.5 1.1 copy-start.11
  140.2 2.1 copy-start.2
  142.4 2.2 %copy-start.14 = (pred[9,144,144]{1,2,0:T(8,128)(4,1)S(1)}, pred[9,144,144]{1,2,0:T(8,128)(4,1)}, u32[]{:S(2)}) copy-start(pred[9,144,144]{1,2,0:T(8,128)(4,1)} %broadcast_compare_fusion) | copy-start | bytes 559876
  144.6 4.0 %copy-start.13 = (bf16[4,2,8,1536]{3,2,0,1:T(8,128)(2,1)S(1)}, bf16[4,2,8,1536]{3,2,0,1:T(8,128)(2,1)}, u32[]{:S(2)}) copy-start(bf16[4,2,8,1536]{3,2,0,1:T(8,128)(2,1)} %copy.96) | copy-start | bytes 589828
  150.7 6.8 %copy-start.12 = (bf16[9,144,1,4,64]{1,4,3,0,2:T(8,128)(2,1)S(1)}, bf16[9,144,1,4,64]{1,4,3,0,2:T(8,128)(2,1)}, u32[]{:S(2)}) copy-start(bf16[9,144,1,4,64]{1,4,3,0,2:T(8,128)(2,1)} %copy.110) | copy-start | bytes 1990660
  150.7 42.7 %all-to-all-start.3 = ((bf16[16,4,2,8,1536]{4,3,1,2,0:T(8,128)(2,1)}), bf16[16,4,2,8,1536]{4,3,1,2,0:T(8,128)(2,1)}, u32[]{:S(2)}, u32[]{:S(2)}) async-start(bf16[16,4,2,8,1536]{4,3,1,2,0:T(8,128)(2,1)} %broadcast_in_dim.40), calls=%async_computation.3 | async-start | bytes 6291456 | tf_op jit(solution)/shard_map/all_to_all | solution.py:82
  171.1 3.0 %copy-start.9 = (bf16[576,512]{1,0:T(8,128)(2,1)}, bf16[576,512]{1,0:T(8,128)(2,1)S(1)}, u32[]{:S(2)}) copy-start(bf16[576,512]{1,0:T(8,128)(2,1)S(1)} %fusion.16) | copy-start | bytes 1769476
  171.1 2.2 copy-start.16
  181.2 14.4 %copy-start.20 = (f32[1024]{0:T(1024)S(1)}, f32[1024]{0:T(1024)}, u32[]{:S(2)}) copy-start(f32[1024]{0:T(1024)} %param.17) | copy-start | bytes 12292
  202.3 5.7 %copy-start.22 = (bf16[1024,1536]{1,0:T(8,128)(2,1)S(1)}, bf16[1024,1536]{1,0:T(8,128)(2,1)}, u32[]{:S(2)}) copy-start(bf16[1024,1536]{1,0:T(8,128)(2,1)} %all-gather.5.cloned.1.call-done) | copy-start | bytes 9437188
  208.5 4.6 %copy-start.19 = (f32[256]{0:T(256)S(1)}, f32[256]{0:T(256)}, u32[]{:S(2)}) copy-start(f32[256]{0:T(256)} %dynamic_slice.25) | copy-start | bytes 3076
  212.4 2.0 copy-start.10
Sparse Core Ops, SparseCore 0:
  31.3 34.6 all-gather.6
  119.5 82.6 all-gather.4

commit v3 on v2

--- a/solution.py
+++ b/solution.py
@@ -1,6 +1,8 @@
 import jax
 import jax.numpy as jnp
 from jax import lax
+from jax.experimental import pallas as pl
+from jax.experimental.pallas import tpu as pltpu
 from jax.sharding import Mesh, PartitionSpec as P
 
 HEAD = 64
@@ -93,10 +95,6 @@
     return sent_to_all(block, ("x", "y")).reshape((4,) * 3 + block.shape[1:])
 
 
-def after(value, earlier):
-    return lax.optimization_barrier((value, earlier))[0]
-
-
 def lat_shift(value, by):
     perm = [(i, (i + by) % 32) for i in range(32)]
     return lax.ppermute(value, ("za", "zq", "x"), perm)
@@ -105,6 +103,56 @@
 def lon_shift(value, by):
     perm = [(i, (i + by) % 8) for i in range(8)]
     return lax.ppermute(value, ("y", "zh"), perm)
+
+
+def window_kernel(tokens, left_weight, right_weight, bias, out):
+    normed = tokens[0]
+    left = jnp.dot(normed, left_weight[...], preferred_element_type=jnp.float32)
+    left = left.astype(jnp.bfloat16)
+    right = jnp.dot(normed, right_weight[:, :128], preferred_element_type=jnp.float32)
+    right = right.astype(jnp.bfloat16)
+    lower = lax.broadcasted_iota(jnp.int32, (1, 2 * HEAD), 1) < HEAD
+    values = (left[:, 512:640], right)
+    for pair in range(2):
+        query = left[:, 128 * pair : 128 * (pair + 1)]
+        keys = left[:, 256 + 128 * pair : 256 + 128 * (pair + 1)]
+        mixed = []
+        for keep in (lower, ~lower):
+            kept = query * jnp.where(keep, HEAD**-0.5, 0.0).astype(jnp.bfloat16)
+            scores = lax.dot_general(
+                kept, keys, (((1,), (1,)), ((), ())), preferred_element_type=jnp.float32
+            )
+            scores = scores + bias[0]
+            weights = jnp.exp(scores - jnp.max(scores, axis=-1, keepdims=True))
+            total = jnp.sum(weights, axis=-1, keepdims=True)
+            mixed.append(
+                jnp.dot(
+                    weights.astype(jnp.bfloat16), values[pair], preferred_element_type=jnp.float32
+                )
+                / total
+            )
+        out[0, :, 128 * pair : 128 * (pair + 1)] = jnp.where(lower, *mixed).astype(jnp.bfloat16)
+
+
+def fine_windows(tokens, left_weight, right_weight, bias):
+    windows, size, features = tokens.shape
+    flops = 2 * windows * size * (features * 768 + 4 * size * 128 * 2)
+    return pl.pallas_call(
+        window_kernel,
+        grid=(windows,),
+        in_specs=[
+            pl.BlockSpec((1, size, features), lambda i: (i, 0, 0)),
+            pl.BlockSpec(left_weight.shape, lambda i: (0, 0)),
+            pl.BlockSpec(right_weight.shape, lambda i: (0, 0)),
+            pl.BlockSpec((1, size, size), lambda i: (i // 3, 0, 0)),
+        ],
+        out_specs=pl.BlockSpec((1, size, 256), lambda i: (i, 0, 0)),
+        out_shape=jax.ShapeDtypeStruct((windows, size, 256), jnp.bfloat16),
+        compiler_params=pltpu.CompilerParams(vmem_limit_bytes=16 * 2**20),
+        cost_estimate=pl.CostEstimate(
+            flops=flops, bytes_accessed=4 * 2**20, transcendentals=windows * 4 * size * size
+        ),
+    )(tokens, left_weight, right_weight, bias)
 
 
 def body(
@@ -130,33 +178,24 @@
     packed_width = 3 * fine_qkv.shape[2]
     first_shard = jnp.concatenate([fine_qkv.reshape(16, packed_width), fine_proj.T], axis=1)
     merge_part = quartered(merge_weight, 4, 1)
-    depth = over_depth(
-        jnp.concatenate(
-            [
-                quartered(first_shard, 2, 2),
-                merge_part[:8],
-                merge_part[8:],
-                quartered(coarse_qkv.reshape(32, -1), 4, 1),
-            ],
-            axis=1,
-        )
-    )
-    first_all = over_plane(depth[..., :640])
-    merge_all = over_plane(after(depth[..., 640:1664], first_all))
-    qkv_all = over_plane(after(depth[..., 1664:], merge_all))
-    first_all = first_all.reshape(4, 2, 2, 4, 2, 8, 640)
-    first_all = first_all.transpose(4, 3, 0, 1, 5, 2, 6).reshape(512, 1280)
-    merge_all = merge_all.reshape(4, 4, 4, 2, 8, 2, 512)
-    merge_all = merge_all.transpose(3, 2, 0, 1, 5, 4, 6).reshape(2048, 512)
-    qkv_all = qkv_all.transpose(3, 2, 0, 1, 4, 5).reshape(1024, 1536)
-
     late_shard = jnp.concatenate([split_weight.reshape(32, -1), coarse_proj.T], axis=1)
-    late = lax.all_gather(jnp.pad(late_shard, ((0, 56), (0, 0))), "x", axis=0, tiled=False)
+    late_shard = jnp.pad(late_shard, ((0, 56), (0, 0)))
+    early = jnp.concatenate(
+        [
+            quartered(first_shard, 2, 2),
+            merge_part[:8],
+            merge_part[8:],
+            quartered(coarse_qkv.reshape(32, -1), 4, 1),
+        ],
+        axis=1,
+    )
+    early, late_shard = lax.optimization_barrier((early, late_shard))
+    depth = over_depth(early)
+    late = lax.all_gather(late_shard, "x", axis=0, tiled=False)
     late = late[:, :32].reshape(128, 1536)
-    late = lax.all_gather(late, ("za", "zq"), axis=0, tiled=True)
 
     own_half = lax.dynamic_slice_in_dim(
-        after(fine_tokens, depth), core * (features // 2), features // 2, 3
+        fine_tokens, core * (features // 2), features // 2, 3
     )
     east = lon_shift(own_half[:, :, :rim_cols], -1)
     west = lon_shift(own_half[:, :, col_count - rim_cols :], 1)
@@ -180,20 +219,40 @@
         [above, jnp.concatenate([west, fine_tokens, east], axis=2), below], axis=1
     )
     wide_rows, wide_cols = extended.shape[1:3]
-    normed = layer_norm(extended.reshape(-1, features).astype(jnp.float32), attn_gain).astype(
-        jnp.bfloat16
-    )
-    fine_heads = fine_qkv.shape[2] // HEAD
-    packed = project_with(normed, first_all[:, :packed_width])
-    packed = packed.astype(jnp.bfloat16).reshape(levels, wide_rows, wide_cols, packed_width)
+    window_rows, window_cols = wide_rows // WIN_LAT, wide_cols // WIN_LON
+    size = levels * WIN_LAT * WIN_LON
+    normed = layer_norm(extended.astype(jnp.float32), attn_gain).astype(jnp.bfloat16)
+    normed = normed.reshape(levels, window_rows, WIN_LAT, window_cols, WIN_LON, features)
+    normed = normed.transpose(1, 3, 0, 2, 4, 5).reshape(-1, size, features)
     global_rows = row_first - rim_rows + jnp.arange(wide_rows, dtype=jnp.int32)
     global_rows = (global_rows + lat_total) % lat_total
-    window_out = window_mix(packed, fine_heads, seam_labels(global_rows, lat_total, rim_rows))
+    labels = seam_labels(global_rows, lat_total, rim_rows).reshape(window_rows, 1, WIN_LAT, 1)
+    labels = jnp.broadcast_to(labels, (window_rows, levels, WIN_LAT, WIN_LON))
+    labels = labels.reshape(window_rows, size)
+    bias = jnp.where(labels[:, :, None] == labels[:, None, :], 0.0, -1e30).astype(jnp.float32)
+
+    depth, normed, bias, late = lax.optimization_barrier((depth, normed, bias, late))
+    first_all = over_plane(depth[..., :640])
+    late = lax.all_gather(late, ("za", "zq"), axis=0, tiled=True)
+    depth, first_all = lax.optimization_barrier((depth, first_all))
+    merge_all = over_plane(depth[..., 640:1664])
+    first_all = first_all.reshape(4, 2, 2, 4, 2, 8, 640)
+    left_weight, right_weight = (
+        first_all[:, :, part].transpose(3, 2, 0, 1, 4, 5).reshape(512, 640) for part in range(2)
+    )
+    window_out = fine_windows(normed, left_weight, right_weight, bias)
+    depth, window_out, merge_all = lax.optimization_barrier((depth, window_out, merge_all))
+    qkv_all = over_plane(depth[..., 1664:])
+    merge_all = jnp.stack([merge_all[..., :512], merge_all[..., 512:]], axis=4)
+    merge_all = merge_all.transpose(3, 2, 0, 1, 4, 5, 6).reshape(2048, 512)
+    qkv_all = qkv_all.transpose(3, 2, 0, 1, 4, 5).reshape(1024, 1536)
+    window_out = window_out.reshape(window_rows, window_cols, levels, WIN_LAT, WIN_LON, 256)
+    window_out = window_out.transpose(2, 0, 3, 1, 4, 5).reshape(levels, wide_rows, wide_cols, 256)
     window_out = window_out[
         :, rim_rows : rim_rows + row_count, rim_cols : rim_cols + col_count
     ]
     all_heads = lax.all_gather(window_out, "core", axis=3, tiled=True).reshape(-1, features)
-    attended = project_with_transposed(all_heads, first_all[:, packed_width:])
+    attended = project_with_transposed(all_heads, right_weight[:, 128:])
     flat_tokens = fine_tokens.reshape(-1, features)
     residual = (flat_tokens.astype(jnp.float32) + attended).astype(jnp.bfloat16)
     half_rows = row_count // 2

time: 223 us -> 237 us (1.063)
  the two profiles are of different devices: /device:TPU:1 before, /device:TPU:509 now
where the time goes in v3:
time: 237 us; the launch traced here: 235 us
  waiting for transfers between devices  68.5 us (29%)
  starting transfers between devices  45.5 us (19%)
  blocking collectives  44.3 us (19%)
  local copies, waits for them, and re-layouts  36.2 us (15%)
  other arithmetic  14.8 us (6%)
  between operations  14.2 us (6%)
  Pallas kernels  6.66 us (3%)
  matrix products  5.33 us (2%)
    all_to_all x3, waiting for transfers between devices, sent_to_all(): return lax.all_to_all(copies, axes, split_axis=0, concat_axis=0, tiled=True)  54.2 us
    all_to_all x1, blocking collectives, sent_to_all(): return lax.all_to_all(copies, axes, split_axis=0, concat_axis=0, tiled=True)  27.5 us
    all_to_all x3, starting transfers between devices, sent_to_all(): return lax.all_to_all(copies, axes, split_axis=0, concat_axis=0, tiled=True)  21 us
    ppermute x2, starting transfers between devices, lon_shift(): return lax.ppermute(value, ('y', 'zh'), perm)  14 us
    ppermute x2, waiting for transfers between devices, lat_shift(): return lax.ppermute(value, ('za', 'zq', 'x'), perm)  7.66 us
    pallas_call x1, Pallas kernels, fine_windows(): pl.pallas_call(window_kernel, grid=(windows,), in_specs=[pl.BlockSpec((1,...  6.66 us
    ppermute x1, waiting for transfers between devices, over_depth(): other = lax.ppermute(block, 'za', [(0, 1), (1, 0)])  5.82 us
    all_to_all x2, local copies, waits for them, and re-layouts, sent_to_all(): return lax.all_to_all(copies, axes, split_axis=0, concat_axis=0, tiled=True)  5.32 us
  transfers between devices with their start and end apart: 10, of which 4 were waited for; matrix products, arithmetic and copies ran while one was open for 19% of the time, Pallas kernels for 3%

profile of v3, /device:TPU:509, one launch (start us, length us, event | category | flops | bytes accessed | tf_op | source)
XLA Modules:
  0.0 235.5 jit_solution(3453653211067227113)
XLA Ops:
  6.5 1.1 constant_dynamic-slice_fusion.1
  7.7 5.7 %collective-permute-start.1 = (bf16[2,12,6,256]{3,2,1,0:T(8,128)(2,1)S(1)}, bf16[2,12,6,256]{3,2,1,0:T(8,128)(2,1)S(1)}, u32[]{:S(2)}, u32[]{:S(2)}) collective-permute-start(bf16[2,12,6,256]{3,2,1,0:T(8,128)(2,1)S(1)} %get-tuple-element.39), channel_id=1, source_target_pairs={{0,2},{2,4},{4,6},{6,8},{8,10},{10,12},{12,14},{14,0},{1,3},{3,5},... | collective-permute-start | bytes 221192 | tf_op jit(solution)/shard_map/ppermute | solution.py:105
  13.4 8.3 %collective-permute-start.2 = (bf16[2,12,6,256]{3,2,1,0:T(8,128)(2,1)S(1)}, bf16[2,12,6,256]{3,2,1,0:T(8,128)(2,1)S(1)}, u32[]{:S(2)}, u32[]{:S(2)}) collective-permute-start(bf16[2,12,6,256]{3,2,1,0:T(8,128)(2,1)S(1)} %get-tuple-element.40), channel_id=1, source_target_pairs={{0,14},{2,0},{4,2},{6,4},{8,6},{10,8},{12,10},{14,12},{1,15},{3,1}... | collective-permute-start | bytes 221192 | tf_op jit(solution)/shard_map/ppermute | solution.py:105
  21.7 0.7 copy.149
  22.4 0.9 copy.150
  23.3 0.8 copy.151
  24.2 0.7 constant_dynamic-slice_fusion.2
  24.9 1.5 fusion.22
  27.1 5.2 %collective-permute-start = (bf16[8,3200]{1,0:T(8,128)(2,1)S(1)}, bf16[8,3200]{1,0:T(8,128)(2,1)S(1)}, u32[]{:S(2)}, u32[]{:S(2)}) collective-permute-start(bf16[8,3200]{1,0:T(8,128)(2,1)S(1)} %pad_maximum_fusion.6), channel_id=1, source_target_pairs={{0,256},{256,0},{1,257},{257,1},{2,258},{258,2},{3,259},{259,3},{4... | collective-permute-start | bytes 153608 | tf_op jit(solution)/shard_map/ppermute | solution.py:88
  32.7 5.8 %collective-permute-done = bf16[8,3200]{1,0:T(8,128)(2,1)S(1)} collective-permute-done((bf16[8,3200]{1,0:T(8,128)(2,1)S(1)}, bf16[8,3200]{1,0:T(8,128)(2,1)S(1)}, u32[]{:S(2)}, u32[]{:S(2)}) %collective-permute-start) | collective-permute-done | bytes 51232 | tf_op jit(solution)/shard_map/ppermute | solution.py:88
  38.7 2.8 %collective-permute-start.3 = (bf16[2,3,36,256]{3,2,1,0:T(8,128)(2,1)S(1)}, bf16[2,3,36,256]{3,2,1,0:T(8,128)(2,1)S(1)}, u32[]{:S(2)}, u32[]{:S(2)}) collective-permute-start(bf16[2,3,36,256]{3,2,1,0:T(8,128)(2,1)S(1)} %get-tuple-element.41), channel_id=1, source_target_pairs={{0,16},{16,32},{32,48},{48,64},{64,80},{80,96},{96,112},{112,128},... | collective-permute-start | bytes 331784 | tf_op jit(solution)/shard_map/ppermute | solution.py:100
  41.5 2.5 %collective-permute-start.4 = (bf16[2,3,36,256]{3,2,1,0:T(8,128)(2,1)S(1)}, bf16[2,3,36,256]{3,2,1,0:T(8,128)(2,1)S(1)}, u32[]{:S(2)}, u32[]{:S(2)}) collective-permute-start(bf16[2,3,36,256]{3,2,1,0:T(8,128)(2,1)S(1)} %get-tuple-element.42), channel_id=1, source_target_pairs={{0,496},{16,0},{32,16},{48,32},{64,48},{80,64},{96,80},{112,96},{1... | collective-permute-start | bytes 331784 | tf_op jit(solution)/shard_map/ppermute | solution.py:100
  44.0 0.8 broadcast_in_dim.28
  44.8 5.1 %all-to-all-start = ((bf16[4,2,8,3200]{3,2,1,0:T(8,128)(2,1)}), bf16[4,2,8,3200]{3,2,1,0:T(8,128)(2,1)}, u32[]{:S(2)}, u32[]{:S(2)}) async-start(bf16[4,2,8,3200]{3,2,1,0:T(8,128)(2,1)} %broadcast_in_dim.28), calls=%async_computation | async-start | bytes 819200 | tf_op jit(solution)/shard_map/all_to_all | solution.py:84
  50.0 7.7 %collective-permute-done.4 = bf16[2,3,36,256]{3,2,1,0:T(8,128)(2,1)S(1)} collective-permute-done((bf16[2,3,36,256]{3,2,1,0:T(8,128)(2,1)S(1)}, bf16[2,3,36,256]{3,2,1,0:T(8,128)(2,1)S(1)}, u32[]{:S(2)}, u32[]{:S(2)}) %collective-permute-start.4) | collective-permute-done | bytes 110624 | tf_op jit(solution)/shard_map/ppermute | solution.py:100
  57.8 3.6 %all_gather.24 = bf16[720,512]{1,0:T(8,128)(2,1)S(1)} all-gather(bf16[720,256]{1,0:T(8,128)(2,1)S(1)} %pad_maximum_fusion.1), channel_id=1, replica_groups=mesh['za'=2,'zq'=4,'x'=4,'y'=4,'zh'=2,'core'=2] {'core'}, dimensions={1}, use_global_device_ids=true | all-gather | bytes 1105920 | tf_op jit(solution)/shard_map/all_gather | solution.py:206
  63.4 2.1 copy.118
  66.7 1.5 reshape.284
  68.1 2.0 multiply_reduce_fusion
  70.2 0.7 reshape.285
  70.9 1.3 copy.122
  72.2 2.1 copy.120
  74.3 3.0 %fusion.5 = bf16[3,3,2,6,12,512]{5,2,4,1,3,0:T(2,128)(2,1)S(1)} fusion(f32[512]{0:T(512)S(1)} %copy-done.12, f32[2,3,6,3,12]{0,4,3,2,1:T(8,128)S(1)} %copy.122, f32[2,3,6,3,12,512]{5,0,4,3,2,1:T(2,128)S(1)} %bitcast.107, f32[2,3,6,3,12]{0,4,3,2,1:T(8,128)} %copy.120), kind=kLoop, calls=%fused_computation.12 | loop fusion | flops 2654208 | bytes 3993728 | tf_op jit(solution)/shard_map/transpose | solution.py:226
  78.2 1.8 slice.114
  80.0 0.9 slice.92
  81.0 27.5 %all_to_all.20 = bf16[16,4,2,8,640]{4,3,2,1,0:T(8,128)(2,1)S(1)} all-to-all(bf16[16,4,2,8,640]{4,3,2,1,0:T(8,128)(2,1)S(1)} %broadcast_in_dim.34), channel_id=1, replica_groups=mesh['za'=2,'zq'=4,'x'=4,'y'=4,'zh'=2,'core'=2] {'x','y'}, dimensions={0} | all-to-all | bytes 2621440 | tf_op jit(solution)/shard_map/all_to_all | solution.py:84
  108.6 0.9 slice.95
  109.5 1.6 broadcast_in_dim.35
  111.1 7.8 %all-to-all-start.2 = ((bf16[16,4,2,8,1024]{4,3,1,2,0:T(8,128)(2,1)}), bf16[16,4,2,8,1024]{4,3,1,2,0:T(8,128)(2,1)}, u32[]{:S(2)}, u32[]{:S(2)}) async-start(bf16[16,4,2,8,1024]{4,3,1,2,0:T(8,128)(2,1)} %broadcast_in_dim.35), calls=%async_computation.2 | async-start | bytes 4194304 | tf_op jit(solution)/shard_map/all_to_all | solution.py:84
  120.1 6.7 %shard_map.109 = bf16[9,144,256]{2,1,0:T(8,128)(2,1)S(1)} custom-call(bf16[9,144,512]{2,1,0:T(8,128)(2,1)S(1)} %reshape.254.tokens, bf16[512,640]{1,0:T(8,128)(2,1)S(1)} %bitcast.105, bf16[512,640]{1,0:T(8,128)(2,1)S(1)} %bitcast.103, f32[3,144,144]{2,1,0:T(8,128)S(1)} %compare_select_fusion.bias), custom_call_target="tpu_custom_call" | custom-call | flops 1401421824 | bytes 4194304 | tf_op jit(solution)/shard_map/pallas_call | solution.py:140
  126.7 16.2 %all-to-all-done.2 = bf16[16,4,2,8,1024]{4,3,1,2,0:T(8,128)(2,1)} async-done(((bf16[16,4,2,8,1024]{4,3,1,2,0:T(8,128)(2,1)}), bf16[16,4,2,8,1024]{4,3,1,2,0:T(8,128)(2,1)}, u32[]{:S(2)}, u32[]{:S(2)}) %all-to-all-start.2) | async-done | bytes 2097184 | tf_op jit(solution)/shard_map/all_to_all | solution.py:84
  142.9 3.1 %copy.127 = bf16[16,4,2,8,1024]{4,3,0,1,2:T(8,128)(2,1)} copy(bf16[16,4,2,8,1024]{4,3,1,2,0:T(8,128)(2,1)} %all-to-all-done.2) | data formatting | bytes 4194304 | tf_op jit(solution)/shard_map/all_to_all | solution.py:84
  147.1 5.2 %all_gather.27 = bf16[2,12,24,512]{3,0,2,1:T(2,128)(2,1)S(1)} all-gather(bf16[2,12,24,256]{3,0,2,1:T(2,128)(2,1)S(1)} %slice.117), channel_id=1, replica_groups=mesh['za'=2,'zq'=4,'x'=4,'y'=4,'zh'=2,'core'=2] {'core'}, dimensions={3}, use_global_device_ids=true | all-gather | bytes 884736 | tf_op jit(solution)/shard_map/all_gather | solution.py:254
  152.4 0.9 slice.100
  153.4 2.1 broadcast_in_dim.36
  155.4 8.0 %all-to-all-start.3 = ((bf16[16,4,2,8,1536]{4,3,1,2,0:T(8,128)(2,1)}), bf16[16,4,2,8,1536]{4,3,1,2,0:T(8,128)(2,1)}, u32[]{:S(2)}, u32[]{:S(2)}) async-start(bf16[16,4,2,8,1536]{4,3,1,2,0:T(8,128)(2,1)} %broadcast_in_dim.36), calls=%async_computation.3 | async-start | bytes 6291456 | tf_op jit(solution)/shard_map/all_to_all | solution.py:84
  163.9 0.7 reshape.276
  165.1 1.0 multiply_reduce_fusion.1
  166.1 1.6 multiply_convert_fusion.1
  167.7 2.2 convert_element_type.95
  170.9 2.3 all_gather.28
  173.6 38.1 %all-to-all-done.3 = bf16[16,4,2,8,1536]{4,3,1,2,0:T(8,128)(2,1)} async-done(((bf16[16,4,2,8,1536]{4,3,1,2,0:T(8,128)(2,1)}), bf16[16,4,2,8,1536]{4,3,1,2,0:T(8,128)(2,1)}, u32[]{:S(2)}, u32[]{:S(2)}) %all-to-all-start.3) | async-done | bytes 3145760 | tf_op jit(solution)/shard_map/all_to_all | solution.py:84
  211.7 2.2 copy.133
  216.2 1.9 convolution_convert_fusion.1
  218.0 3.1 %all-gather.1 = bf16[288,1024]{1,0:T(8,128)(2,1)S(1)} all-gather(bf16[144,1024]{1,0:T(8,128)(2,1)S(1)} %convolution_convert_fusion.1), channel_id=3, replica_groups=mesh['za'=2,'zq'=4,'x'=4,'y'=4,'zh'=2,'core'=2] {'core'}, dimensions={0}, use_global_device_ids=true | all-gather | bytes 884736 | tf_op jit(solution)/shard_map/all_gather | solution.py:276
  223.2 2.5 %all-reduce.1 = (f32[144,4]{0,1:T(4,128)S(1)}, f32[144,4]{0,1:T(4,128)S(1)}) all-reduce(f32[144,4]{0,1:T(4,128)S(1)} %copy.140, f32[144,4]{0,1:T(4,128)S(1)} %copy.138), channel_id=1, replica_groups=mesh['za'=2,'zq'=4,'x'=4,'y'=4,'zh'=2,'core'=2] {'core'}, use_global_device_ids=true, to_apply=%region_11.12 | all-reduce | flops 1152 | bytes 9216 | tf_op jit(solution)/shard_map/psum | solution.py:281
  226.4 0.8 multiply_bitcast_fusion
  227.8 0.8 add_convert_fusion
  (109 shorter events, 15.3 us)
Async XLA Ops:
  6.5 26.2 %copy-start = (bf16[2,12,24,512]{3,2,1,0:T(8,128)(2,1)S(1)}, bf16[2,12,24,512]{3,2,1,0:T(8,128)(2,1)}, u32[]{:S(2)}) copy-start(bf16[2,12,24,512]{3,2,1,0:T(8,128)(2,1)} %param.11) | copy-start | bytes 1769476
  6.5 71.6 %all-gather.7.cloned.1.call-start = ((), (), s32[]{:S(2)}) async-start(), calls=%async_computation.5 | async-start | bytes 1351680 | tf_op jit(solution)/shard_map/all_gather | solution.py:194
  7.7 30.9 %collective-permute-start.1 = (bf16[2,12,6,256]{3,2,1,0:T(8,128)(2,1)S(1)}, bf16[2,12,6,256]{3,2,1,0:T(8,128)(2,1)S(1)}, u32[]{:S(2)}, u32[]{:S(2)}) collective-permute-start(bf16[2,12,6,256]{3,2,1,0:T(8,128)(2,1)S(1)} %get-tuple-element.39), channel_id=1, source_target_pairs={{0,2},{2,4},{4,6},{6,8},{8,10},{10,12},{12,14},{14,0},{1,3},{3,5},... | collective-permute-start | bytes 221192 | tf_op jit(solution)/shard_map/ppermute | solution.py:105
  13.4 25.2 %collective-permute-start.2 = (bf16[2,12,6,256]{3,2,1,0:T(8,128)(2,1)S(1)}, bf16[2,12,6,256]{3,2,1,0:T(8,128)(2,1)S(1)}, u32[]{:S(2)}, u32[]{:S(2)}) collective-permute-start(bf16[2,12,6,256]{3,2,1,0:T(8,128)(2,1)S(1)} %get-tuple-element.40), channel_id=1, source_target_pairs={{0,14},{2,0},{4,2},{6,4},{8,6},{10,8},{12,10},{14,12},{1,15},{3,1}... | collective-permute-start | bytes 221192 | tf_op jit(solution)/shard_map/ppermute | solution.py:105
  27.1 11.4 %collective-permute-start = (bf16[8,3200]{1,0:T(8,128)(2,1)S(1)}, bf16[8,3200]{1,0:T(8,128)(2,1)S(1)}, u32[]{:S(2)}, u32[]{:S(2)}) collective-permute-start(bf16[8,3200]{1,0:T(8,128)(2,1)S(1)} %pad_maximum_fusion.6), channel_id=1, source_target_pairs={{0,256},{256,0},{1,257},{257,1},{2,258},{258,2},{3,259},{259,3},{4... | collective-permute-start | bytes 153608 | tf_op jit(solution)/shard_map/ppermute | solution.py:88
  38.7 11.3 %collective-permute-start.3 = (bf16[2,3,36,256]{3,2,1,0:T(8,128)(2,1)S(1)}, bf16[2,3,36,256]{3,2,1,0:T(8,128)(2,1)S(1)}, u32[]{:S(2)}, u32[]{:S(2)}) collective-permute-start(bf16[2,3,36,256]{3,2,1,0:T(8,128)(2,1)S(1)} %get-tuple-element.41), channel_id=1, source_target_pairs={{0,16},{16,32},{32,48},{48,64},{64,80},{80,96},{96,112},{112,128},... | collective-permute-start | bytes 331784 | tf_op jit(solution)/shard_map/ppermute | solution.py:100
  41.5 16.2 %collective-permute-start.4 = (bf16[2,3,36,256]{3,2,1,0:T(8,128)(2,1)S(1)}, bf16[2,3,36,256]{3,2,1,0:T(8,128)(2,1)S(1)}, u32[]{:S(2)}, u32[]{:S(2)}) collective-permute-start(bf16[2,3,36,256]{3,2,1,0:T(8,128)(2,1)S(1)} %get-tuple-element.42), channel_id=1, source_target_pairs={{0,496},{16,0},{32,16},{48,32},{64,48},{80,64},{96,80},{112,96},{1... | collective-permute-start | bytes 331784 | tf_op jit(solution)/shard_map/ppermute | solution.py:100
  44.8 35.2 %all-to-all-start = ((bf16[4,2,8,3200]{3,2,1,0:T(8,128)(2,1)}), bf16[4,2,8,3200]{3,2,1,0:T(8,128)(2,1)}, u32[]{:S(2)}, u32[]{:S(2)}) async-start(bf16[4,2,8,3200]{3,2,1,0:T(8,128)(2,1)} %broadcast_in_dim.28), calls=%async_computation | async-start | bytes 819200 | tf_op jit(solution)/shard_map/all_to_all | solution.py:84
  61.6 0.7 copy-start.4
  62.3 0.7 copy-start.6
  63.4 2.1 copy-start.1
  63.4 2.1 copy-start.5
  63.4 2.1 copy-start.7
  65.5 8.8 %copy-start.12 = (f32[512]{0:T(512)S(1)}, f32[512]{0:T(512)}, u32[]{:S(2)}) copy-start(f32[512]{0:T(512)} %param.12) | copy-start | bytes 6148
  111.1 8.6 %copy-start.10 = (f32[2048]{0:T(1024)S(1)}, f32[2048]{0:T(1024)}, u32[]{:S(2)}) copy-start(f32[2048]{0:T(1024)} %param.15) | copy-start | bytes 24580
  111.1 8.6 %copy-start.13 = (f32[512]{0:T(512)S(1)}, f32[512]{0:T(512)}, u32[]{:S(2)}) copy-start(f32[512]{0:T(512)} %param.21) | copy-start | bytes 6148
  111.1 31.8 %all-to-all-start.2 = ((bf16[16,4,2,8,1024]{4,3,1,2,0:T(8,128)(2,1)}), bf16[16,4,2,8,1024]{4,3,1,2,0:T(8,128)(2,1)}, u32[]{:S(2)}, u32[]{:S(2)}) async-start(bf16[16,4,2,8,1024]{4,3,1,2,0:T(8,128)(2,1)} %broadcast_in_dim.35), calls=%async_computation.2 | async-start | bytes 4194304 | tf_op jit(solution)/shard_map/all_to_all | solution.py:84
  118.9 97.2 %all-gather.5.cloned.1.call-start = ((), (), s32[]{:S(2)}) async-start(), calls=%async_computation.4 | async-start | bytes 3538944 | tf_op jit(solution)/shard_map/all_gather | solution.py:236
  155.4 8.0 %copy-start.2 = (bf16[2,12,24,512]{3,2,1,0:T(8,128)(2,1)S(1)}, bf16[2,12,24,512]{3,2,1,0:T(8,128)(2,1)}, u32[]{:S(2)}) copy-start(bf16[2,12,24,512]{3,2,1,0:T(8,128)(2,1)} %param.11) | copy-start | bytes 1769476
  155.4 56.3 %all-to-all-start.3 = ((bf16[16,4,2,8,1536]{4,3,1,2,0:T(8,128)(2,1)}), bf16[16,4,2,8,1536]{4,3,1,2,0:T(8,128)(2,1)}, u32[]{:S(2)}, u32[]{:S(2)}) async-start(bf16[16,4,2,8,1536]{4,3,1,2,0:T(8,128)(2,1)} %broadcast_in_dim.36), calls=%async_computation.3 | async-start | bytes 6291456 | tf_op jit(solution)/shard_map/all_to_all | solution.py:84
  163.9 1.2 copy-start.8
  165.1 4.8 %copy-start.3 = (bf16[16,4,2,8,1024]{4,3,0,1,2:T(8,128)(2,1)S(1)}, bf16[16,4,2,8,1024]{4,3,0,1,2:T(8,128)(2,1)}, u32[]{:S(2)}) copy-start(bf16[16,4,2,8,1024]{4,3,0,1,2:T(8,128)(2,1)} %copy.127) | copy-start | bytes 6291460
  173.6 40.3 %copy-start.11 = (f32[1024]{0:T(1024)S(1)}, f32[1024]{0:T(1024)}, u32[]{:S(2)}) copy-start(f32[1024]{0:T(1024)} %param.17) | copy-start | bytes 12292
  216.2 5.2 %copy-start.14 = (bf16[1024,1536]{1,0:T(8,128)(2,1)S(1)}, bf16[1024,1536]{1,0:T(8,128)(2,1)}, u32[]{:S(2)}) copy-start(bf16[1024,1536]{1,0:T(8,128)(2,1)} %all-gather.5.cloned.1.call-done) | copy-start | bytes 9437188
  225.8 2.0 copy-start.9
Sparse Core Ops, SparseCore 0:
  32.5 29.5 all-gather.6
  121.8 79.6 all-gather.4

commit v4 on v1

v4 whole, which is shorter than its diff:
```python
import jax
import jax.numpy as jnp
import numpy as np
from jax import lax
from jax.experimental import pallas as pl
from jax.experimental.pallas import tpu as pltpu
from jax.sharding import Mesh, PartitionSpec as P

HEAD = 64
WIN_LAT = 6
WIN_LON = 12


EPSILON = 1e-05

LEVELS, ROWS, COLS = 2, 12, 24
RIM_ROWS, RIM_COLS = WIN_LAT // 2, WIN_LON // 2
OWN = LEVELS * ROWS * COLS
SIDE = LEVELS * ROWS * RIM_COLS
ENDS = LEVELS * RIM_ROWS * (COLS + 2 * RIM_COLS)
RIMS = 2 * SIDE + 2 * ENDS
WINDOW = LEVELS * WIN_LAT * WIN_LON
COARSE = OWN // 4


def wide_places():
    wide = np.zeros((LEVELS, ROWS + 2 * RIM_ROWS, COLS + 2 * RIM_COLS), np.int32)
    rows, cols = slice(RIM_ROWS, RIM_ROWS + ROWS), slice(RIM_COLS, RIM_COLS + COLS)
    start = 0
    for part in (
        wide[:, rows, cols],
        wide[:, rows, :RIM_COLS],
        wide[:, rows, RIM_COLS + COLS :],
        wide[:, :RIM_ROWS],
        wide[:, RIM_ROWS + ROWS :],
    ):
        part[...] = start + np.arange(part.size).reshape(part.shape)
        start += part.size
    return wide


WIDE = wide_places()
OWN_ROWS = slice(RIM_ROWS, RIM_ROWS + ROWS)
FIRST_COLS = WIDE[:, OWN_ROWS, RIM_COLS : 2 * RIM_COLS].reshape(-1, 1)
LAST_COLS = WIDE[:, OWN_ROWS, COLS : COLS + RIM_COLS].reshape(-1, 1)
FIRST_ROWS = WIDE[:, RIM_ROWS : 2 * RIM_ROWS].reshape(-1, 1)
LAST_ROWS = WIDE[:, ROWS : ROWS + RIM_ROWS].reshape(-1, 1)
WINDOWS = (
    WIDE.reshape(LEVELS, 3, WIN_LAT, 3, WIN_LON).transpose(1, 3, 0, 2, 4).reshape(9, WINDOW)
)
QUARTETS = (
    np.arange(OWN, dtype=np.int32)
    .reshape(LEVELS, ROWS // 2, 2, COLS // 2, 2)
    .transpose(2, 4, 0, 1, 3)
    .reshape(4, COARSE)
)


def layer_norm(values, gain_row):
    average = jnp.mean(values, axis=-1, keepdims=True)
    centred = values - average
    spread = jnp.mean(centred * centred, axis=-1, keepdims=True)
    return centred * lax.rsqrt(spread + EPSILON) * gain_row


def seam_labels(global_rows, lat_total, rim_rows):
    return jnp.where(
        global_rows >= lat_total - rim_rows, 1, jnp.where(global_rows < rim_rows, 2, 0)
    ).astype(jnp.int32)


def project_with(left_side, fragment):
    return jnp.dot(left_side, fragment, preferred_element_type=jnp.float32)


def project_with_transposed(left_side, fragment):
    return lax.dot_general(
        left_side, fragment, (((1,), (1,)), ((), ())), preferred_element_type=jnp.float32
    )


def picked(column, count):
    places = lax.broadcasted_iota(jnp.int32, (column.shape[0], count), 1)
    return (places == column).astype(jnp.bfloat16)


def spread_out(row, count):
    places = lax.broadcasted_iota(jnp.int32, (count, row.shape[1]), 0)
    return (places == row).astype(jnp.bfloat16)


def pair_mix(query, keys, values, lower, bias):
    mixed = []
    for keep in (lower, ~lower):
        kept = query * jnp.where(keep, HEAD**-0.5, 0.0).astype(jnp.bfloat16)
        scores = project_with_transposed(kept, keys)
        if bias is not None:
            scores = scores + bias
        weights = jnp.exp(scores - jnp.max(scores, axis=-1, keepdims=True))
        total = jnp.sum(weights, axis=-1, keepdims=True)
        mixed.append(project_with(weights.astype(jnp.bfloat16), values) / total)
    return jnp.where(lower, *mixed)


def call(kernel, out_shape, operands, scalars=0, limit=24, flops=10**8, **options):
    whole = pl.BlockSpec(memory_space=pltpu.VMEM)
    options.setdefault(
        "in_specs",
        [pl.BlockSpec(memory_space=pltpu.SMEM)] * scalars + [whole] * (len(operands) - scalars),
    )
    options.setdefault("out_specs", jax.tree.map(lambda _: whole, out_shape))
    return pl.pallas_call(
        kernel,
        out_shape=out_shape,
        compiler_params=pltpu.CompilerParams(vmem_limit_bytes=limit * 2**20),
        cost_estimate=pl.CostEstimate(flops=flops, bytes_accessed=2**20, transcendentals=0),
        **options,
    )(*operands)


def shape(*sizes, dtype=jnp.bfloat16):
    return jax.ShapeDtypeStruct(sizes, dtype)


def pack_kernel(place, fine_qkv, fine_proj, merge, coarse_qkv, coarse_proj, split, early, late):
    y = place[0]
    wide = jnp.concatenate(
        [fine_qkv[:, part, :].astype(jnp.float32) for part in range(3)]
        + [fine_proj[...].astype(jnp.float32)],
        axis=1,
    )
    half = jnp.where(y >= 2, wide[8:], wide[:8])
    odd = (y == 1) | (y == 3)
    early[:, :640] = jnp.where(odd, half[:, 640:], half[:, :640]).astype(jnp.bfloat16)
    rows = merge[pl.ds(pl.multiple_of(y * 16, 16), 16), :].astype(jnp.float32)
    early[:, 640:1152] = rows[:8].astype(jnp.bfloat16)
    early[:, 1152:1664] = rows[8:].astype(jnp.bfloat16)
    for part in range(3):
        cols = coarse_qkv[:, part, pl.ds(pl.multiple_of(y * 128, 128), 128)].astype(jnp.float32)
        for block in range(4):
            start = 1664 + 384 * block + 128 * part
            early[:, start : start + 128] = cols[8 * block : 8 * block + 8].astype(jnp.bfloat16)
    late[...] = jnp.zeros_like(late)
    for part in range(4):
        late[:32, 256 * part : 256 * (part + 1)] = split[:, part, :]
    late[:32, 1024:] = coarse_proj[...]


def norm_kernel(core, tokens, gain, first_place, last_place, normed, first, last):
    values = layer_norm(tokens[...].astype(jnp.float32), gain[...]).astype(jnp.bfloat16)
    normed[...] = values
    half = jnp.where(core[0] == 0, values[:, :256], values[:, 256:])
    first[...] = project_with(picked(first_place[...], OWN), half).astype(jnp.bfloat16)
    last[...] = project_with(picked(last_place[...], OWN), half).astype(jnp.bfloat16)


def ends_kernel(core, normed, west, east, first_place, last_place, first, last):
    half = jnp.where(core[0] == 0, normed[:, :256], normed[:, 256:])
    for place, out in ((first_place, first), (last_place, last)):
        pick = picked(place[...], OWN + 2 * SIDE)
        rows = project_with(pick[:, :OWN], half)
        rows += project_with(pick[:, OWN : OWN + SIDE], west[...])
        rows += project_with(pick[:, OWN + SIDE :], east[...])
        out[...] = rows.astype(jnp.bfloat16)


def fine_kernel(normed, rims, left_weight, right_weight, bias, column, row, out, total):
    window = pl.program_id(0)
    pick = picked(column[0], OWN + RIMS)
    tokens = project_with(pick[:, :OWN], normed[...]) + project_with(pick[:, OWN:], rims[...])
    tokens = tokens.astype(jnp.bfloat16)
    left = project_with(tokens, left_weight[...]).astype(jnp.bfloat16)
    right = project_with(tokens, right_weight[:, :128]).astype(jnp.bfloat16)
    lower = lax.broadcasted_iota(jnp.int32, (1, 2 * HEAD), 1) < HEAD
    values = (left[:, 512:640], right)
    mixed = [
        pair_mix(
            left[:, 128 * pair : 128 * (pair + 1)],
            left[:, 256 + 128 * pair : 256 + 128 * (pair + 1)],
            values[pair],
            lower,
            bias[0],
        ).astype(jnp.bfloat16)
        for pair in range(2)
    ]

    @pl.when(window == 0)
    def _():
        total[...] = jnp.zeros_like(total)

    total[...] += project_with(spread_out(row[0], OWN), jnp.concatenate(mixed, axis=1))

    @pl.when(window == 8)
    def _():
        out[...] = total[...].astype(jnp.bfloat16)


def merge_kernel(heads, weight, tokens, gain, places, residual, merged):
    attended = project_with_transposed(heads[...], weight[:, 128:])
    values = (tokens[...].astype(jnp.float32) + attended).astype(jnp.bfloat16)
    residual[...] = values
    quartet = jnp.concatenate(
        [project_with(picked(places[part], OWN), values) for part in range(4)], axis=1
    )
    merged[...] = layer_norm(quartet, gain[...]).astype(jnp.bfloat16)


def coarse_kernel(order, coarse, gain, row_order, first, second, third, fourth, out):
    normed = layer_norm(coarse[...].astype(jnp.float32), gain[...]).astype(jnp.bfloat16)
    normed = project_with(normed, row_order[...]).astype(jnp.bfloat16)
    lower = lax.broadcasted_iota(jnp.int32, (1, 2 * HEAD), 1) < HEAD
    for place, piece in enumerate((first, second, third, fourth)):
        packed = jnp.zeros((normed.shape[0], 384), jnp.float32)
        for part in range(4):
            packed += project_with(
                normed[:, 256 * part : 256 * (part + 1)], piece[:, 384 * part : 384 * (part + 1)]
            )
        packed = packed.astype(jnp.bfloat16)
        mixed = pair_mix(packed[:, :128], packed[:, 128:256], packed[:, 256:], lower, None)
        out[order[place]] = mixed.astype(jnp.bfloat16)


def final_kernel(core, expanded, first_sum, second_sum, gain, residual, places, out):
    half = jnp.where(core[0] == 0, residual[:, :256], residual[:, 256:]).astype(jnp.float32)
    own_gain = jnp.where(core[0] == 0, gain[:, :256], gain[:, 256:])
    total = half
    for part in range(4):
        average = first_sum[:, part : part + 1] / 512
        spread = second_sum[:, part : part + 1] / 512 - average * average
        values = expanded[:, 256 * part : 256 * (part + 1)] - average
        values = values * lax.rsqrt(spread + EPSILON) * own_gain
        high = values.astype(jnp.bfloat16)
        low = (values - high.astype(jnp.float32)).astype(jnp.bfloat16)
        back = spread_out(places[part], OWN)
        total = total + (project_with(back, high) + project_with(back, low))
    out[...] = total.astype(jnp.bfloat16)


def sent_to_all(block, axes):
    peers = lax.axis_size(axes)
    copies = jnp.broadcast_to(block[None], (peers,) + block.shape)
    return lax.all_to_all(copies, axes, split_axis=0, concat_axis=0, tiled=True)


def over_depth(block):
    other = lax.ppermute(block, "za", [(0, 1), (1, 0)])
    upper = lax.axis_index("za") == 1
    pair = jnp.stack([jnp.where(upper, other, block), jnp.where(upper, block, other)])
    return sent_to_all(pair, "zq")


def from_others(block, axis):
    return [block] + [
        lax.ppermute(block, axis, [((i + by) % 4, i) for i in range(4)]) for by in (1, 2, 3)
    ]


def lat_shift(value, by):
    perm = [(i, (i + by) % 32) for i in range(32)]
    return lax.ppermute(value, ("za", "zq", "x"), perm)


def lon_shift(value, by):
    perm = [(i, (i + by) % 8) for i in range(8)]
    return lax.ppermute(value, ("y", "zh"), perm)


def body(
    fine_tokens,
    attn_gain,
    fine_qkv,
    fine_proj,
    merge_gain,
    merge_weight,
    coarse_gain,
    coarse_qkv,
    coarse_proj,
    split_weight,
    split_gain,
):
    lat_total = ROWS * 32
    row_first = lax.axis_index(("za", "zq", "x")) * ROWS
    core = lax.axis_index("core").astype(jnp.int32)[None]
    x_place, y_place = lax.axis_index("x"), lax.axis_index("y")
    flat_tokens = fine_tokens.reshape(OWN, 512)

    early, late_shard = call(
        pack_kernel,
        (shape(8, 3200), shape(88, 1536)),
        (
            y_place.astype(jnp.int32)[None],
            fine_qkv,
            fine_proj.T,
            merge_weight,
            coarse_qkv,
            coarse_proj.T,
            split_weight,
        ),
        scalars=1,
    )
    late = lax.all_gather(late_shard, "x", axis=0, tiled=False)
    late = late[:, :32].reshape(128, 1536)

    normed, first_cols, last_cols = call(
        norm_kernel,
        (shape(OWN, 512), shape(SIDE, 256), shape(SIDE, 256)),
        (core, flat_tokens, attn_gain[None], FIRST_COLS, LAST_COLS),
        scalars=1,
    )
    east = lon_shift(first_cols, -1)
    west = lon_shift(last_cols, 1)
    early, east, west = lax.optimization_barrier((early, east, west))
    first_rows, last_rows = call(
        ends_kernel,
        (shape(ENDS, 256), shape(ENDS, 256)),
        (core, normed, west, east, FIRST_ROWS, LAST_ROWS),
        scalars=1,
    )
    below = lat_shift(first_rows, -1)
    above = lat_shift(last_rows, 1)
    depth = over_depth(early)
    depth, above, below, late = lax.optimization_barrier((depth, above, below, late))
    late = lax.all_gather(late, ("za", "zq"), axis=0, tiled=True)

    rims = jnp.concatenate([west, east, above, below], axis=0)
    rims = lax.all_gather(rims, "core", axis=1, tiled=True)
    global_rows = row_first - RIM_ROWS + jnp.arange(ROWS + 2 * RIM_ROWS, dtype=jnp.int32)
    labels = seam_labels((global_rows + lat_total) % lat_total, lat_total, RIM_ROWS)
    labels = labels.reshape(3, 1, WIN_LAT, 1)
    labels = jnp.broadcast_to(labels, (3, LEVELS, WIN_LAT, WIN_LON)).reshape(3, WINDOW)
    bias = jnp.where(labels[:, :, None] == labels[:, None, :], 0.0, -1e30).astype(jnp.float32)

    merge_side = sent_to_all(depth[..., :1664], "y")
    qkv_quad = jnp.stack(from_others(depth[..., 1664:], "x")).reshape(256, 1536)
    merge_side, qkv_quad = lax.optimization_barrier((merge_side, qkv_quad))
    qkv_pieces = from_others(qkv_quad, "y")
    first_all = sent_to_all(merge_side[..., :640], "x")
    merge_side, first_all = lax.optimization_barrier((merge_side, first_all))
    merge_all = sent_to_all(merge_side[..., 640:], "x")
    first_all = first_all.reshape(4, 2, 2, 4, 2, 8, 640)
    left_weight, right_weight = (
        first_all[:, :, part].transpose(3, 2, 0, 1, 4, 5).reshape(512, 640) for part in range(2)
    )

    constant = lambda i: (0, 0)
    window_out = call(
        fine_kernel,
        shape(OWN, 256),
        (normed, rims, left_weight, right_weight, bias, WINDOWS[:, :, None], WINDOWS[:, None, :]),
        grid=(9,),
        in_specs=[
            pl.BlockSpec((OWN, 512), constant),
            pl.BlockSpec((RIMS, 512), constant),
            pl.BlockSpec((512, 640), constant),
            pl.BlockSpec((512, 640), constant),
            pl.BlockSpec((1, WINDOW, WINDOW), lambda i: (i // 3, 0, 0)),
            pl.BlockSpec((1, WINDOW, 1), lambda i: (i, 0, 0)),
            pl.BlockSpec((1, 1, WINDOW), lambda i: (i, 0, 0)),
        ],
        out_specs=pl.BlockSpec((OWN, 256), constant),
        scratch_shapes=[pltpu.VMEM((OWN, 256), jnp.float32)],
    )
    all_heads = lax.all_gather(window_out, "core", axis=1, tiled=True)
    residual, merged_in = call(
        merge_kernel,
        (shape(OWN, 512), shape(COARSE, 2048)),
        (all_heads, right_weight, flat_tokens, merge_gain[None], QUARTETS[:, :, None]),
    )
    merge_all, qkv_pieces = lax.optimization_barrier((merge_all, qkv_pieces))
    merge_all = merge_all.reshape(4, 4, 4, 2, 8, 1024)
    merge_all = jnp.stack([merge_all[..., :512], merge_all[..., 512:]], axis=4)
    merge_all = merge_all.transpose(3, 2, 0, 1, 4, 5, 6).reshape(2048, 512)
    coarse_half = project_with(merged_in, merge_all).astype(jnp.bfloat16)
    coarse_full = lax.all_gather(coarse_half, "core", axis=1, tiled=True)

    place = jnp.arange(1024, dtype=jnp.int32)
    feature = place // 8 % 2 * 512 + place // 16 % 4 * 128 + (place // 64 + x_place) % 4 * 32
    feature = feature + place // 256 * 8 + place % 8
    row_order = (place[:, None] == feature[None, :]).astype(jnp.bfloat16)
    qkv_pieces, late = lax.optimization_barrier((qkv_pieces, late))
    order = (y_place + jnp.arange(4, dtype=jnp.int32)) % 4
    coarse_mixed = call(
        coarse_kernel,
        shape(4, COARSE, 128),
        (order, coarse_full, coarse_gain[None], row_order, *qkv_pieces),
        scalars=1,
    )
    coarse_mixed = coarse_mixed.transpose(1, 0, 2).reshape(COARSE, 512)
    partial_value = project_with_transposed(coarse_mixed, late[:, 1024:]).astype(jnp.bfloat16)
    both = lax.all_gather(partial_value, "core", axis=0, tiled=False).astype(jnp.float32)
    coarse_out = (coarse_full.astype(jnp.float32) + (both[0] + both[1])).astype(jnp.bfloat16)
    expanded = project_with(coarse_out, late[:, :1024])
    parts = expanded.reshape(COARSE, 4, 256)
    first_sum, second_sum = lax.psum(
        (jnp.sum(parts, axis=-1), jnp.sum(parts * parts, axis=-1)), "core"
    )
    restored = call(
        final_kernel,
        shape(OWN, 256),
        (
            core,
            expanded,
            first_sum,
            second_sum,
            split_gain[None],
            residual,
            QUARTETS[:, None, :],
        ),
        scalars=1,
    )
    return restored.reshape(LEVELS, ROWS, COLS, 256)


def solution(mesh):
    finer = Mesh(
        mesh.devices.reshape(2, 4, 4, 4, 2, 2), ("za", "zq", "x", "y", "zh", "core")
    )
    lat, lon, tp = ("za", "zq", "x"), ("y", "zh"), "core"
    in_specs = (
        P(None, lat, lon, None),
        P(),
        P(lat, None, tp),
        P(None, lat),
        P(),
        P(lat, tp),
        P(),
        P(lat, None, tp),
        P(tp, lat),
        P(lat, None, tp),
        P(),
    )
    out_specs = P(None, lat, lon, tp)
    return jax.shard_map(body, mesh=finer, in_specs=in_specs, out_specs=out_specs, check_vma=False)
```

time: 225 us -> 207 us (0.920)
  the two profiles are of different devices: /device:TPU:57 before, /device:TPU:1 now
where the time goes in v4:
time: 207 us; the launch traced here: 204 us
  starting transfers between devices  73.6 us (36%)
  waiting for transfers between devices  43.6 us (21%)
  local copies, waits for them, and re-layouts  27.4 us (13%)
  blocking collectives  20.9 us (10%)
  Pallas kernels  20.8 us (10%)
  between operations  13.9 us (7%)
  other arithmetic  2.88 us (1%)
    pallas_call x7, Pallas kernels, call(): pl.pallas_call(kernel, out_shape=out_shape, compiler_params=pltpu.Compile...  20.8 us
    ppermute x2, starting transfers between devices, lon_shift(): return lax.ppermute(value, ('y', 'zh'), perm)  20.6 us
    all_to_all x4, starting transfers between devices, sent_to_all(): return lax.all_to_all(copies, axes, split_axis=0, concat_axis=0, tiled=True)  19.1 us
    unnamed x66, local copies, waits for them, and re-layouts  16.9 us
    all_to_all x4, waiting for transfers between devices, sent_to_all(): return lax.all_to_all(copies, axes, split_axis=0, concat_axis=0, tiled=True)  16.6 us
    ppermute x6, starting transfers between devices, from_others(): lax.ppermute(block, axis, [((i + by) % 4, i) for i in range(4)])  16.5 us
    ppermute x2, starting transfers between devices, lat_shift(): return lax.ppermute(value, ('za', 'zq', 'x'), perm)  14 us
    ppermute x6, waiting for transfers between devices, from_others(): lax.ppermute(block, axis, [((i + by) % 4, i) for i in range(4)])  9.48 us
  transfers between devices with their start and end apart: 17, of which 7 were waited for; matrix products, arithmetic and copies ran while one was open for 7% of the time, Pallas kernels for 8%

profile of v4, /device:TPU:1, one launch (start us, length us, event | category | flops | bytes accessed | tf_op | source)
XLA Modules:
  0.0 204.5 jit_solution(15374692173675658311)
XLA Ops:
  6.5 1.1 copy-done
  7.6 0.9 copy-done.15
  8.5 0.9 copy-done.16
  10.7 18.7 %collective-permute-start = (bf16[144,256]{1,0:T(8,128)(2,1)S(1)}, bf16[144,256]{1,0:T(8,128)(2,1)S(1)}, u32[]{:S(2)}, u32[]{:S(2)}) collective-permute-start(bf16[144,256]{1,0:T(8,128)(2,1)S(1)} %get-tuple-element.37), channel_id=1, source_target_pairs={{0,14},{2,0},{4,2},{6,4},{8,6},{10,8},{12,10},{14,12},{1,15},{3,1}... | collective-permute-start | bytes 221192 | tf_op jit(solution)/shard_map/ppermute | solution.py:265
  29.5 1.9 collective-permute-start.1
  31.4 1.0 copy.30.coarse_qkv
  37.1 9.0 %collective-permute-done.1.west = bf16[144,256]{1,0:T(8,128)(2,1)S(1)} collective-permute-done((bf16[144,256]{1,0:T(8,128)(2,1)S(1)}, bf16[144,256]{1,0:T(8,128)(2,1)S(1)}, u32[]{:S(2)}, u32[]{:S(2)}) %collective-permute-start.1) | collective-permute-done | bytes 73760 | tf_op jit(solution)/shard_map/ppermute | solution.py:265
  46.1 3.3 %collective-permute-start.2 = (bf16[8,3200]{1,0:T(8,128)(2,1)S(1)}, bf16[8,3200]{1,0:T(8,128)(2,1)S(1)}, u32[]{:S(2)}, u32[]{:S(2)}) collective-permute-start(bf16[8,3200]{1,0:T(8,128)(2,1)S(1)} %get-tuple-element.41), channel_id=1, source_target_pairs={{0,256},{256,0},{1,257},{257,1},{2,258},{258,2},{3,259},{259,3},{4... | collective-permute-start | bytes 153608 | tf_op jit(solution)/shard_map/ppermute | solution.py:246
  49.4 5.7 %collective-permute-done.2 = bf16[8,3200]{1,0:T(8,128)(2,1)S(1)} collective-permute-done((bf16[8,3200]{1,0:T(8,128)(2,1)S(1)}, bf16[8,3200]{1,0:T(8,128)(2,1)S(1)}, u32[]{:S(2)}, u32[]{:S(2)}) %collective-permute-start.2) | collective-permute-done | bytes 51232 | tf_op jit(solution)/shard_map/ppermute | solution.py:246
  56.0 6.5 %all-to-all-start = ((bf16[4,2,8,3200]{3,2,1,0:T(8,128)(2,1)}), bf16[4,2,8,3200]{3,2,1,0:T(8,128)(2,1)S(1)}, u32[]{:S(2)}, u32[]{:S(2)}) async-start(bf16[4,2,8,3200]{3,2,1,0:T(8,128)(2,1)} %broadcast_in_dim.70), calls=%async_computation | async-start | bytes 819200 | tf_op jit(solution)/shard_map/all_to_all | solution.py:242
  63.2 3.1 %collective-permute-start.3 = (bf16[216,256]{1,0:T(8,128)(2,1)S(1)}, bf16[216,256]{1,0:T(8,128)(2,1)}, u32[]{:S(2)}, u32[]{:S(2)}) collective-permute-start(bf16[216,256]{1,0:T(8,128)(2,1)S(1)} %get-tuple-element.42), channel_id=1, source_target_pairs={{0,16},{16,32},{32,48},{48,64},{64,80},{80,96},{96,112},{112,128},... | collective-permute-start | bytes 331784 | tf_op jit(solution)/shard_map/ppermute | solution.py:260
  66.3 10.9 %collective-permute-start.4 = (bf16[216,256]{1,0:T(8,128)(2,1)S(1)}, bf16[216,256]{1,0:T(8,128)(2,1)S(1)}, u32[]{:S(2)}, u32[]{:S(2)}) collective-permute-start(bf16[216,256]{1,0:T(8,128)(2,1)S(1)} %get-tuple-element.43), channel_id=1, source_target_pairs={{0,496},{16,0},{32,16},{48,32},{64,48},{80,64},{96,80},{112,96},{1... | collective-permute-start | bytes 331784 | tf_op jit(solution)/shard_map/ppermute | solution.py:260
  77.2 2.9 %all-gather.7.cloned.1.call-done = bf16[352,1536]{1,0:T(8,128)(2,1)} async-done(((bf16[88,1536]{1,0:T(8,128)(2,1)}), bf16[352,1536]{1,0:T(8,128)(2,1)}) %all-gather.7.cloned.1.call-update) | async-done | bytes 1081360 | tf_op jit(solution)/shard_map/all_gather | solution.py:301
  80.0 1.8 slice.54
  82.5 1.0 broadcast_in_dim.71
  83.5 4.6 %all-to-all-start.1 = ((bf16[4,4,2,8,1664]{4,3,2,1,0:T(8,128)(2,1)}), bf16[4,4,2,8,1664]{4,3,2,1,0:T(8,128)(2,1)S(1)}, u32[]{:S(2)}, u32[]{:S(2)}) async-start(bf16[4,4,2,8,1664]{4,3,2,1,0:T(8,128)(2,1)} %broadcast_in_dim.71), calls=%async_computation.1 | async-start | bytes 1703936 | tf_op jit(solution)/shard_map/all_to_all | solution.py:242
  88.1 2.2 %collective-permute-start.5 = (bf16[4,2,8,1536]{3,2,1,0:T(8,128)(2,1)S(1)}, bf16[4,2,8,1536]{3,2,1,0:T(8,128)(2,1)S(1)}, u32[]{:S(2)}, u32[]{:S(2)}) collective-permute-start(bf16[4,2,8,1536]{3,2,1,0:T(8,128)(2,1)S(1)} %get-tuple-element.74), channel_id=1, source_target_pairs={{16,0},{32,16},{48,32},{0,48},{17,1},{33,17},{49,33},{1,49},{18,2}... | collective-permute-start | bytes 589832 | tf_op jit(solution)/shard_map/ppermute | solution.py:254
  90.3 2.6 %collective-permute-start.6 = (bf16[4,2,8,1536]{3,2,1,0:T(8,128)(2,1)S(1)}, bf16[4,2,8,1536]{3,2,1,0:T(8,128)(2,1)S(1)}, u32[]{:S(2)}, u32[]{:S(2)}) collective-permute-start(bf16[4,2,8,1536]{3,2,1,0:T(8,128)(2,1)S(1)} %get-tuple-element.74), channel_id=1, source_target_pairs={{32,0},{48,16},{0,32},{16,48},{33,1},{49,17},{1,33},{17,49},{34,2}... | collective-permute-start | bytes 589832 | tf_op jit(solution)/shard_map/ppermute | solution.py:254
  92.9 2.4 %collective-permute-start.7 = (bf16[4,2,8,1536]{3,2,1,0:T(8,128)(2,1)S(1)}, bf16[4,2,8,1536]{3,2,1,0:T(8,128)(2,1)S(1)}, u32[]{:S(2)}, u32[]{:S(2)}) collective-permute-start(bf16[4,2,8,1536]{3,2,1,0:T(8,128)(2,1)S(1)} %get-tuple-element.74), channel_id=1, source_target_pairs={{48,0},{0,16},{16,32},{32,48},{49,1},{1,17},{17,33},{33,49},{50,2}... | collective-permute-start | bytes 589832 | tf_op jit(solution)/shard_map/ppermute | solution.py:254
  95.3 2.9 %collective-permute-done.6 = bf16[4,2,8,1536]{3,2,1,0:T(8,128)(2,1)S(1)} collective-permute-done((bf16[4,2,8,1536]{3,2,1,0:T(8,128)(2,1)S(1)}, bf16[4,2,8,1536]{3,2,1,0:T(8,128)(2,1)S(1)}, u32[]{:S(2)}, u32[]{:S(2)}) %collective-permute-start.6) | collective-permute-done | bytes 196640 | tf_op jit(solution)/shard_map/ppermute | solution.py:254
  98.2 6.0 %collective-permute-done.7 = bf16[4,2,8,1536]{3,2,1,0:T(8,128)(2,1)S(1)} collective-permute-done((bf16[4,2,8,1536]{3,2,1,0:T(8,128)(2,1)S(1)}, bf16[4,2,8,1536]{3,2,1,0:T(8,128)(2,1)S(1)}, u32[]{:S(2)}, u32[]{:S(2)}) %collective-permute-start.7) | collective-permute-done | bytes 196640 | tf_op jit(solution)/shard_map/ppermute | solution.py:254
  104.4 1.3 broadcast_in_dim.72
  105.7 3.5 %all-to-all-start.2 = ((bf16[4,4,4,2,8,640]{5,4,3,2,1,0:T(8,128)(2,1)}), bf16[4,4,4,2,8,640]{5,4,3,2,1,0:T(8,128)(2,1)S(1)}, u32[]{:S(2)}, u32[]{:S(2)}) async-start(bf16[4,4,4,2,8,640]{5,4,3,2,1,0:T(8,128)(2,1)} %broadcast_in_dim.72), calls=%async_computation.2 | async-start | bytes 2621440 | tf_op jit(solution)/shard_map/all_to_all | solution.py:242
  109.2 16.6 %all-to-all-done.2 = bf16[4,4,4,2,8,640]{5,4,3,2,1,0:T(8,128)(2,1)S(1)} async-done(((bf16[4,4,4,2,8,640]{5,4,3,2,1,0:T(8,128)(2,1)}), bf16[4,4,4,2,8,640]{5,4,3,2,1,0:T(8,128)(2,1)S(1)}, u32[]{:S(2)}, u32[]{:S(2)}) %all-to-all-start.2) | async-done | bytes 1310752 | tf_op jit(solution)/shard_map/all_to_all | solution.py:242
  125.8 1.4 slice.45
  127.3 1.6 broadcast_in_dim.79
  128.9 4.4 %all-to-all-start.3 = ((bf16[4,4,4,2,8,1024]{5,4,1,2,3,0:T(8,128)(2,1)}), bf16[4,4,4,2,8,1024]{5,4,1,2,3,0:T(8,128)(2,1)}, u32[]{:S(2)}, u32[]{:S(2)}) async-start(bf16[4,4,4,2,8,1024]{5,4,1,2,3,0:T(8,128)(2,1)} %broadcast_in_dim.79), calls=%async_computation.3 | async-start | bytes 4194304 | tf_op jit(solution)/shard_map/all_to_all | solution.py:242
  133.7 0.9 fusion.row_order
  134.6 2.6 %collective-permute-start.10 = (bf16[256,1536]{1,0:T(8,128)(2,1)S(1)}, bf16[256,1536]{1,0:T(8,128)(2,1)S(1)}, u32[]{:S(2)}, u32[]{:S(2)}) collective-permute-start(bf16[256,1536]{1,0:T(8,128)(2,1)S(1)} %bitcast.52), channel_id=1, source_target_pairs={{12,0},{0,4},{4,8},{8,12},{13,1},{1,5},{5,9},{9,13},{14,2},{2,6},{... | collective-permute-start | bytes 2359304 | tf_op jit(solution)/shard_map/ppermute | solution.py:254
  137.1 3.9 %collective-permute-start.8 = (bf16[256,1536]{1,0:T(8,128)(2,1)S(1)}, bf16[256,1536]{1,0:T(8,128)(2,1)S(1)}, u32[]{:S(2)}, u32[]{:S(2)}) collective-permute-start(bf16[256,1536]{1,0:T(8,128)(2,1)S(1)} %bitcast.53), channel_id=1, source_target_pairs={{4,0},{8,4},{12,8},{0,12},{5,1},{9,5},{13,9},{1,13},{6,2},{10,6},{... | collective-permute-start | bytes 2359304 | tf_op jit(solution)/shard_map/ppermute | solution.py:254
  141.1 2.8 %collective-permute-start.9 = (bf16[256,1536]{1,0:T(8,128)(2,1)S(1)}, bf16[256,1536]{1,0:T(8,128)(2,1)S(1)}, u32[]{:S(2)}, u32[]{:S(2)}) collective-permute-start(bf16[256,1536]{1,0:T(8,128)(2,1)S(1)} %bitcast.54), channel_id=1, source_target_pairs={{8,0},{12,4},{0,8},{4,12},{9,1},{13,5},{1,9},{5,13},{10,2},{14,6},... | collective-permute-start | bytes 2359304 | tf_op jit(solution)/shard_map/ppermute | solution.py:254
  143.9 1.0 pad_maximum_fusion.2
  145.0 5.5 %all_gather.26.rims = bf16[720,512]{1,0:T(8,128)(2,1)S(1)} all-gather(bf16[720,256]{1,0:T(8,128)(2,1)S(1)} %pad_maximum_fusion.2), channel_id=1, replica_groups=mesh['za'=2,'zq'=4,'x'=4,'y'=4,'zh'=2,'core'=2] {'core'}, dimensions={1}, use_global_device_ids=true | all-gather | bytes 1105920 | tf_op jit(solution)/shard_map/all_gather | solution.py:326
  151.5 12.8 %shard_map.184 = bf16[576,256]{1,0:T(8,128)(2,1)S(1)} custom-call(bf16[576,512]{1,0:T(8,128)(2,1)S(1)} %get-tuple-element.35.normed, bf16[720,512]{1,0:T(8,128)(2,1)S(1)} %all_gather.26.rims, bf16[512,640]{1,0:T(8,128)(2,1)S(1)} %bitcast.56, bf16[512,640]{1,0:T(8,128)(2,1)S(1)} %bitcast.50, f32[3,144,144]{2,1,0:T(8,128)S(1)} %compare_select_fusion.bias, ...), custom_call_target="tpu_custom_call" | custom-call | flops 100000000 | bytes 1048576 | tf_op jit(solution)/shard_map/pallas_call | solution.py:112
  164.3 2.3 %all_gather.27.heads = bf16[576,512]{1,0:T(8,128)(2,1)S(1)} all-gather(bf16[576,256]{1,0:T(8,128)(2,1)S(1)} %shard_map.184), channel_id=1, replica_groups=mesh['za'=2,'zq'=4,'x'=4,'y'=4,'zh'=2,'core'=2] {'core'}, dimensions={1}, use_global_device_ids=true | all-gather | bytes 884736 | tf_op jit(solution)/shard_map/all_gather | solution.py:363
  166.6 1.4 shard_map.185
  168.8 0.9 copy-done.2
  169.7 1.0 copy-done.4
  171.3 0.9 copy-done.6
  172.2 1.8 slice_bitcast_fusion.1
  174.7 7.1 %all_gather.28.coarse = bf16[144,1024]{1,0:T(8,128)(2,1)S(1)} all-gather(bf16[144,512]{1,0:T(8,128)(2,1)S(1)} %convolution_convert_fusion.1), channel_id=1, replica_groups=mesh['za'=2,'zq'=4,'x'=4,'y'=4,'zh'=2,'core'=2] {'core'}, dimensions={1}, use_global_device_ids=true | all-gather | bytes 442368 | tf_op jit(solution)/shard_map/all_gather | solution.py:374
  181.7 1.1 copy-done.3
  182.9 1.1 copy-done.5
  184.0 1.1 copy-done.7
  185.1 2.8 %shard_map.186 = bf16[4,144,128]{2,1,0:T(8,128)(2,1)S(1)} custom-call(s32[4]{0:T(128)S(1)} %and_select_fusion.order, bf16[144,1024]{1,0:T(8,128)(2,1)S(1)} %all_gather.28.coarse, f32[1,1024]{1,0:T(1,128)S(1)} %bitcast.60, bf16[1024,1024]{1,0:T(8,128)(2,1)S(1)} %fusion.row_order, bf16[256,1536]{1,0:T(8,128)(2,1)S(1)} %bitcast.55, ...), custom_call_target="tpu_custom_call" | custom-call | flops 100000000 | bytes 1048576 | tf_op jit(solution)/shard_map/pallas_call | solution.py:112
  188.5 2.2 %all-gather.1 = bf16[288,1024]{1,0:T(8,128)(2,1)S(1)} all-gather(bf16[144,1024]{1,0:T(8,128)(2,1)S(1)} %convolution_convert_fusion), channel_id=3, replica_groups=mesh['za'=2,'zq'=4,'x'=4,'y'=4,'zh'=2,'core'=2] {'core'}, dimensions={0}, use_global_device_ids=true | all-gather | bytes 884736 | tf_op jit(solution)/shard_map/all_gather | solution.py:390
  192.0 3.9 %all-reduce = (f32[144,4]{1,0:T(8,128)S(1)}, f32[144,4]{1,0:T(8,128)S(1)}) all-reduce(f32[144,4]{1,0:T(8,128)S(1)} %get-tuple-element.66, f32[144,4]{1,0:T(8,128)S(1)} %get-tuple-element.65), channel_id=1, replica_groups=mesh['za'=2,'zq'=4,'x'=4,'y'=4,'zh'=2,'core'=2] {'core'}, use_global_device_ids=true, to_apply=%region_1.2 | all-reduce | flops 1152 | bytes 9216 | tf_op jit(solution)/shard_map/psum | solution.py:394
  196.0 1.7 shard_map.187
  (98 shorter events, 13.8 us)
Async XLA Ops:
  6.5 73.5 %all-gather.7.cloned.1.call-start = ((), (), s32[]{:S(2)}) async-start(), calls=%async_computation.5 | async-start | bytes 1351680 | tf_op jit(solution)/shard_map/all_gather | solution.py:301
  6.5 1.1 copy-start
  7.6 0.9 copy-start.15
  8.5 0.9 copy-start.16
  9.4 0.7 copy-start.21
  10.1 52.4 %copy-start.13 = (s32[216,1]{1,0:T(8,128)S(1)}, s32[216,1]{1,0:T(8,128)}, u32[]{:S(2)}) copy-start(s32[216,1]{1,0:T(8,128)} %constant.177.clone.first_place) | copy-start | bytes 2596
  10.1 52.4 %copy-start.14 = (s32[216,1]{1,0:T(8,128)S(1)}, s32[216,1]{1,0:T(8,128)}, u32[]{:S(2)}) copy-start(s32[216,1]{1,0:T(8,128)} %constant.178.clone.last_place) | copy-start | bytes 2596
  10.7 26.4 %collective-permute-start = (bf16[144,256]{1,0:T(8,128)(2,1)S(1)}, bf16[144,256]{1,0:T(8,128)(2,1)S(1)}, u32[]{:S(2)}, u32[]{:S(2)}) collective-permute-start(bf16[144,256]{1,0:T(8,128)(2,1)S(1)} %get-tuple-element.37), channel_id=1, source_target_pairs={{0,14},{2,0},{4,2},{6,4},{8,6},{10,8},{12,10},{14,12},{1,15},{3,1}... | collective-permute-start | bytes 221192 | tf_op jit(solution)/shard_map/ppermute | solution.py:265
  29.5 16.6 %collective-permute-start.1 = (bf16[144,256]{1,0:T(8,128)(2,1)S(1)}, bf16[144,256]{1,0:T(8,128)(2,1)S(1)}, u32[]{:S(2)}, u32[]{:S(2)}) collective-permute-start(bf16[144,256]{1,0:T(8,128)(2,1)S(1)} %get-tuple-element.38), channel_id=1, source_target_pairs={{0,2},{2,4},{4,6},{6,8},{8,10},{10,12},{12,14},{14,0},{1,3},{3,5},... | collective-permute-start | bytes 221192 | tf_op jit(solution)/shard_map/ppermute | solution.py:265
  33.1 0.8 copy-start.23
  34.0 0.8 copy-start.24
  34.8 0.8 copy-start.25
  35.6 0.7 copy-start.26
  46.1 59.6 %copy-start.11 = (bf16[144,256]{1,0:T(8,128)(2,1)}, bf16[144,256]{1,0:T(8,128)(2,1)S(1)}, u32[]{:S(2)}) copy-start(bf16[144,256]{1,0:T(8,128)(2,1)S(1)} %collective-permute-done.1.west) | copy-start | bytes 221188
  46.1 9.1 %collective-permute-start.2 = (bf16[8,3200]{1,0:T(8,128)(2,1)S(1)}, bf16[8,3200]{1,0:T(8,128)(2,1)S(1)}, u32[]{:S(2)}, u32[]{:S(2)}) collective-permute-start(bf16[8,3200]{1,0:T(8,128)(2,1)S(1)} %get-tuple-element.41), channel_id=1, source_target_pairs={{0,256},{256,0},{1,257},{257,1},{2,258},{258,2},{3,259},{259,3},{4... | collective-permute-start | bytes 153608 | tf_op jit(solution)/shard_map/ppermute | solution.py:246
  56.0 25.8 %all-to-all-start = ((bf16[4,2,8,3200]{3,2,1,0:T(8,128)(2,1)}), bf16[4,2,8,3200]{3,2,1,0:T(8,128)(2,1)S(1)}, u32[]{:S(2)}, u32[]{:S(2)}) async-start(bf16[4,2,8,3200]{3,2,1,0:T(8,128)(2,1)} %broadcast_in_dim.70), calls=%async_computation | async-start | bytes 819200 | tf_op jit(solution)/shard_map/all_to_all | solution.py:242
  62.5 119.2 %all-gather.5.cloned.1.call-start = ((), (), s32[]{:S(2)}) async-start(), calls=%async_computation.4 | async-start | bytes 3538944 | tf_op jit(solution)/shard_map/all_gather | solution.py:323
  63.2 18.6 %collective-permute-start.3 = (bf16[216,256]{1,0:T(8,128)(2,1)S(1)}, bf16[216,256]{1,0:T(8,128)(2,1)}, u32[]{:S(2)}, u32[]{:S(2)}) collective-permute-start(bf16[216,256]{1,0:T(8,128)(2,1)S(1)} %get-tuple-element.42), channel_id=1, source_target_pairs={{0,16},{16,32},{32,48},{48,64},{64,80},{80,96},{96,112},{112,128},... | collective-permute-start | bytes 331784 | tf_op jit(solution)/shard_map/ppermute | solution.py:260
  66.3 15.5 %collective-permute-start.4 = (bf16[216,256]{1,0:T(8,128)(2,1)S(1)}, bf16[216,256]{1,0:T(8,128)(2,1)S(1)}, u32[]{:S(2)}, u32[]{:S(2)}) collective-permute-start(bf16[216,256]{1,0:T(8,128)(2,1)S(1)} %get-tuple-element.43), channel_id=1, source_target_pairs={{0,496},{16,0},{32,16},{48,32},{64,48},{80,64},{96,80},{112,96},{1... | collective-permute-start | bytes 331784 | tf_op jit(solution)/shard_map/ppermute | solution.py:260
  83.5 20.9 %all-to-all-start.1 = ((bf16[4,4,2,8,1664]{4,3,2,1,0:T(8,128)(2,1)}), bf16[4,4,2,8,1664]{4,3,2,1,0:T(8,128)(2,1)S(1)}, u32[]{:S(2)}, u32[]{:S(2)}) async-start(bf16[4,4,2,8,1664]{4,3,2,1,0:T(8,128)(2,1)} %broadcast_in_dim.71), calls=%async_computation.1 | async-start | bytes 1703936 | tf_op jit(solution)/shard_map/all_to_all | solution.py:242
  88.1 7.2 %collective-permute-start.5 = (bf16[4,2,8,1536]{3,2,1,0:T(8,128)(2,1)S(1)}, bf16[4,2,8,1536]{3,2,1,0:T(8,128)(2,1)S(1)}, u32[]{:S(2)}, u32[]{:S(2)}) collective-permute-start(bf16[4,2,8,1536]{3,2,1,0:T(8,128)(2,1)S(1)} %get-tuple-element.74), channel_id=1, source_target_pairs={{16,0},{32,16},{48,32},{0,48},{17,1},{33,17},{49,33},{1,49},{18,2}... | collective-permute-start | bytes 589832 | tf_op jit(solution)/shard_map/ppermute | solution.py:254
  90.3 7.9 %collective-permute-start.6 = (bf16[4,2,8,1536]{3,2,1,0:T(8,128)(2,1)S(1)}, bf16[4,2,8,1536]{3,2,1,0:T(8,128)(2,1)S(1)}, u32[]{:S(2)}, u32[]{:S(2)}) collective-permute-start(bf16[4,2,8,1536]{3,2,1,0:T(8,128)(2,1)S(1)} %get-tuple-element.74), channel_id=1, source_target_pairs={{32,0},{48,16},{0,32},{16,48},{33,1},{49,17},{1,33},{17,49},{34,2}... | collective-permute-start | bytes 589832 | tf_op jit(solution)/shard_map/ppermute | solution.py:254
  92.9 11.3 %collective-permute-start.7 = (bf16[4,2,8,1536]{3,2,1,0:T(8,128)(2,1)S(1)}, bf16[4,2,8,1536]{3,2,1,0:T(8,128)(2,1)S(1)}, u32[]{:S(2)}, u32[]{:S(2)}) collective-permute-start(bf16[4,2,8,1536]{3,2,1,0:T(8,128)(2,1)S(1)} %get-tuple-element.74), channel_id=1, source_target_pairs={{48,0},{0,16},{16,32},{32,48},{49,1},{1,17},{17,33},{33,49},{50,2}... | collective-permute-start | bytes 589832 | tf_op jit(solution)/shard_map/ppermute | solution.py:254
  104.3 1.3 copy-start.29
  105.7 20.1 %all-to-all-start.2 = ((bf16[4,4,4,2,8,640]{5,4,3,2,1,0:T(8,128)(2,1)}), bf16[4,4,4,2,8,640]{5,4,3,2,1,0:T(8,128)(2,1)S(1)}, u32[]{:S(2)}, u32[]{:S(2)}) async-start(bf16[4,4,4,2,8,640]{5,4,3,2,1,0:T(8,128)(2,1)} %broadcast_in_dim.72), calls=%async_computation.2 | async-start | bytes 2621440 | tf_op jit(solution)/shard_map/all_to_all | solution.py:242
  125.8 3.1 %copy-start.27 = (bf16[4,4,4,2,8,640]{5,4,3,2,1,0:T(8,128)(2,1)}, bf16[4,4,4,2,8,640]{5,4,3,2,1,0:T(8,128)(2,1)S(1)}, u32[]{:S(2)}) copy-start(bf16[4,4,4,2,8,640]{5,4,3,2,1,0:T(8,128)(2,1)S(1)} %all-to-all-done.2) | copy-start | bytes 3932164
  128.9 43.3 %all-to-all-start.3 = ((bf16[4,4,4,2,8,1024]{5,4,1,2,3,0:T(8,128)(2,1)}), bf16[4,4,4,2,8,1024]{5,4,1,2,3,0:T(8,128)(2,1)}, u32[]{:S(2)}, u32[]{:S(2)}) async-start(bf16[4,4,4,2,8,1024]{5,4,1,2,3,0:T(8,128)(2,1)} %broadcast_in_dim.79), calls=%async_computation.3 | async-start | bytes 4194304 | tf_op jit(solution)/shard_map/all_to_all | solution.py:242
  133.5 16.9 %copy-start.28 = (bf16[4,4,4,2,8,640]{5,4,3,2,1,0:T(8,128)(2,1)S(1)}, bf16[4,4,4,2,8,640]{5,4,3,2,1,0:T(8,128)(2,1)}, u32[]{:S(2)}) copy-start(bf16[4,4,4,2,8,640]{5,4,3,2,1,0:T(8,128)(2,1)} %copy-done.27) | copy-start | bytes 3932164
  134.6 34.3 %collective-permute-start.10 = (bf16[256,1536]{1,0:T(8,128)(2,1)S(1)}, bf16[256,1536]{1,0:T(8,128)(2,1)S(1)}, u32[]{:S(2)}, u32[]{:S(2)}) collective-permute-start(bf16[256,1536]{1,0:T(8,128)(2,1)S(1)} %bitcast.52), channel_id=1, source_target_pairs={{12,0},{0,4},{4,8},{8,12},{13,1},{1,5},{5,9},{9,13},{14,2},{2,6},{... | collective-permute-start | bytes 2359304 | tf_op jit(solution)/shard_map/ppermute | solution.py:254
  137.1 32.6 %collective-permute-start.8 = (bf16[256,1536]{1,0:T(8,128)(2,1)S(1)}, bf16[256,1536]{1,0:T(8,128)(2,1)S(1)}, u32[]{:S(2)}, u32[]{:S(2)}) collective-permute-start(bf16[256,1536]{1,0:T(8,128)(2,1)S(1)} %bitcast.53), channel_id=1, source_target_pairs={{4,0},{8,4},{12,8},{0,12},{5,1},{9,5},{13,9},{1,13},{6,2},{10,6},{... | collective-permute-start | bytes 2359304 | tf_op jit(solution)/shard_map/ppermute | solution.py:254
  141.1 30.2 %collective-permute-start.9 = (bf16[256,1536]{1,0:T(8,128)(2,1)S(1)}, bf16[256,1536]{1,0:T(8,128)(2,1)S(1)}, u32[]{:S(2)}, u32[]{:S(2)}) collective-permute-start(bf16[256,1536]{1,0:T(8,128)(2,1)S(1)} %bitcast.54), channel_id=1, source_target_pairs={{8,0},{12,4},{0,8},{4,12},{9,1},{13,5},{1,9},{5,13},{10,2},{14,6},... | collective-permute-start | bytes 2359304 | tf_op jit(solution)/shard_map/ppermute | solution.py:254
  150.4 1.1 copy-start.8
  150.4 1.1 copy-start.17
  151.5 15.1 %copy-start.1 = (bf16[2,12,24,512]{3,2,1,0:T(8,128)(2,1)S(1)}, bf16[2,12,24,512]{3,2,1,0:T(8,128)(2,1)}, u32[]{:S(2)}) copy-start(bf16[2,12,24,512]{3,2,1,0:T(8,128)(2,1)} %param.19) | copy-start | bytes 1769476
  151.5 15.1 %copy-start.12 = (s32[4,144,1]{2,1,0:T(8,128)S(1)}, s32[4,144,1]{2,1,0:T(8,128)}, u32[]{:S(2)}) copy-start(s32[4,144,1]{2,1,0:T(8,128)} %constant.181.clone.places) | copy-start | bytes 6916
  151.5 15.1 %copy-start.18 = (f32[2048]{0:T(1024)S(1)}, f32[2048]{0:T(1024)}, u32[]{:S(2)}) copy-start(f32[2048]{0:T(1024)} %param.23) | copy-start | bytes 24580
  168.0 0.8 copy-start.9
  168.8 0.9 copy-start.2
  169.7 1.0 copy-start.4
  171.3 0.9 copy-start.6
  174.2 7.6 %copy-start.19 = (f32[1024]{0:T(1024)S(1)}, f32[1024]{0:T(1024)}, u32[]{:S(2)}) copy-start(f32[1024]{0:T(1024)} %param.25) | copy-start | bytes 12292
  181.7 1.1 copy-start.3
  182.9 1.1 copy-start.5
  184.0 1.1 copy-start.7
  185.1 2.8 %copy-start.31 = (bf16[1024,1536]{1,0:T(8,128)(2,1)S(1)}, bf16[1024,1536]{1,0:T(8,128)(2,1)}, u32[]{:S(2)}) copy-start(bf16[1024,1536]{1,0:T(8,128)(2,1)} %all-gather.5.cloned.1.call-done) | copy-start | bytes 9437188
  190.8 5.1 %copy-start.10 = (bf16[576,512]{1,0:T(8,128)(2,1)S(1)}, bf16[576,512]{1,0:T(8,128)(2,1)}, u32[]{:S(2)}) copy-start(bf16[576,512]{1,0:T(8,128)(2,1)} %copy-done.9) | copy-start | bytes 1769476
  190.8 5.1 %copy-start.20 = (s32[4,1,144]{2,1,0:T(1,128)S(1)}, s32[4,1,144]{2,1,0:T(1,128)}, u32[]{:S(2)}) copy-start(s32[4,1,144]{2,1,0:T(1,128)} %constant.182.clone.places) | copy-start | bytes 6916
  190.8 5.1 %copy-start.22 = (f32[512]{0:T(512)S(1)}, f32[512]{0:T(512)}, u32[]{:S(2)}) copy-start(f32[512]{0:T(512)} %param.29) | copy-start | bytes 6148
  (1 other events, 0.6 us)
Sparse Core Ops, SparseCore 0:
  49.6 30.4 all-gather.6
  82.6 85.0 all-gather.4

commit v5 on v4

--- a/solution.py
+++ b/solution.py
@@ -164,11 +164,15 @@
         out[...] = rows.astype(jnp.bfloat16)
 
 
-def fine_kernel(normed, rims, left_weight, right_weight, bias, column, row, out, total):
+def window_kernel(normed, rims, column, out):
+    pick = picked(column[0], OWN + RIMS)
+    rows = project_with(pick[:, :OWN], normed[...]) + project_with(pick[:, OWN:], rims[...])
+    out[0] = rows.astype(jnp.bfloat16)
+
+
+def fine_kernel(windows, left_weight, right_weight, bias, row, out, total):
     window = pl.program_id(0)
-    pick = picked(column[0], OWN + RIMS)
-    tokens = project_with(pick[:, :OWN], normed[...]) + project_with(pick[:, OWN:], rims[...])
-    tokens = tokens.astype(jnp.bfloat16)
+    tokens = windows[0]
     left = project_with(tokens, left_weight[...]).astype(jnp.bfloat16)
     right = project_with(tokens, right_weight[:, :128]).astype(jnp.bfloat16)
     lower = lax.broadcasted_iota(jnp.int32, (1, 2 * HEAD), 1) < HEAD
@@ -205,15 +209,25 @@
     merged[...] = layer_norm(quartet, gain[...]).astype(jnp.bfloat16)
 
 
-def coarse_kernel(order, coarse, gain, row_order, first, second, third, fourth, out):
+def coarse_kernel(
+    order, coarse, gain, row_order, first, second, third, fourth, out, pieces, arrived
+):
+    copies = [
+        pltpu.make_async_copy(piece, pieces.at[place], arrived.at[place])
+        for place, piece in enumerate((first, second, third, fourth))
+    ]
+    for copy in copies:
+        copy.start()
     normed = layer_norm(coarse[...].astype(jnp.float32), gain[...]).astype(jnp.bfloat16)
     normed = project_with(normed, row_order[...]).astype(jnp.bfloat16)
     lower = lax.broadcasted_iota(jnp.int32, (1, 2 * HEAD), 1) < HEAD
-    for place, piece in enumerate((first, second, third, fourth)):
+    for place, copy in enumerate(copies):
+        copy.wait()
         packed = jnp.zeros((normed.shape[0], 384), jnp.float32)
         for part in range(4):
             packed += project_with(
-                normed[:, 256 * part : 256 * (part + 1)], piece[:, 384 * part : 384 * (part + 1)]
+                normed[:, 256 * part : 256 * (part + 1)],
+                pieces[place, :, 384 * part : 384 * (part + 1)],
             )
         packed = packed.astype(jnp.bfloat16)
         mixed = pair_mix(packed[:, :128], packed[:, 128:256], packed[:, 256:], lower, None)
@@ -242,11 +256,10 @@
     return lax.all_to_all(copies, axes, split_axis=0, concat_axis=0, tiled=True)
 
 
-def over_depth(block):
+def depth_pair(block):
     other = lax.ppermute(block, "za", [(0, 1), (1, 0)])
     upper = lax.axis_index("za") == 1
-    pair = jnp.stack([jnp.where(upper, other, block), jnp.where(upper, block, other)])
-    return sent_to_all(pair, "zq")
+    return jnp.stack([jnp.where(upper, other, block), jnp.where(upper, block, other)])
 
 
 def from_others(block, axis):
@@ -298,18 +311,27 @@
         ),
         scalars=1,
     )
-    late = lax.all_gather(late_shard, "x", axis=0, tiled=False)
-    late = late[:, :32].reshape(128, 1536)
-
+    early, late_shard, first_tokens = lax.optimization_barrier((early, late_shard, flat_tokens))
     normed, first_cols, last_cols = call(
         norm_kernel,
         (shape(OWN, 512), shape(SIDE, 256), shape(SIDE, 256)),
-        (core, flat_tokens, attn_gain[None], FIRST_COLS, LAST_COLS),
+        (core, first_tokens, attn_gain[None], FIRST_COLS, LAST_COLS),
         scalars=1,
     )
+    late = lax.all_gather(late_shard, "x", axis=0, tiled=False)
+    late = late[:, :32].reshape(128, 1536)
+    depth = sent_to_all(depth_pair(early), "zq")
     east = lon_shift(first_cols, -1)
     west = lon_shift(last_cols, 1)
-    early, east, west = lax.optimization_barrier((early, east, west))
+    depth, late, east, west = lax.optimization_barrier((depth, late, east, west))
+    late = lax.all_gather(late, ("za", "zq"), axis=0, tiled=True)
+    merge_side = sent_to_all(depth[..., :1664], "y")
+    qkv_quad = jnp.stack(from_others(depth[..., 1664:], "x")).reshape(256, 1536)
+    merge_side, qkv_quad, east, west = lax.optimization_barrier(
+        (merge_side, qkv_quad, east, west)
+    )
+    qkv_pieces = from_others(qkv_quad, "y")
+    both_all = sent_to_all(merge_side, "x")
     first_rows, last_rows = call(
         ends_kernel,
         (shape(ENDS, 256), shape(ENDS, 256)),
@@ -318,26 +340,27 @@
     )
     below = lat_shift(first_rows, -1)
     above = lat_shift(last_rows, 1)
-    depth = over_depth(early)
-    depth, above, below, late = lax.optimization_barrier((depth, above, below, late))
-    late = lax.all_gather(late, ("za", "zq"), axis=0, tiled=True)
-
     rims = jnp.concatenate([west, east, above, below], axis=0)
     rims = lax.all_gather(rims, "core", axis=1, tiled=True)
+    windows = call(
+        window_kernel,
+        shape(9, WINDOW, 512),
+        (normed, rims, WINDOWS[:, :, None]),
+        grid=(9,),
+        in_specs=[
+            pl.BlockSpec((OWN, 512), lambda i: (0, 0)),
+            pl.BlockSpec((RIMS, 512), lambda i: (0, 0)),
+            pl.BlockSpec((1, WINDOW, 1), lambda i: (i, 0, 0)),
+        ],
+        out_specs=pl.BlockSpec((1, WINDOW, 512), lambda i: (i, 0, 0)),
+    )
     global_rows = row_first - RIM_ROWS + jnp.arange(ROWS + 2 * RIM_ROWS, dtype=jnp.int32)
     labels = seam_labels((global_rows + lat_total) % lat_total, lat_total, RIM_ROWS)
     labels = labels.reshape(3, 1, WIN_LAT, 1)
     labels = jnp.broadcast_to(labels, (3, LEVELS, WIN_LAT, WIN_LON)).reshape(3, WINDOW)
     bias = jnp.where(labels[:, :, None] == labels[:, None, :], 0.0, -1e30).astype(jnp.float32)
 
-    merge_side = sent_to_all(depth[..., :1664], "y")
-    qkv_quad = jnp.stack(from_others(depth[..., 1664:], "x")).reshape(256, 1536)
-    merge_side, qkv_quad = lax.optimization_barrier((merge_side, qkv_quad))
-    qkv_pieces = from_others(qkv_quad, "y")
-    first_all = sent_to_all(merge_side[..., :640], "x")
-    merge_side, first_all = lax.optimization_barrier((merge_side, first_all))
-    merge_all = sent_to_all(merge_side[..., 640:], "x")
-    first_all = first_all.reshape(4, 2, 2, 4, 2, 8, 640)
+    first_all = both_all[..., :640].reshape(4, 2, 2, 4, 2, 8, 640)
     left_weight, right_weight = (
         first_all[:, :, part].transpose(3, 2, 0, 1, 4, 5).reshape(512, 640) for part in range(2)
     )
@@ -346,15 +369,13 @@
     window_out = call(
         fine_kernel,
         shape(OWN, 256),
-        (normed, rims, left_weight, right_weight, bias, WINDOWS[:, :, None], WINDOWS[:, None, :]),
+        (windows, left_weight, right_weight, bias, WINDOWS[:, None, :]),
         grid=(9,),
         in_specs=[
-            pl.BlockSpec((OWN, 512), constant),
-            pl.BlockSpec((RIMS, 512), constant),
+            pl.BlockSpec((1, WINDOW, 512), lambda i: (i, 0, 0)),
             pl.BlockSpec((512, 640), constant),
             pl.BlockSpec((512, 640), constant),
             pl.BlockSpec((1, WINDOW, WINDOW), lambda i: (i // 3, 0, 0)),
-            pl.BlockSpec((1, WINDOW, 1), lambda i: (i, 0, 0)),
             pl.BlockSpec((1, 1, WINDOW), lambda i: (i, 0, 0)),
         ],
         out_specs=pl.BlockSpec((OWN, 256), constant),
@@ -366,9 +387,7 @@
         (shape(OWN, 512), shape(COARSE, 2048)),
         (all_heads, right_weight, flat_tokens, merge_gain[None], QUARTETS[:, :, None]),
     )
-    merge_all, qkv_pieces = lax.optimization_barrier((merge_all, qkv_pieces))
-    merge_all = merge_all.reshape(4, 4, 4, 2, 8, 1024)
-    merge_all = jnp.stack([merge_all[..., :512], merge_all[..., 512:]], axis=4)
+    merge_all = jnp.stack([both_all[..., 640:1152], both_all[..., 1152:]], axis=4)
     merge_all = merge_all.transpose(3, 2, 0, 1, 4, 5, 6).reshape(2048, 512)
     coarse_half = project_with(merged_in, merge_all).astype(jnp.bfloat16)
     coarse_full = lax.all_gather(coarse_half, "core", axis=1, tiled=True)
@@ -383,7 +402,13 @@
         coarse_kernel,
         shape(4, COARSE, 128),
         (order, coarse_full, coarse_gain[None], row_order, *qkv_pieces),
-        scalars=1,
+        in_specs=[pl.BlockSpec(memory_space=pltpu.SMEM)]
+        + [pl.BlockSpec(memory_space=pltpu.VMEM)] * 3
+        + [pl.BlockSpec(memory_space=pl.ANY)] * 4,
+        scratch_shapes=[
+            pltpu.VMEM((4, 256, 1536), jnp.bfloat16),
+            pltpu.SemaphoreType.DMA((4,)),
+        ],
     )
     coarse_mixed = coarse_mixed.transpose(1, 0, 2).reshape(COARSE, 512)
     partial_value = project_with_transposed(coarse_mixed, late[:, 1024:]).astype(jnp.bfloat16)

time: 207 us -> 184 us (0.89)
  the two profiles are of different devices: /device:TPU:1 before, /device:TPU:129 now
where the time goes in v5:
time: 184 us; the launch traced here: 183 us
  starting transfers between devices  60.3 us (33%)
  waiting for transfers between devices  50 us (27%)
  Pallas kernels  23.7 us (13%)
  local copies, waits for them, and re-layouts  15.6 us (8%)
  blocking collectives  14 us (8%)
  between operations  13.9 us (8%)
  other arithmetic  3.56 us (2%)
    pallas_call x8, Pallas kernels, call(): pl.pallas_call(kernel, out_shape=out_shape, compiler_params=pltpu.Compile...  23.7 us
    ppermute x2, waiting for transfers between devices, lat_shift(): return lax.ppermute(value, ('za', 'zq', 'x'), perm)  19.1 us
    ppermute x6, starting transfers between devices, from_others(): lax.ppermute(block, axis, [((i + by) % 4, i) for i in range(4)])  19.1 us
    all_to_all x3, starting transfers between devices, sent_to_all(): return lax.all_to_all(copies, axes, split_axis=0, concat_axis=0, tiled=True)  16.5 us
    ppermute x2, starting transfers between devices, lon_shift(): return lax.ppermute(value, ('y', 'zh'), perm)  14 us
    ppermute x2, waiting for transfers between devices, lon_shift(): return lax.ppermute(value, ('y', 'zh'), perm)  9.17 us
    ppermute x6, waiting for transfers between devices, from_others(): lax.ppermute(block, axis, [((i + by) % 4, i) for i in range(4)])  9.15 us
    ppermute x2, starting transfers between devices, lat_shift(): return lax.ppermute(value, ('za', 'zq', 'x'), perm)  8.73 us
  transfers between devices with their start and end apart: 16, of which 7 were waited for; matrix products, arithmetic and copies ran while one was open for 7% of the time, Pallas kernels for 9%

profile of v5, /device:TPU:129, one launch (start us, length us, event | category | flops | bytes accessed | tf_op | source)
XLA Modules:
  0.0 182.6 jit_solution(4672815928000540565)
XLA Ops:
  6.6 1.0 copy.23.coarse_qkv
  7.6 0.8 copy.22.fine_qkv
  8.4 0.8 copy-done.17
  9.2 0.8 copy-done.18
  10.1 0.8 copy-done.19
  10.8 0.7 copy-done.20
  11.6 0.8 shard_map.181
  12.4 1.9 %collective-permute-start = (bf16[8,3200]{1,0:T(8,128)(2,1)S(1)}, bf16[8,3200]{1,0:T(8,128)(2,1)S(1)}, u32[]{:S(2)}, u32[]{:S(2)}) collective-permute-start(bf16[8,3200]{1,0:T(8,128)(2,1)S(1)} %get-tuple-element.34), channel_id=1, source_target_pairs={{0,256},{256,0},{1,257},{257,1},{2,258},{258,2},{3,259},{259,3},{4... | collective-permute-start | bytes 153608 | tf_op jit(solution)/shard_map/ppermute | solution.py:260
  14.3 6.8 %collective-permute-done = bf16[8,3200]{1,0:T(8,128)(2,1)S(1)} collective-permute-done((bf16[8,3200]{1,0:T(8,128)(2,1)S(1)}, bf16[8,3200]{1,0:T(8,128)(2,1)S(1)}, u32[]{:S(2)}, u32[]{:S(2)}) %collective-permute-start) | collective-permute-done | bytes 51232 | tf_op jit(solution)/shard_map/ppermute | solution.py:260
  21.2 0.8 broadcast_in_dim.64
  22.0 8.3 %all-to-all-start = ((bf16[4,2,8,3200]{3,2,1,0:T(8,128)(2,1)}), bf16[4,2,8,3200]{3,2,1,0:T(8,128)(2,1)S(1)}, u32[]{:S(2)}, u32[]{:S(2)}) async-start(bf16[4,2,8,3200]{3,2,1,0:T(8,128)(2,1)} %broadcast_in_dim.64), calls=%async_computation | async-start | bytes 819200 | tf_op jit(solution)/shard_map/all_to_all | solution.py:256
  30.9 11.0 %collective-permute-start.1 = (bf16[144,256]{1,0:T(8,128)(2,1)S(1)}, bf16[144,256]{1,0:T(8,128)(2,1)S(1)}, u32[]{:S(2)}, u32[]{:S(2)}) collective-permute-start(bf16[144,256]{1,0:T(8,128)(2,1)S(1)} %get-tuple-element.36), channel_id=1, source_target_pairs={{0,14},{2,0},{4,2},{6,4},{8,6},{10,8},{12,10},{14,12},{1,15},{3,1}... | collective-permute-start | bytes 221192 | tf_op jit(solution)/shard_map/ppermute | solution.py:278
  42.0 3.0 %collective-permute-start.2 = (bf16[144,256]{1,0:T(8,128)(2,1)S(1)}, bf16[144,256]{1,0:T(8,128)(2,1)S(1)}, u32[]{:S(2)}, u32[]{:S(2)}) collective-permute-start(bf16[144,256]{1,0:T(8,128)(2,1)S(1)} %get-tuple-element.37), channel_id=1, source_target_pairs={{0,2},{2,4},{4,6},{6,8},{8,10},{10,12},{12,14},{14,0},{1,3},{3,5},... | collective-permute-start | bytes 221192 | tf_op jit(solution)/shard_map/ppermute | solution.py:278
  45.0 5.7 %all-gather.7.cloned.1.call-done = bf16[352,1536]{1,0:T(8,128)(2,1)} async-done(((bf16[88,1536]{1,0:T(8,128)(2,1)}), bf16[352,1536]{1,0:T(8,128)(2,1)}) %all-gather.7.cloned.1.call-update) | async-done | bytes 1081360 | tf_op jit(solution)/shard_map/all_gather | solution.py:321
  50.7 1.8 slice.50
  52.4 9.2 %collective-permute-done.2.west = bf16[144,256]{1,0:T(8,128)(2,1)S(1)} collective-permute-done((bf16[144,256]{1,0:T(8,128)(2,1)S(1)}, bf16[144,256]{1,0:T(8,128)(2,1)S(1)}, u32[]{:S(2)}, u32[]{:S(2)}) %collective-permute-start.2) | collective-permute-done | bytes 73760 | tf_op jit(solution)/shard_map/ppermute | solution.py:278
  61.7 1.0 broadcast_in_dim.65
  62.6 3.5 %all-to-all-start.1 = ((bf16[4,4,2,8,1664]{4,3,2,1,0:T(8,128)(2,1)}), bf16[4,4,2,8,1664]{4,3,2,1,0:T(8,128)(2,1)S(1)}, u32[]{:S(2)}, u32[]{:S(2)}) async-start(bf16[4,4,2,8,1664]{4,3,2,1,0:T(8,128)(2,1)} %broadcast_in_dim.65), calls=%async_computation.1 | async-start | bytes 1703936 | tf_op jit(solution)/shard_map/all_to_all | solution.py:256
  66.2 4.4 %collective-permute-start.3 = (bf16[4,2,8,1536]{3,2,1,0:T(8,128)(2,1)S(1)}, bf16[4,2,8,1536]{3,2,1,0:T(8,128)(2,1)S(1)}, u32[]{:S(2)}, u32[]{:S(2)}) collective-permute-start(bf16[4,2,8,1536]{3,2,1,0:T(8,128)(2,1)S(1)} %get-tuple-element.64), channel_id=1, source_target_pairs={{16,0},{32,16},{48,32},{0,48},{17,1},{33,17},{49,33},{1,49},{18,2}... | collective-permute-start | bytes 589832 | tf_op jit(solution)/shard_map/ppermute | solution.py:267
  70.6 2.4 %collective-permute-start.4 = (bf16[4,2,8,1536]{3,2,1,0:T(8,128)(2,1)S(1)}, bf16[4,2,8,1536]{3,2,1,0:T(8,128)(2,1)S(1)}, u32[]{:S(2)}, u32[]{:S(2)}) collective-permute-start(bf16[4,2,8,1536]{3,2,1,0:T(8,128)(2,1)S(1)} %get-tuple-element.64), channel_id=1, source_target_pairs={{32,0},{48,16},{0,32},{16,48},{33,1},{49,17},{1,33},{17,49},{34,2}... | collective-permute-start | bytes 589832 | tf_op jit(solution)/shard_map/ppermute | solution.py:267
  73.0 2.5 %collective-permute-start.5 = (bf16[4,2,8,1536]{3,2,1,0:T(8,128)(2,1)S(1)}, bf16[4,2,8,1536]{3,2,1,0:T(8,128)(2,1)S(1)}, u32[]{:S(2)}, u32[]{:S(2)}) collective-permute-start(bf16[4,2,8,1536]{3,2,1,0:T(8,128)(2,1)S(1)} %get-tuple-element.64), channel_id=1, source_target_pairs={{48,0},{0,16},{16,32},{32,48},{49,1},{1,17},{17,33},{33,49},{50,2}... | collective-permute-start | bytes 589832 | tf_op jit(solution)/shard_map/ppermute | solution.py:267
  75.5 3.9 %collective-permute-done.4 = bf16[4,2,8,1536]{3,2,1,0:T(8,128)(2,1)S(1)} collective-permute-done((bf16[4,2,8,1536]{3,2,1,0:T(8,128)(2,1)S(1)}, bf16[4,2,8,1536]{3,2,1,0:T(8,128)(2,1)S(1)}, u32[]{:S(2)}, u32[]{:S(2)}) %collective-permute-start.4) | collective-permute-done | bytes 196640 | tf_op jit(solution)/shard_map/ppermute | solution.py:267
  79.4 5.2 %collective-permute-done.5 = bf16[4,2,8,1536]{3,2,1,0:T(8,128)(2,1)S(1)} collective-permute-done((bf16[4,2,8,1536]{3,2,1,0:T(8,128)(2,1)S(1)}, bf16[4,2,8,1536]{3,2,1,0:T(8,128)(2,1)S(1)}, u32[]{:S(2)}, u32[]{:S(2)}) %collective-permute-start.5) | collective-permute-done | bytes 196640 | tf_op jit(solution)/shard_map/ppermute | solution.py:267
  84.6 1.0 pad_maximum_fusion
  85.6 2.2 %broadcast_in_dim.66 = bf16[4,4,4,2,8,1664]{5,4,3,2,1,0:T(8,128)(2,1)} broadcast(bf16[4,4,2,8,1664]{4,3,2,1,0:T(8,128)(2,1)S(1)} %all-to-all-done.1), dimensions={1,2,3,4,5} | broadcast | bytes 4259840 | tf_op jit(solution)/shard_map/broadcast_in_dim | solution.py:255
  87.8 4.7 %all-to-all-start.2 = ((bf16[4,4,4,2,8,1664]{5,4,3,2,1,0:T(8,128)(2,1)}), bf16[4,4,4,2,8,1664]{5,4,3,2,1,0:T(8,128)(2,1)}, u32[]{:S(2)}, u32[]{:S(2)}) async-start(bf16[4,4,4,2,8,1664]{5,4,3,2,1,0:T(8,128)(2,1)} %broadcast_in_dim.66), calls=%async_computation.2 | async-start | bytes 6815744 | tf_op jit(solution)/shard_map/all_to_all | solution.py:256
  92.7 0.9 compare_select_fusion.bias
  93.6 0.9 fusion.row_order
  95.2 3.4 %collective-permute-start.6 = (bf16[216,256]{1,0:T(8,128)(2,1)S(1)}, bf16[216,256]{1,0:T(8,128)(2,1)S(1)}, u32[]{:S(2)}, u32[]{:S(2)}) collective-permute-start(bf16[216,256]{1,0:T(8,128)(2,1)S(1)} %get-tuple-element.43), channel_id=1, source_target_pairs={{0,16},{16,32},{32,48},{48,64},{64,80},{80,96},{96,112},{112,128},... | collective-permute-start | bytes 331784 | tf_op jit(solution)/shard_map/ppermute | solution.py:273
  98.6 5.3 %collective-permute-start.7 = (bf16[216,256]{1,0:T(8,128)(2,1)S(1)}, bf16[216,256]{1,0:T(8,128)(2,1)S(1)}, u32[]{:S(2)}, u32[]{:S(2)}) collective-permute-start(bf16[216,256]{1,0:T(8,128)(2,1)S(1)} %get-tuple-element.44), channel_id=1, source_target_pairs={{0,496},{16,0},{32,16},{48,32},{64,48},{80,64},{96,80},{112,96},{1... | collective-permute-start | bytes 331784 | tf_op jit(solution)/shard_map/ppermute | solution.py:273
  104.0 3.0 %collective-permute-start.10 = (bf16[256,1536]{1,0:T(8,128)(2,1)}, bf16[256,1536]{1,0:T(8,128)(2,1)}, u32[]{:S(2)}, u32[]{:S(2)}) collective-permute-start(bf16[256,1536]{1,0:T(8,128)(2,1)} %bitcast.14.first), channel_id=1, source_target_pairs={{12,0},{0,4},{4,8},{8,12},{13,1},{1,5},{5,9},{9,13},{14,2},{2,6},{... | collective-permute-start | bytes 2359304 | tf_op jit(solution)/shard_map/ppermute | solution.py:267
  107.0 3.4 %collective-permute-start.8 = (bf16[256,1536]{1,0:T(8,128)(2,1)}, bf16[256,1536]{1,0:T(8,128)(2,1)}, u32[]{:S(2)}, u32[]{:S(2)}) collective-permute-start(bf16[256,1536]{1,0:T(8,128)(2,1)} %bitcast.14.first), channel_id=1, source_target_pairs={{4,0},{8,4},{12,8},{0,12},{5,1},{9,5},{13,9},{1,13},{6,2},{10,6},{... | collective-permute-start | bytes 2359304 | tf_op jit(solution)/shard_map/ppermute | solution.py:267
  110.5 3.3 %collective-permute-start.9 = (bf16[256,1536]{1,0:T(8,128)(2,1)}, bf16[256,1536]{1,0:T(8,128)(2,1)}, u32[]{:S(2)}, u32[]{:S(2)}) collective-permute-start(bf16[256,1536]{1,0:T(8,128)(2,1)} %bitcast.14.first), channel_id=1, source_target_pairs={{8,0},{12,4},{0,8},{4,12},{9,1},{13,5},{1,9},{5,13},{10,2},{14,6},... | collective-permute-start | bytes 2359304 | tf_op jit(solution)/shard_map/ppermute | solution.py:267
  113.8 17.2 %collective-permute-done.6 = bf16[216,256]{1,0:T(8,128)(2,1)S(1)} collective-permute-done((bf16[216,256]{1,0:T(8,128)(2,1)S(1)}, bf16[216,256]{1,0:T(8,128)(2,1)S(1)}, u32[]{:S(2)}, u32[]{:S(2)}) %collective-permute-start.6) | collective-permute-done | bytes 110624 | tf_op jit(solution)/shard_map/ppermute | solution.py:273
  131.1 1.9 %collective-permute-done.7 = bf16[216,256]{1,0:T(8,128)(2,1)S(1)} collective-permute-done((bf16[216,256]{1,0:T(8,128)(2,1)S(1)}, bf16[216,256]{1,0:T(8,128)(2,1)S(1)}, u32[]{:S(2)}, u32[]{:S(2)}) %collective-permute-start.7) | collective-permute-done | bytes 110624 | tf_op jit(solution)/shard_map/ppermute | solution.py:273
  133.0 3.6 %all_gather.26.rims = bf16[720,512]{1,0:T(8,128)(2,1)S(1)} all-gather(bf16[720,256]{1,0:T(8,128)(2,1)S(1)} %pad_maximum_fusion.1), channel_id=1, replica_groups=mesh['za'=2,'zq'=4,'x'=4,'y'=4,'zh'=2,'core'=2] {'core'}, dimensions={1}, use_global_device_ids=true | all-gather | bytes 1105920 | tf_op jit(solution)/shard_map/all_gather | solution.py:344
  136.6 4.7 %shard_map.184.windows = bf16[9,144,512]{2,1,0:T(8,128)(2,1)S(1)} custom-call(bf16[576,512]{1,0:T(8,128)(2,1)S(1)} %copy-done.1, bf16[720,512]{1,0:T(8,128)(2,1)S(1)} %all_gather.26.rims, s32[9,144,1]{2,1,0:T(8,128)S(1)} %copy-done.5), custom_call_target="tpu_custom_call" | custom-call | flops 100000000 | bytes 1048576 | tf_op jit(solution)/shard_map/pallas_call | solution.py:112
  141.4 1.8 slice_bitcast_fusion.1
  143.6 1.4 slice.51
  145.4 0.7 copy-done.4
  146.1 8.7 %shard_map.185 = bf16[576,256]{1,0:T(8,128)(2,1)S(1)} custom-call(bf16[9,144,512]{2,1,0:T(8,128)(2,1)S(1)} %shard_map.184.windows, bf16[512,640]{1,0:T(8,128)(2,1)S(1)} %bitcast.52, bf16[512,640]{1,0:T(8,128)(2,1)S(1)} %bitcast.50, f32[3,144,144]{2,1,0:T(8,128)S(1)} %copy-done.4, s32[9,1,144]{2,1,0:T(1,128)S(1)} %copy-done.11), custom_call_target="tpu_custom_call" | custom-call | flops 100000000 | bytes 1048576 | tf_op jit(solution)/shard_map/pallas_call | solution.py:112
  154.8 2.2 %all_gather.27.heads = bf16[576,512]{1,0:T(8,128)(2,1)S(1)} all-gather(bf16[576,256]{1,0:T(8,128)(2,1)S(1)} %shard_map.185), channel_id=1, replica_groups=mesh['za'=2,'zq'=4,'x'=4,'y'=4,'zh'=2,'core'=2] {'core'}, dimensions={1}, use_global_device_ids=true | all-gather | bytes 884736 | tf_op jit(solution)/shard_map/all_gather | solution.py:384
  157.0 1.4 shard_map.186
  158.9 2.0 %all_gather.28.coarse = bf16[144,1024]{1,0:T(8,128)(2,1)S(1)} all-gather(bf16[144,512]{1,0:T(8,128)(2,1)S(1)} %convolution_convert_fusion.1), channel_id=1, replica_groups=mesh['za'=2,'zq'=4,'x'=4,'y'=4,'zh'=2,'core'=2] {'core'}, dimensions={1}, use_global_device_ids=true | all-gather | bytes 442368 | tf_op jit(solution)/shard_map/all_gather | solution.py:393
  161.0 5.1 %shard_map.187 = bf16[4,144,128]{2,1,0:T(8,128)(2,1)S(1)} custom-call(s32[4]{0:T(128)S(1)} %and_select_fusion.order, bf16[144,1024]{1,0:T(8,128)(2,1)S(1)} %all_gather.28.coarse, f32[1,1024]{1,0:T(1,128)S(1)} %bitcast.56, bf16[1024,1024]{1,0:T(8,128)(2,1)S(1)} %fusion.row_order, bf16[256,1536]{1,0:T(8,128)(2,1)} %bitcast.14.first, ...), custom_call_target="tpu_custom_call" | custom-call | flops 100000000 | bytes 1048576 | tf_op jit(solution)/shard_map/pallas_call | solution.py:112
  166.6 2.2 %all-gather.1 = bf16[288,1024]{1,0:T(8,128)(2,1)S(1)} all-gather(bf16[144,1024]{1,0:T(8,128)(2,1)S(1)} %convolution_convert_fusion), channel_id=3, replica_groups=mesh['za'=2,'zq'=4,'x'=4,'y'=4,'zh'=2,'core'=2] {'core'}, dimensions={0}, use_global_device_ids=true | all-gather | bytes 884736 | tf_op jit(solution)/shard_map/all_gather | solution.py:415
  170.1 3.9 %all-reduce = (f32[144,4]{1,0:T(8,128)S(1)}, f32[144,4]{1,0:T(8,128)S(1)}) all-reduce(f32[144,4]{1,0:T(8,128)S(1)} %get-tuple-element.56, f32[144,4]{1,0:T(8,128)S(1)} %get-tuple-element.55), channel_id=1, replica_groups=mesh['za'=2,'zq'=4,'x'=4,'y'=4,'zh'=2,'core'=2] {'core'}, use_global_device_ids=true, to_apply=%region_1.2 | all-reduce | flops 1152 | bytes 9216 | tf_op jit(solution)/shard_map/psum | solution.py:419
  174.1 1.7 shard_map.188
  (75 shorter events, 4.8 us)
Async XLA Ops:
  6.5 23.7 %copy-start.9 = (s32[144,1]{1,0:T(8,128)S(1)}, s32[144,1]{1,0:T(8,128)}, u32[]{:S(2)}) copy-start(s32[144,1]{1,0:T(8,128)} %constant.175.clone.first_place) | copy-start | bytes 1732
  6.5 23.7 %copy-start.10 = (s32[144,1]{1,0:T(8,128)S(1)}, s32[144,1]{1,0:T(8,128)}, u32[]{:S(2)}) copy-start(s32[144,1]{1,0:T(8,128)} %constant.176.clone.last_place) | copy-start | bytes 1732
  6.5 23.7 %copy-start.2 = (bf16[2,12,24,512]{3,2,1,0:T(8,128)(2,1)S(1)}, bf16[2,12,24,512]{3,2,1,0:T(8,128)(2,1)}, u32[]{:S(2)}) copy-start(bf16[2,12,24,512]{3,2,1,0:T(8,128)(2,1)} %param.19) | copy-start | bytes 1769476
  6.5 23.7 %copy-start.15 = (f32[512]{0:T(512)S(1)}, f32[512]{0:T(512)}, u32[]{:S(2)}) copy-start(f32[512]{0:T(512)} %param.20) | copy-start | bytes 6148
  6.5 44.1 %all-gather.7.cloned.1.call-start = ((), (), s32[]{:S(2)}) async-start(), calls=%async_computation.4 | async-start | bytes 1351680 | tf_op jit(solution)/shard_map/all_gather | solution.py:321
  8.4 0.8 copy-start.17
  9.2 0.8 copy-start.18
  10.1 0.8 copy-start.19
  10.8 0.7 copy-start.20
  12.4 8.8 %collective-permute-start = (bf16[8,3200]{1,0:T(8,128)(2,1)S(1)}, bf16[8,3200]{1,0:T(8,128)(2,1)S(1)}, u32[]{:S(2)}, u32[]{:S(2)}) collective-permute-start(bf16[8,3200]{1,0:T(8,128)(2,1)S(1)} %get-tuple-element.34), channel_id=1, source_target_pairs={{0,256},{256,0},{1,257},{257,1},{2,258},{258,2},{3,259},{259,3},{4... | collective-permute-start | bytes 153608 | tf_op jit(solution)/shard_map/ppermute | solution.py:260
  22.0 39.7 %all-to-all-start = ((bf16[4,2,8,3200]{3,2,1,0:T(8,128)(2,1)}), bf16[4,2,8,3200]{3,2,1,0:T(8,128)(2,1)S(1)}, u32[]{:S(2)}, u32[]{:S(2)}) async-start(bf16[4,2,8,3200]{3,2,1,0:T(8,128)(2,1)} %broadcast_in_dim.64), calls=%async_computation | async-start | bytes 819200 | tf_op jit(solution)/shard_map/all_to_all | solution.py:256
  30.2 130.7 %all-gather.5.cloned.1.call-start = ((), (), s32[]{:S(2)}) async-start(), calls=%async_computation.3 | async-start | bytes 3538944 | tf_op jit(solution)/shard_map/all_gather | solution.py:327
  30.9 63.6 %copy-start = (bf16[576,512]{1,0:T(8,128)(2,1)}, bf16[576,512]{1,0:T(8,128)(2,1)S(1)}, u32[]{:S(2)}) copy-start(bf16[576,512]{1,0:T(8,128)(2,1)S(1)} %get-tuple-element.33.normed) | copy-start | bytes 1769476
  30.9 21.5 %collective-permute-start.1 = (bf16[144,256]{1,0:T(8,128)(2,1)S(1)}, bf16[144,256]{1,0:T(8,128)(2,1)S(1)}, u32[]{:S(2)}, u32[]{:S(2)}) collective-permute-start(bf16[144,256]{1,0:T(8,128)(2,1)S(1)} %get-tuple-element.36), channel_id=1, source_target_pairs={{0,14},{2,0},{4,2},{6,4},{8,6},{10,8},{12,10},{14,12},{1,15},{3,1}... | collective-permute-start | bytes 221192 | tf_op jit(solution)/shard_map/ppermute | solution.py:278
  42.0 19.6 %collective-permute-start.2 = (bf16[144,256]{1,0:T(8,128)(2,1)S(1)}, bf16[144,256]{1,0:T(8,128)(2,1)S(1)}, u32[]{:S(2)}, u32[]{:S(2)}) collective-permute-start(bf16[144,256]{1,0:T(8,128)(2,1)S(1)} %get-tuple-element.37), channel_id=1, source_target_pairs={{0,2},{2,4},{4,6},{6,8},{8,10},{10,12},{12,14},{14,0},{1,3},{3,5},... | collective-permute-start | bytes 221192 | tf_op jit(solution)/shard_map/ppermute | solution.py:278
  62.6 23.0 %all-to-all-start.1 = ((bf16[4,4,2,8,1664]{4,3,2,1,0:T(8,128)(2,1)}), bf16[4,4,2,8,1664]{4,3,2,1,0:T(8,128)(2,1)S(1)}, u32[]{:S(2)}, u32[]{:S(2)}) async-start(bf16[4,4,2,8,1664]{4,3,2,1,0:T(8,128)(2,1)} %broadcast_in_dim.65), calls=%async_computation.1 | async-start | bytes 1703936 | tf_op jit(solution)/shard_map/all_to_all | solution.py:256
  66.2 9.3 %collective-permute-start.3 = (bf16[4,2,8,1536]{3,2,1,0:T(8,128)(2,1)S(1)}, bf16[4,2,8,1536]{3,2,1,0:T(8,128)(2,1)S(1)}, u32[]{:S(2)}, u32[]{:S(2)}) collective-permute-start(bf16[4,2,8,1536]{3,2,1,0:T(8,128)(2,1)S(1)} %get-tuple-element.64), channel_id=1, source_target_pairs={{16,0},{32,16},{48,32},{0,48},{17,1},{33,17},{49,33},{1,49},{18,2}... | collective-permute-start | bytes 589832 | tf_op jit(solution)/shard_map/ppermute | solution.py:267
  70.6 8.9 %collective-permute-start.4 = (bf16[4,2,8,1536]{3,2,1,0:T(8,128)(2,1)S(1)}, bf16[4,2,8,1536]{3,2,1,0:T(8,128)(2,1)S(1)}, u32[]{:S(2)}, u32[]{:S(2)}) collective-permute-start(bf16[4,2,8,1536]{3,2,1,0:T(8,128)(2,1)S(1)} %get-tuple-element.64), channel_id=1, source_target_pairs={{32,0},{48,16},{0,32},{16,48},{33,1},{49,17},{1,33},{17,49},{34,2}... | collective-permute-start | bytes 589832 | tf_op jit(solution)/shard_map/ppermute | solution.py:267
  73.0 11.7 %collective-permute-start.5 = (bf16[4,2,8,1536]{3,2,1,0:T(8,128)(2,1)S(1)}, bf16[4,2,8,1536]{3,2,1,0:T(8,128)(2,1)S(1)}, u32[]{:S(2)}, u32[]{:S(2)}) collective-permute-start(bf16[4,2,8,1536]{3,2,1,0:T(8,128)(2,1)S(1)} %get-tuple-element.64), channel_id=1, source_target_pairs={{48,0},{0,16},{16,32},{32,48},{49,1},{1,17},{17,33},{33,49},{50,2}... | collective-permute-start | bytes 589832 | tf_op jit(solution)/shard_map/ppermute | solution.py:267
  87.8 53.6 %all-to-all-start.2 = ((bf16[4,4,4,2,8,1664]{5,4,3,2,1,0:T(8,128)(2,1)}), bf16[4,4,4,2,8,1664]{5,4,3,2,1,0:T(8,128)(2,1)}, u32[]{:S(2)}, u32[]{:S(2)}) async-start(bf16[4,4,4,2,8,1664]{5,4,3,2,1,0:T(8,128)(2,1)} %broadcast_in_dim.66), calls=%async_computation.2 | async-start | bytes 6815744 | tf_op jit(solution)/shard_map/all_to_all | solution.py:256
  92.5 2.0 %copy-start.7 = (s32[216,1]{1,0:T(8,128)S(1)}, s32[216,1]{1,0:T(8,128)}, u32[]{:S(2)}) copy-start(s32[216,1]{1,0:T(8,128)} %constant.177.clone.first_place) | copy-start | bytes 2596
  92.5 2.0 %copy-start.8 = (s32[216,1]{1,0:T(8,128)S(1)}, s32[216,1]{1,0:T(8,128)}, u32[]{:S(2)}) copy-start(s32[216,1]{1,0:T(8,128)} %constant.178.clone.last_place) | copy-start | bytes 2596
  93.6 43.0 %copy-start.5 = (s32[9,144,1]{2,1,0:T(8,128)S(1)}, s32[9,144,1]{2,1,0:T(8,128)}, u32[]{:S(2)}) copy-start(s32[9,144,1]{2,1,0:T(8,128)} %constant.179.clone.column) | copy-start | bytes 15556
  95.2 41.4 %copy-start.1 = (bf16[576,512]{1,0:T(8,128)(2,1)S(1)}, bf16[576,512]{1,0:T(8,128)(2,1)}, u32[]{:S(2)}) copy-start(bf16[576,512]{1,0:T(8,128)(2,1)} %copy-done) | copy-start | bytes 1769476
  95.2 35.8 %collective-permute-start.6 = (bf16[216,256]{1,0:T(8,128)(2,1)S(1)}, bf16[216,256]{1,0:T(8,128)(2,1)S(1)}, u32[]{:S(2)}, u32[]{:S(2)}) collective-permute-start(bf16[216,256]{1,0:T(8,128)(2,1)S(1)} %get-tuple-element.43), channel_id=1, source_target_pairs={{0,16},{16,32},{32,48},{48,64},{64,80},{80,96},{96,112},{112,128},... | collective-permute-start | bytes 331784 | tf_op jit(solution)/shard_map/ppermute | solution.py:273
  98.6 34.3 %collective-permute-start.7 = (bf16[216,256]{1,0:T(8,128)(2,1)S(1)}, bf16[216,256]{1,0:T(8,128)(2,1)S(1)}, u32[]{:S(2)}, u32[]{:S(2)}) collective-permute-start(bf16[216,256]{1,0:T(8,128)(2,1)S(1)} %get-tuple-element.44), channel_id=1, source_target_pairs={{0,496},{16,0},{32,16},{48,32},{64,48},{80,64},{96,80},{112,96},{1... | collective-permute-start | bytes 331784 | tf_op jit(solution)/shard_map/ppermute | solution.py:273
  104.0 57.0 %collective-permute-start.10 = (bf16[256,1536]{1,0:T(8,128)(2,1)}, bf16[256,1536]{1,0:T(8,128)(2,1)}, u32[]{:S(2)}, u32[]{:S(2)}) collective-permute-start(bf16[256,1536]{1,0:T(8,128)(2,1)} %bitcast.14.first), channel_id=1, source_target_pairs={{12,0},{0,4},{4,8},{8,12},{13,1},{1,5},{5,9},{9,13},{14,2},{2,6},{... | collective-permute-start | bytes 2359304 | tf_op jit(solution)/shard_map/ppermute | solution.py:267
  107.0 53.9 %collective-permute-start.8 = (bf16[256,1536]{1,0:T(8,128)(2,1)}, bf16[256,1536]{1,0:T(8,128)(2,1)}, u32[]{:S(2)}, u32[]{:S(2)}) collective-permute-start(bf16[256,1536]{1,0:T(8,128)(2,1)} %bitcast.14.first), channel_id=1, source_target_pairs={{4,0},{8,4},{12,8},{0,12},{5,1},{9,5},{13,9},{1,13},{6,2},{10,6},{... | collective-permute-start | bytes 2359304 | tf_op jit(solution)/shard_map/ppermute | solution.py:267
  110.5 50.5 %collective-permute-start.9 = (bf16[256,1536]{1,0:T(8,128)(2,1)}, bf16[256,1536]{1,0:T(8,128)(2,1)}, u32[]{:S(2)}, u32[]{:S(2)}) collective-permute-start(bf16[256,1536]{1,0:T(8,128)(2,1)} %bitcast.14.first), channel_id=1, source_target_pairs={{8,0},{12,4},{0,8},{4,12},{9,1},{13,5},{1,9},{5,13},{10,2},{14,6},... | collective-permute-start | bytes 2359304 | tf_op jit(solution)/shard_map/ppermute | solution.py:267
  145.0 1.0 copy-start.4
  145.1 1.0 copy-start.11
  146.1 11.0 %copy-start.3 = (bf16[2,12,24,512]{3,2,1,0:T(8,128)(2,1)S(1)}, bf16[2,12,24,512]{3,2,1,0:T(8,128)(2,1)}, u32[]{:S(2)}) copy-start(bf16[2,12,24,512]{3,2,1,0:T(8,128)(2,1)} %param.19) | copy-start | bytes 1769476
  146.1 11.0 %copy-start.6 = (s32[4,144,1]{2,1,0:T(8,128)S(1)}, s32[4,144,1]{2,1,0:T(8,128)}, u32[]{:S(2)}) copy-start(s32[4,144,1]{2,1,0:T(8,128)} %constant.181.clone.places) | copy-start | bytes 6916
  146.1 11.0 %copy-start.12 = (f32[2048]{0:T(1024)S(1)}, f32[2048]{0:T(1024)}, u32[]{:S(2)}) copy-start(f32[2048]{0:T(1024)} %param.23) | copy-start | bytes 24580
  158.4 2.6 %copy-start.13 = (f32[1024]{0:T(1024)S(1)}, f32[1024]{0:T(1024)}, u32[]{:S(2)}) copy-start(f32[1024]{0:T(1024)} %param.25) | copy-start | bytes 12292
  161.0 5.1 %copy-start.21 = (bf16[1024,1536]{1,0:T(8,128)(2,1)S(1)}, bf16[1024,1536]{1,0:T(8,128)(2,1)}, u32[]{:S(2)}) copy-start(bf16[1024,1536]{1,0:T(8,128)(2,1)} %all-gather.5.cloned.1.call-done) | copy-start | bytes 9437188
  168.9 5.1 %copy-start.14 = (s32[4,1,144]{2,1,0:T(1,128)S(1)}, s32[4,1,144]{2,1,0:T(1,128)}, u32[]{:S(2)}) copy-start(s32[4,1,144]{2,1,0:T(1,128)} %constant.182.clone.places) | copy-start | bytes 6916
  168.9 5.1 %copy-start.16 = (f32[512]{0:T(512)S(1)}, f32[512]{0:T(512)}, u32[]{:S(2)}) copy-start(f32[512]{0:T(512)} %param.29) | copy-start | bytes 6148
Sparse Core Ops, SparseCore 0:
  14.4 36.1 all-gather.6
  61.8 75.0 all-gather.4

commit v6 on v5

--- a/solution.py
+++ b/solution.py
@@ -125,7 +125,7 @@
 def pack_kernel(place, fine_qkv, fine_proj, merge, coarse_qkv, coarse_proj, split, early, late):
     y = place[0]
     wide = jnp.concatenate(
-        [fine_qkv[:, part, :].astype(jnp.float32) for part in range(3)]
+        [fine_qkv[part].astype(jnp.float32) for part in range(3)]
         + [fine_proj[...].astype(jnp.float32)],
         axis=1,
     )
@@ -136,7 +136,7 @@
     early[:, 640:1152] = rows[:8].astype(jnp.bfloat16)
     early[:, 1152:1664] = rows[8:].astype(jnp.bfloat16)
     for part in range(3):
-        cols = coarse_qkv[:, part, pl.ds(pl.multiple_of(y * 128, 128), 128)].astype(jnp.float32)
+        cols = coarse_qkv[part, :, pl.ds(pl.multiple_of(y * 128, 128), 128)].astype(jnp.float32)
         for block in range(4):
             start = 1664 + 384 * block + 128 * part
             early[:, start : start + 128] = cols[8 * block : 8 * block + 8].astype(jnp.bfloat16)
@@ -213,16 +213,23 @@
     order, coarse, gain, row_order, first, second, third, fourth, out, pieces, arrived
 ):
     copies = [
-        pltpu.make_async_copy(piece, pieces.at[place], arrived.at[place])
-        for place, piece in enumerate((first, second, third, fourth))
+        [
+            pltpu.make_async_copy(
+                quad.at[place], pieces.at[place, 64 * x : 64 * (x + 1)], arrived.at[place, x]
+            )
+            for x, quad in enumerate((first, second, third, fourth))
+        ]
+        for place in range(4)
     ]
-    for copy in copies:
-        copy.start()
+    for piece in copies:
+        for copy in piece:
+            copy.start()
     normed = layer_norm(coarse[...].astype(jnp.float32), gain[...]).astype(jnp.bfloat16)
     normed = project_with(normed, row_order[...]).astype(jnp.bfloat16)
     lower = lax.broadcasted_iota(jnp.int32, (1, 2 * HEAD), 1) < HEAD
-    for place, copy in enumerate(copies):
-        copy.wait()
+    for place, piece in enumerate(copies):
+        for copy in piece:
+            copy.wait()
         packed = jnp.zeros((normed.shape[0], 384), jnp.float32)
         for part in range(4):
             packed += project_with(
@@ -234,13 +241,14 @@
         out[order[place]] = mixed.astype(jnp.bfloat16)
 
 
-def final_kernel(core, expanded, first_sum, second_sum, gain, residual, places, out):
+def final_kernel(core, expanded, sums, gain, residual, places, out):
     half = jnp.where(core[0] == 0, residual[:, :256], residual[:, 256:]).astype(jnp.float32)
     own_gain = jnp.where(core[0] == 0, gain[:, :256], gain[:, 256:])
+    both = sums[:COARSE] + sums[COARSE:]
     total = half
     for part in range(4):
-        average = first_sum[:, part : part + 1] / 512
-        spread = second_sum[:, part : part + 1] / 512 - average * average
+        average = both[:, part : part + 1] / 512
+        spread = both[:, 4 + part : 5 + part] / 512 - average * average
         values = expanded[:, 256 * part : 256 * (part + 1)] - average
         values = values * lax.rsqrt(spread + EPSILON) * own_gain
         high = values.astype(jnp.bfloat16)
@@ -271,11 +279,6 @@
 def lat_shift(value, by):
     perm = [(i, (i + by) % 32) for i in range(32)]
     return lax.ppermute(value, ("za", "zq", "x"), perm)
-
-
-def lon_shift(value, by):
-    perm = [(i, (i + by) % 8) for i in range(8)]
-    return lax.ppermute(value, ("y", "zh"), perm)
 
 
 def body(
@@ -302,10 +305,10 @@
         (shape(8, 3200), shape(88, 1536)),
         (
             y_place.astype(jnp.int32)[None],
-            fine_qkv,
+            fine_qkv.transpose(1, 0, 2),
             fine_proj.T,
             merge_weight,
-            coarse_qkv,
+            coarse_qkv.transpose(1, 0, 2),
             coarse_proj.T,
             split_weight,
         ),
@@ -321,17 +324,22 @@
     late = lax.all_gather(late_shard, "x", axis=0, tiled=False)
     late = late[:, :32].reshape(128, 1536)
     depth = sent_to_all(depth_pair(early), "zq")
-    east = lon_shift(first_cols, -1)
-    west = lon_shift(last_cols, 1)
-    depth, late, east, west = lax.optimization_barrier((depth, late, east, west))
+    even = lax.axis_index("zh") == 0
+    same_row = lax.ppermute(jnp.where(even, last_cols, first_cols), "zh", [(0, 1), (1, 0)])
+    perm = [(2 * i + 1, (2 * i + 2) % 8) for i in range(4)]
+    perm += [(there, here) for here, there in perm]
+    next_row = lax.ppermute(jnp.where(even, first_cols, last_cols), ("y", "zh"), perm)
+    depth, late, same_row = lax.optimization_barrier((depth, late, same_row))
     late = lax.all_gather(late, ("za", "zq"), axis=0, tiled=True)
-    merge_side = sent_to_all(depth[..., :1664], "y")
-    qkv_quad = jnp.stack(from_others(depth[..., 1664:], "x")).reshape(256, 1536)
-    merge_side, qkv_quad, east, west = lax.optimization_barrier(
-        (merge_side, qkv_quad, east, west)
-    )
-    qkv_pieces = from_others(qkv_quad, "y")
-    both_all = sent_to_all(merge_side, "x")
+    merge_side = sent_to_all(depth[..., :1664], "x")
+    qkv_quad = jnp.stack(from_others(depth[..., 1664:], "y")).reshape(4, 64, 1536)
+    merge_side, qkv_quad, same_row, next_row = lax.optimization_barrier(
+        (merge_side, qkv_quad, same_row, next_row)
+    )
+    east = jnp.where(even, same_row, next_row)
+    west = jnp.where(even, next_row, same_row)
+    qkv_pieces = from_others(qkv_quad, "x")
+    both_all = sent_to_all(merge_side, "y")
     first_rows, last_rows = call(
         ends_kernel,
         (shape(ENDS, 256), shape(ENDS, 256)),
@@ -360,9 +368,9 @@
     labels = jnp.broadcast_to(labels, (3, LEVELS, WIN_LAT, WIN_LON)).reshape(3, WINDOW)
     bias = jnp.where(labels[:, :, None] == labels[:, None, :], 0.0, -1e30).astype(jnp.float32)
 
-    first_all = both_all[..., :640].reshape(4, 2, 2, 4, 2, 8, 640)
+    first_all = both_all[..., :640].reshape(2, 2, 4, 4, 2, 8, 640)
     left_weight, right_weight = (
-        first_all[:, :, part].transpose(3, 2, 0, 1, 4, 5).reshape(512, 640) for part in range(2)
+        first_all[:, part].transpose(3, 2, 1, 0, 4, 5).reshape(512, 640) for part in range(2)
     )
 
     constant = lambda i: (0, 0)
@@ -388,7 +396,7 @@
         (all_heads, right_weight, flat_tokens, merge_gain[None], QUARTETS[:, :, None]),
     )
     merge_all = jnp.stack([both_all[..., 640:1152], both_all[..., 1152:]], axis=4)
-    merge_all = merge_all.transpose(3, 2, 0, 1, 4, 5, 6).reshape(2048, 512)
+    merge_all = merge_all.transpose(3, 2, 1, 0, 4, 5, 6).reshape(2048, 512)
     coarse_half = project_with(merged_in, merge_all).astype(jnp.bfloat16)
     coarse_full = lax.all_gather(coarse_half, "core", axis=1, tiled=True)
 
@@ -407,7 +415,7 @@
         + [pl.BlockSpec(memory_space=pl.ANY)] * 4,
         scratch_shapes=[
             pltpu.VMEM((4, 256, 1536), jnp.bfloat16),
-            pltpu.SemaphoreType.DMA((4,)),
+            pltpu.SemaphoreType.DMA((4, 4)),
         ],
     )
     coarse_mixed = coarse_mixed.transpose(1, 0, 2).reshape(COARSE, 512)
@@ -416,17 +424,15 @@
     coarse_out = (coarse_full.astype(jnp.float32) + (both[0] + both[1])).astype(jnp.bfloat16)
     expanded = project_with(coarse_out, late[:, :1024])
     parts = expanded.reshape(COARSE, 4, 256)
-    first_sum, second_sum = lax.psum(
-        (jnp.sum(parts, axis=-1), jnp.sum(parts * parts, axis=-1)), "core"
-    )
+    sums = jnp.concatenate([jnp.sum(parts, axis=-1), jnp.sum(parts * parts, axis=-1)], axis=1)
+    sums = lax.all_gather(sums, "core", axis=0, tiled=True)
     restored = call(
         final_kernel,
         shape(OWN, 256),
         (
             core,
             expanded,
-            first_sum,
-            second_sum,
+            sums,
             split_gain[None],
             residual,
             QUARTETS[:, None, :],

time: 184 us -> 179 us (0.973)
  the two profiles are of different devices: /device:TPU:129 before, /device:TPU:195 now
where the time goes in v6:
time: 179 us; the launch traced here: 178 us
  starting transfers between devices  58 us (32%)
  waiting for transfers between devices  44.2 us (25%)
  Pallas kernels  23.9 us (13%)
  blocking collectives  16.7 us (9%)
  local copies, waits for them, and re-layouts  15.8 us (9%)
  between operations  14 us (8%)
  other arithmetic  3.63 us (2%)
    pallas_call x8, Pallas kernels, call(): pl.pallas_call(kernel, out_shape=out_shape, compiler_params=pltpu.Compile...  23.9 us
    ppermute x6, starting transfers between devices, from_others(): lax.ppermute(block, axis, [((i + by) % 4, i) for i in range(4)])  19.2 us
    ppermute x1, waiting for transfers between devices, body(): lax.ppermute(jnp.where(even, first_cols, last_cols), ('y', 'zh'), perm)  15.6 us
    all_to_all x3, starting transfers between devices, sent_to_all(): return lax.all_to_all(copies, axes, split_axis=0, concat_axis=0, tiled=True)  15.2 us
    all_gather x1, waiting for transfers between devices, body(): late = lax.all_gather(late_shard, 'x', axis=0, tiled=False)  9.86 us
    all_to_all x3, waiting for transfers between devices, sent_to_all(): return lax.all_to_all(copies, axes, split_axis=0, concat_axis=0, tiled=True)  9.78 us
    ppermute x1, waiting for transfers between devices, depth_pair(): other = lax.ppermute(block, 'za', [(0, 1), (1, 0)])  8.87 us
    ppermute x1, starting transfers between devices, body(): lax.ppermute(jnp.where(even, last_cols, first_cols), 'zh', [(0, 1), (1, 0)])  8.56 us
  transfers between devices with their start and end apart: 16, of which 5 were waited for; matrix products, arithmetic and copies ran while one was open for 7% of the time, Pallas kernels for 9%

profile of v6, /device:TPU:195, one launch (start us, length us, event | category | flops | bytes accessed | tf_op | source)
XLA Modules:
  0.0 177.7 jit_solution(2138039084908568697)
XLA Ops:
  6.6 0.9 copy-done.17
  7.6 0.8 copy-done.18
  8.4 0.8 copy-done.19
  9.2 0.8 copy-done.20
  10.0 0.7 copy-done.21
  10.7 0.7 copy-done.22
  11.4 0.8 shard_map.181
  12.3 1.9 %collective-permute-start = (bf16[8,3200]{1,0:T(8,128)(2,1)S(1)}, bf16[8,3200]{1,0:T(8,128)(2,1)S(1)}, u32[]{:S(2)}, u32[]{:S(2)}) collective-permute-start(bf16[8,3200]{1,0:T(8,128)(2,1)S(1)} %get-tuple-element.33), channel_id=1, source_target_pairs={{0,256},{256,0},{1,257},{257,1},{2,258},{258,2},{3,259},{259,3},{4... | collective-permute-start | bytes 153608 | tf_op jit(solution)/shard_map/ppermute | solution.py:268
  14.2 8.9 %collective-permute-done = bf16[8,3200]{1,0:T(8,128)(2,1)S(1)} collective-permute-done((bf16[8,3200]{1,0:T(8,128)(2,1)S(1)}, bf16[8,3200]{1,0:T(8,128)(2,1)S(1)}, u32[]{:S(2)}, u32[]{:S(2)}) %collective-permute-start) | collective-permute-done | bytes 51232 | tf_op jit(solution)/shard_map/ppermute | solution.py:268
  23.1 0.8 broadcast_in_dim.64
  23.9 5.6 %all-to-all-start = ((bf16[4,2,8,3200]{3,2,1,0:T(8,128)(2,1)}), bf16[4,2,8,3200]{3,2,1,0:T(8,128)(2,1)S(1)}, u32[]{:S(2)}, u32[]{:S(2)}) async-start(bf16[4,2,8,3200]{3,2,1,0:T(8,128)(2,1)} %broadcast_in_dim.64), calls=%async_computation | async-start | bytes 819200 | tf_op jit(solution)/shard_map/all_to_all | solution.py:264
  29.5 0.7 shard_map.182
  30.2 8.6 %collective-permute-start.1 = (bf16[144,256]{1,0:T(8,128)(2,1)S(1)}, bf16[144,256]{1,0:T(8,128)(2,1)S(1)}, u32[]{:S(2)}, u32[]{:S(2)}) collective-permute-start(bf16[144,256]{1,0:T(8,128)(2,1)S(1)} %get-tuple-element.62), channel_id=1, source_target_pairs={{0,2},{2,0},{1,3},{3,1},{4,6},{6,4},{5,7},{7,5},{8,10},{10,8},{9,1... | collective-permute-start | bytes 221192 | tf_op jit(solution)/shard_map/ppermute | solution.py:328
  38.8 9.9 %all-gather.8.cloned.1.call-done = bf16[352,1536]{1,0:T(8,128)(2,1)} async-done(((bf16[88,1536]{1,0:T(8,128)(2,1)}), bf16[352,1536]{1,0:T(8,128)(2,1)}) %all-gather.8.cloned.1.call-update) | async-done | bytes 1081360 | tf_op jit(solution)/shard_map/all_gather | solution.py:324
  48.7 1.8 slice.50
  50.5 1.0 broadcast_in_dim.65
  51.5 4.9 %all-to-all-start.1 = ((bf16[4,4,2,8,1664]{4,3,2,1,0:T(8,128)(2,1)}), bf16[4,4,2,8,1664]{4,3,2,1,0:T(8,128)(2,1)S(1)}, u32[]{:S(2)}, u32[]{:S(2)}) async-start(bf16[4,4,2,8,1664]{4,3,2,1,0:T(8,128)(2,1)} %broadcast_in_dim.65), calls=%async_computation.1 | async-start | bytes 1703936 | tf_op jit(solution)/shard_map/all_to_all | solution.py:264
  56.4 4.4 %collective-permute-start.2 = (bf16[4,2,8,1536]{3,2,1,0:T(8,128)(2,1)S(1)}, bf16[4,2,8,1536]{3,2,1,0:T(8,128)(2,1)S(1)}, u32[]{:S(2)}, u32[]{:S(2)}) collective-permute-start(bf16[4,2,8,1536]{3,2,1,0:T(8,128)(2,1)S(1)} %slice.38), channel_id=1, source_target_pairs={{4,0},{8,4},{12,8},{0,12},{5,1},{9,5},{13,9},{1,13},{6,2},{10,6},{... | collective-permute-start | bytes 589832 | tf_op jit(solution)/shard_map/ppermute | solution.py:275
  60.8 2.4 %collective-permute-start.3 = (bf16[4,2,8,1536]{3,2,1,0:T(8,128)(2,1)S(1)}, bf16[4,2,8,1536]{3,2,1,0:T(8,128)(2,1)S(1)}, u32[]{:S(2)}, u32[]{:S(2)}) collective-permute-start(bf16[4,2,8,1536]{3,2,1,0:T(8,128)(2,1)S(1)} %slice.38), channel_id=1, source_target_pairs={{8,0},{12,4},{0,8},{4,12},{9,1},{13,5},{1,9},{5,13},{10,2},{14,6},... | collective-permute-start | bytes 589832 | tf_op jit(solution)/shard_map/ppermute | solution.py:275
  63.2 2.5 %collective-permute-start.4 = (bf16[4,2,8,1536]{3,2,1,0:T(8,128)(2,1)S(1)}, bf16[4,2,8,1536]{3,2,1,0:T(8,128)(2,1)S(1)}, u32[]{:S(2)}, u32[]{:S(2)}) collective-permute-start(bf16[4,2,8,1536]{3,2,1,0:T(8,128)(2,1)S(1)} %slice.38), channel_id=1, source_target_pairs={{12,0},{0,4},{4,8},{8,12},{13,1},{1,5},{5,9},{9,13},{14,2},{2,6},{... | collective-permute-start | bytes 589832 | tf_op jit(solution)/shard_map/ppermute | solution.py:275
  65.7 7.7 %collective-permute-start.5 = (bf16[144,256]{1,0:T(8,128)(2,1)S(1)}, bf16[144,256]{1,0:T(8,128)(2,1)S(1)}, u32[]{:S(2)}, u32[]{:S(2)}) collective-permute-start(bf16[144,256]{1,0:T(8,128)(2,1)S(1)} %get-tuple-element.61), channel_id=1, source_target_pairs={{2,4},{6,8},{10,12},{14,0},{4,2},{8,6},{12,10},{0,14},{3,5},{7,9},... | collective-permute-start | bytes 221192 | tf_op jit(solution)/shard_map/ppermute | solution.py:331
  73.6 1.0 pad_maximum_fusion.first
  74.6 15.6 %collective-permute-done.5 = bf16[144,256]{1,0:T(8,128)(2,1)S(1)} collective-permute-done((bf16[144,256]{1,0:T(8,128)(2,1)S(1)}, bf16[144,256]{1,0:T(8,128)(2,1)S(1)}, u32[]{:S(2)}, u32[]{:S(2)}) %collective-permute-start.5) | collective-permute-done | bytes 73760 | tf_op jit(solution)/shard_map/ppermute | solution.py:331
  90.1 2.1 %broadcast_in_dim.66 = bf16[4,4,4,2,8,1664]{5,4,3,2,1,0:T(8,128)(2,1)} broadcast(bf16[4,4,2,8,1664]{4,3,2,1,0:T(8,128)(2,1)S(1)} %all-to-all-done.1), dimensions={1,2,3,4,5} | broadcast | bytes 4259840 | tf_op jit(solution)/shard_map/broadcast_in_dim | solution.py:263
  92.3 4.7 %all-to-all-start.2 = ((bf16[4,4,4,2,8,1664]{5,4,3,2,1,0:T(8,128)(2,1)}), bf16[4,4,4,2,8,1664]{5,4,3,2,1,0:T(8,128)(2,1)}, u32[]{:S(2)}, u32[]{:S(2)}) async-start(bf16[4,4,4,2,8,1664]{5,4,3,2,1,0:T(8,128)(2,1)} %broadcast_in_dim.66), calls=%async_computation.2 | async-start | bytes 6815744 | tf_op jit(solution)/shard_map/all_to_all | solution.py:264
  97.2 0.9 compare_select_fusion.bias
  98.1 0.9 fusion.row_order
  99.1 0.6 shard_map.183
  99.7 3.2 %collective-permute-start.6 = (bf16[216,256]{1,0:T(8,128)(2,1)S(1)}, bf16[216,256]{1,0:T(8,128)(2,1)S(1)}, u32[]{:S(2)}, u32[]{:S(2)}) collective-permute-start(bf16[216,256]{1,0:T(8,128)(2,1)S(1)} %get-tuple-element.41), channel_id=1, source_target_pairs={{0,16},{16,32},{32,48},{48,64},{64,80},{80,96},{96,112},{112,128},... | collective-permute-start | bytes 331784 | tf_op jit(solution)/shard_map/ppermute | solution.py:281
  103.0 2.2 %collective-permute-start.7 = (bf16[216,256]{1,0:T(8,128)(2,1)S(1)}, bf16[216,256]{1,0:T(8,128)(2,1)S(1)}, u32[]{:S(2)}, u32[]{:S(2)}) collective-permute-start(bf16[216,256]{1,0:T(8,128)(2,1)S(1)} %get-tuple-element.42), channel_id=1, source_target_pairs={{0,496},{16,0},{32,16},{48,32},{64,48},{80,64},{96,80},{112,96},{1... | collective-permute-start | bytes 331784 | tf_op jit(solution)/shard_map/ppermute | solution.py:281
  105.2 3.1 %collective-permute-start.10 = (bf16[4,64,1536]{2,1,0:T(8,128)(2,1)}, bf16[4,64,1536]{2,1,0:T(8,128)(2,1)}, u32[]{:S(2)}, u32[]{:S(2)}) collective-permute-start(bf16[4,64,1536]{2,1,0:T(8,128)(2,1)} %pad_maximum_fusion.first), channel_id=1, source_target_pairs={{48,0},{0,16},{16,32},{32,48},{49,1},{1,17},{17,33},{33,49},{50,2}... | collective-permute-start | bytes 2359304 | tf_op jit(solution)/shard_map/ppermute | solution.py:275
  108.3 3.1 %collective-permute-start.8 = (bf16[4,64,1536]{2,1,0:T(8,128)(2,1)}, bf16[4,64,1536]{2,1,0:T(8,128)(2,1)}, u32[]{:S(2)}, u32[]{:S(2)}) collective-permute-start(bf16[4,64,1536]{2,1,0:T(8,128)(2,1)} %pad_maximum_fusion.first), channel_id=1, source_target_pairs={{16,0},{32,16},{48,32},{0,48},{17,1},{33,17},{49,33},{1,49},{18,2}... | collective-permute-start | bytes 2359304 | tf_op jit(solution)/shard_map/ppermute | solution.py:275
  111.4 3.7 %collective-permute-start.9 = (bf16[4,64,1536]{2,1,0:T(8,128)(2,1)}, bf16[4,64,1536]{2,1,0:T(8,128)(2,1)}, u32[]{:S(2)}, u32[]{:S(2)}) collective-permute-start(bf16[4,64,1536]{2,1,0:T(8,128)(2,1)} %pad_maximum_fusion.first), channel_id=1, source_target_pairs={{32,0},{48,16},{0,32},{16,48},{33,1},{49,17},{1,33},{17,49},{34,2}... | collective-permute-start | bytes 2359304 | tf_op jit(solution)/shard_map/ppermute | solution.py:275
  115.1 5.2 %all_gather.29.rims = bf16[720,512]{1,0:T(8,128)(2,1)S(1)} all-gather(bf16[720,256]{1,0:T(8,128)(2,1)S(1)} %pad_maximum_fusion.1), channel_id=1, replica_groups=mesh['za'=2,'zq'=4,'x'=4,'y'=4,'zh'=2,'core'=2] {'core'}, dimensions={1}, use_global_device_ids=true | all-gather | bytes 1105920 | tf_op jit(solution)/shard_map/all_gather | solution.py:352
  120.3 4.7 %shard_map.184.windows = bf16[9,144,512]{2,1,0:T(8,128)(2,1)S(1)} custom-call(bf16[576,512]{1,0:T(8,128)(2,1)S(1)} %copy-done.1, bf16[720,512]{1,0:T(8,128)(2,1)S(1)} %all_gather.29.rims, s32[9,144,1]{2,1,0:T(8,128)S(1)} %copy-done.5), custom_call_target="tpu_custom_call" | custom-call | flops 100000000 | bytes 1048576 | tf_op jit(solution)/shard_map/pallas_call | solution.py:112
  125.0 9.8 %all-to-all-done.2 = bf16[4,4,4,2,8,1664]{5,4,3,2,1,0:T(8,128)(2,1)} async-done(((bf16[4,4,4,2,8,1664]{5,4,3,2,1,0:T(8,128)(2,1)}), bf16[4,4,4,2,8,1664]{5,4,3,2,1,0:T(8,128)(2,1)}, u32[]{:S(2)}, u32[]{:S(2)}) %all-to-all-start.2) | async-done | bytes 3407904 | tf_op jit(solution)/shard_map/all_to_all | solution.py:264
  134.8 1.8 slice_bitcast_fusion.1
  137.0 1.4 slice.51
  138.8 0.7 copy-done.4
  139.5 8.7 %shard_map.185 = bf16[576,256]{1,0:T(8,128)(2,1)S(1)} custom-call(bf16[9,144,512]{2,1,0:T(8,128)(2,1)S(1)} %shard_map.184.windows, bf16[512,640]{1,0:T(8,128)(2,1)S(1)} %bitcast.55, bf16[512,640]{1,0:T(8,128)(2,1)S(1)} %bitcast.53, f32[3,144,144]{2,1,0:T(8,128)S(1)} %copy-done.4, s32[9,1,144]{2,1,0:T(1,128)S(1)} %copy-done.11), custom_call_target="tpu_custom_call" | custom-call | flops 100000000 | bytes 1048576 | tf_op jit(solution)/shard_map/pallas_call | solution.py:112
  148.2 5.4 %all_gather.30.heads = bf16[576,512]{1,0:T(8,128)(2,1)S(1)} all-gather(bf16[576,256]{1,0:T(8,128)(2,1)S(1)} %shard_map.185), channel_id=1, replica_groups=mesh['za'=2,'zq'=4,'x'=4,'y'=4,'zh'=2,'core'=2] {'core'}, dimensions={1}, use_global_device_ids=true | all-gather | bytes 884736 | tf_op jit(solution)/shard_map/all_gather | solution.py:392
  153.7 1.4 shard_map.186
  155.5 2.0 %all_gather.31.coarse = bf16[144,1024]{1,0:T(8,128)(2,1)S(1)} all-gather(bf16[144,512]{1,0:T(8,128)(2,1)S(1)} %convolution_convert_fusion.1), channel_id=1, replica_groups=mesh['za'=2,'zq'=4,'x'=4,'y'=4,'zh'=2,'core'=2] {'core'}, dimensions={1}, use_global_device_ids=true | all-gather | bytes 442368 | tf_op jit(solution)/shard_map/all_gather | solution.py:401
  157.6 5.3 %shard_map.187 = bf16[4,144,128]{2,1,0:T(8,128)(2,1)S(1)} custom-call(s32[4]{0:T(128)S(1)} %and_select_fusion.order, bf16[144,1024]{1,0:T(8,128)(2,1)S(1)} %all_gather.31.coarse, f32[1,1024]{1,0:T(1,128)S(1)} %bitcast.60, bf16[1024,1024]{1,0:T(8,128)(2,1)S(1)} %fusion.row_order, bf16[4,64,1536]{2,1,0:T(8,128)(2,1)} %pad_maximum_fusion.first, ...), custom_call_target="tpu_custom_call" | custom-call | flops 100000000 | bytes 1048576 | tf_op jit(solution)/shard_map/pallas_call | solution.py:112
  163.4 2.2 %all-gather.1 = bf16[288,1024]{1,0:T(8,128)(2,1)S(1)} all-gather(bf16[144,1024]{1,0:T(8,128)(2,1)S(1)} %convolution_convert_fusion), channel_id=3, replica_groups=mesh['za'=2,'zq'=4,'x'=4,'y'=4,'zh'=2,'core'=2] {'core'}, dimensions={0}, use_global_device_ids=true | all-gather | bytes 884736 | tf_op jit(solution)/shard_map/all_gather | solution.py:423
  165.8 0.5 fusion.1.expanded
  167.2 1.9 %all-gather.2 = f32[2,144,8]{1,2,0:T(8,128)S(1)} all-gather(f32[1,144,8]{1,2,0:T(8,128)S(1)} %maximum_bitcast_fusion.1), channel_id=1, replica_groups=mesh['za'=2,'zq'=4,'x'=4,'y'=4,'zh'=2,'core'=2] {'core'}, dimensions={0}, use_global_device_ids=true | all-gather | bytes 13824 | tf_op jit(solution)/shard_map/all_gather | solution.py:428
  169.2 1.7 shard_map.188
  (83 shorter events, 3.4 us)
Async XLA Ops:
  6.5 23.0 %copy-start.9 = (s32[144,1]{1,0:T(8,128)S(1)}, s32[144,1]{1,0:T(8,128)}, u32[]{:S(2)}) copy-start(s32[144,1]{1,0:T(8,128)} %constant.177.clone.first_place) | copy-start | bytes 1732
  6.5 23.0 %copy-start.10 = (s32[144,1]{1,0:T(8,128)S(1)}, s32[144,1]{1,0:T(8,128)}, u32[]{:S(2)}) copy-start(s32[144,1]{1,0:T(8,128)} %constant.178.clone.last_place) | copy-start | bytes 1732
  6.5 23.0 %copy-start.2 = (bf16[2,12,24,512]{3,2,1,0:T(8,128)(2,1)S(1)}, bf16[2,12,24,512]{3,2,1,0:T(8,128)(2,1)}, u32[]{:S(2)}) copy-start(bf16[2,12,24,512]{3,2,1,0:T(8,128)(2,1)} %param.19) | copy-start | bytes 1769476
  6.5 23.0 %copy-start.15 = (f32[512]{0:T(512)S(1)}, f32[512]{0:T(512)}, u32[]{:S(2)}) copy-start(f32[512]{0:T(512)} %param.20) | copy-start | bytes 6148
  6.5 42.1 %all-gather.8.cloned.1.call-start = ((), (), s32[]{:S(2)}) async-start(), calls=%async_computation.4 | async-start | bytes 1351680 | tf_op jit(solution)/shard_map/all_gather | solution.py:324
  6.6 1.0 copy-start.17
  7.5 0.8 copy-start.18
  8.4 0.8 copy-start.19
  9.2 0.8 copy-start.20
  10.0 0.7 copy-start.21
  10.7 0.7 copy-start.22
  12.3 10.8 %collective-permute-start = (bf16[8,3200]{1,0:T(8,128)(2,1)S(1)}, bf16[8,3200]{1,0:T(8,128)(2,1)S(1)}, u32[]{:S(2)}, u32[]{:S(2)}) collective-permute-start(bf16[8,3200]{1,0:T(8,128)(2,1)S(1)} %get-tuple-element.33), channel_id=1, source_target_pairs={{0,256},{256,0},{1,257},{257,1},{2,258},{258,2},{3,259},{259,3},{4... | collective-permute-start | bytes 153608 | tf_op jit(solution)/shard_map/ppermute | solution.py:268
  23.9 26.5 %all-to-all-start = ((bf16[4,2,8,3200]{3,2,1,0:T(8,128)(2,1)}), bf16[4,2,8,3200]{3,2,1,0:T(8,128)(2,1)S(1)}, u32[]{:S(2)}, u32[]{:S(2)}) async-start(bf16[4,2,8,3200]{3,2,1,0:T(8,128)(2,1)} %broadcast_in_dim.64), calls=%async_computation | async-start | bytes 819200 | tf_op jit(solution)/shard_map/all_to_all | solution.py:264
  29.5 128.1 %all-gather.6.cloned.1.call-start = ((), (), s32[]{:S(2)}) async-start(), calls=%async_computation.3 | async-start | bytes 3538944 | tf_op jit(solution)/shard_map/all_gather | solution.py:333
  30.2 68.8 %copy-start = (bf16[576,512]{1,0:T(8,128)(2,1)}, bf16[576,512]{1,0:T(8,128)(2,1)S(1)}, u32[]{:S(2)}) copy-start(bf16[576,512]{1,0:T(8,128)(2,1)S(1)} %get-tuple-element.32.normed) | copy-start | bytes 1769476
  30.2 20.2 %collective-permute-start.1 = (bf16[144,256]{1,0:T(8,128)(2,1)S(1)}, bf16[144,256]{1,0:T(8,128)(2,1)S(1)}, u32[]{:S(2)}, u32[]{:S(2)}) collective-permute-start(bf16[144,256]{1,0:T(8,128)(2,1)S(1)} %get-tuple-element.62), channel_id=1, source_target_pairs={{0,2},{2,0},{1,3},{3,1},{4,6},{6,4},{5,7},{7,5},{8,10},{10,8},{9,1... | collective-permute-start | bytes 221192 | tf_op jit(solution)/shard_map/ppermute | solution.py:328
  51.5 38.6 %all-to-all-start.1 = ((bf16[4,4,2,8,1664]{4,3,2,1,0:T(8,128)(2,1)}), bf16[4,4,2,8,1664]{4,3,2,1,0:T(8,128)(2,1)S(1)}, u32[]{:S(2)}, u32[]{:S(2)}) async-start(bf16[4,4,2,8,1664]{4,3,2,1,0:T(8,128)(2,1)} %broadcast_in_dim.65), calls=%async_computation.1 | async-start | bytes 1703936 | tf_op jit(solution)/shard_map/all_to_all | solution.py:264
  56.4 17.1 %collective-permute-start.2 = (bf16[4,2,8,1536]{3,2,1,0:T(8,128)(2,1)S(1)}, bf16[4,2,8,1536]{3,2,1,0:T(8,128)(2,1)S(1)}, u32[]{:S(2)}, u32[]{:S(2)}) collective-permute-start(bf16[4,2,8,1536]{3,2,1,0:T(8,128)(2,1)S(1)} %slice.38), channel_id=1, source_target_pairs={{4,0},{8,4},{12,8},{0,12},{5,1},{9,5},{13,9},{1,13},{6,2},{10,6},{... | collective-permute-start | bytes 589832 | tf_op jit(solution)/shard_map/ppermute | solution.py:275
  60.8 12.7 %collective-permute-start.3 = (bf16[4,2,8,1536]{3,2,1,0:T(8,128)(2,1)S(1)}, bf16[4,2,8,1536]{3,2,1,0:T(8,128)(2,1)S(1)}, u32[]{:S(2)}, u32[]{:S(2)}) collective-permute-start(bf16[4,2,8,1536]{3,2,1,0:T(8,128)(2,1)S(1)} %slice.38), channel_id=1, source_target_pairs={{8,0},{12,4},{0,8},{4,12},{9,1},{13,5},{1,9},{5,13},{10,2},{14,6},... | collective-permute-start | bytes 589832 | tf_op jit(solution)/shard_map/ppermute | solution.py:275
  63.2 10.4 %collective-permute-start.4 = (bf16[4,2,8,1536]{3,2,1,0:T(8,128)(2,1)S(1)}, bf16[4,2,8,1536]{3,2,1,0:T(8,128)(2,1)S(1)}, u32[]{:S(2)}, u32[]{:S(2)}) collective-permute-start(bf16[4,2,8,1536]{3,2,1,0:T(8,128)(2,1)S(1)} %slice.38), channel_id=1, source_target_pairs={{12,0},{0,4},{4,8},{8,12},{13,1},{1,5},{5,9},{9,13},{14,2},{2,6},{... | collective-permute-start | bytes 589832 | tf_op jit(solution)/shard_map/ppermute | solution.py:275
  65.7 24.4 %collective-permute-start.5 = (bf16[144,256]{1,0:T(8,128)(2,1)S(1)}, bf16[144,256]{1,0:T(8,128)(2,1)S(1)}, u32[]{:S(2)}, u32[]{:S(2)}) collective-permute-start(bf16[144,256]{1,0:T(8,128)(2,1)S(1)} %get-tuple-element.61), channel_id=1, source_target_pairs={{2,4},{6,8},{10,12},{14,0},{4,2},{8,6},{12,10},{0,14},{3,5},{7,9},... | collective-permute-start | bytes 221192 | tf_op jit(solution)/shard_map/ppermute | solution.py:331
  92.3 42.5 %all-to-all-start.2 = ((bf16[4,4,4,2,8,1664]{5,4,3,2,1,0:T(8,128)(2,1)}), bf16[4,4,4,2,8,1664]{5,4,3,2,1,0:T(8,128)(2,1)}, u32[]{:S(2)}, u32[]{:S(2)}) async-start(bf16[4,4,4,2,8,1664]{5,4,3,2,1,0:T(8,128)(2,1)} %broadcast_in_dim.66), calls=%async_computation.2 | async-start | bytes 6815744 | tf_op jit(solution)/shard_map/all_to_all | solution.py:264
  97.0 2.1 %copy-start.7 = (s32[216,1]{1,0:T(8,128)S(1)}, s32[216,1]{1,0:T(8,128)}, u32[]{:S(2)}) copy-start(s32[216,1]{1,0:T(8,128)} %constant.179.clone.first_place) | copy-start | bytes 2596
  97.0 2.1 %copy-start.8 = (s32[216,1]{1,0:T(8,128)S(1)}, s32[216,1]{1,0:T(8,128)}, u32[]{:S(2)}) copy-start(s32[216,1]{1,0:T(8,128)} %constant.180.clone.last_place) | copy-start | bytes 2596
  98.1 22.2 %copy-start.5 = (s32[9,144,1]{2,1,0:T(8,128)S(1)}, s32[9,144,1]{2,1,0:T(8,128)}, u32[]{:S(2)}) copy-start(s32[9,144,1]{2,1,0:T(8,128)} %constant.181.clone.column) | copy-start | bytes 15556
  99.7 20.6 %copy-start.1 = (bf16[576,512]{1,0:T(8,128)(2,1)S(1)}, bf16[576,512]{1,0:T(8,128)(2,1)}, u32[]{:S(2)}) copy-start(bf16[576,512]{1,0:T(8,128)(2,1)} %copy-done) | copy-start | bytes 1769476
  99.7 15.3 %collective-permute-start.6 = (bf16[216,256]{1,0:T(8,128)(2,1)S(1)}, bf16[216,256]{1,0:T(8,128)(2,1)S(1)}, u32[]{:S(2)}, u32[]{:S(2)}) collective-permute-start(bf16[216,256]{1,0:T(8,128)(2,1)S(1)} %get-tuple-element.41), channel_id=1, source_target_pairs={{0,16},{16,32},{32,48},{48,64},{64,80},{80,96},{96,112},{112,128},... | collective-permute-start | bytes 331784 | tf_op jit(solution)/shard_map/ppermute | solution.py:281
  103.0 12.1 %collective-permute-start.7 = (bf16[216,256]{1,0:T(8,128)(2,1)S(1)}, bf16[216,256]{1,0:T(8,128)(2,1)S(1)}, u32[]{:S(2)}, u32[]{:S(2)}) collective-permute-start(bf16[216,256]{1,0:T(8,128)(2,1)S(1)} %get-tuple-element.42), channel_id=1, source_target_pairs={{0,496},{16,0},{32,16},{48,32},{64,48},{80,64},{96,80},{112,96},{1... | collective-permute-start | bytes 331784 | tf_op jit(solution)/shard_map/ppermute | solution.py:281
  105.2 52.4 %collective-permute-start.10 = (bf16[4,64,1536]{2,1,0:T(8,128)(2,1)}, bf16[4,64,1536]{2,1,0:T(8,128)(2,1)}, u32[]{:S(2)}, u32[]{:S(2)}) collective-permute-start(bf16[4,64,1536]{2,1,0:T(8,128)(2,1)} %pad_maximum_fusion.first), channel_id=1, source_target_pairs={{48,0},{0,16},{16,32},{32,48},{49,1},{1,17},{17,33},{33,49},{50,2}... | collective-permute-start | bytes 2359304 | tf_op jit(solution)/shard_map/ppermute | solution.py:275
  108.3 49.3 %collective-permute-start.8 = (bf16[4,64,1536]{2,1,0:T(8,128)(2,1)}, bf16[4,64,1536]{2,1,0:T(8,128)(2,1)}, u32[]{:S(2)}, u32[]{:S(2)}) collective-permute-start(bf16[4,64,1536]{2,1,0:T(8,128)(2,1)} %pad_maximum_fusion.first), channel_id=1, source_target_pairs={{16,0},{32,16},{48,32},{0,48},{17,1},{33,17},{49,33},{1,49},{18,2}... | collective-permute-start | bytes 2359304 | tf_op jit(solution)/shard_map/ppermute | solution.py:275
  111.4 46.2 %collective-permute-start.9 = (bf16[4,64,1536]{2,1,0:T(8,128)(2,1)}, bf16[4,64,1536]{2,1,0:T(8,128)(2,1)}, u32[]{:S(2)}, u32[]{:S(2)}) collective-permute-start(bf16[4,64,1536]{2,1,0:T(8,128)(2,1)} %pad_maximum_fusion.first), channel_id=1, source_target_pairs={{32,0},{48,16},{0,32},{16,48},{33,1},{49,17},{1,33},{17,49},{34,2}... | collective-permute-start | bytes 2359304 | tf_op jit(solution)/shard_map/ppermute | solution.py:275
  138.5 1.0 copy-start.4
  138.5 1.0 copy-start.11
  139.5 14.2 %copy-start.3 = (bf16[2,12,24,512]{3,2,1,0:T(8,128)(2,1)S(1)}, bf16[2,12,24,512]{3,2,1,0:T(8,128)(2,1)}, u32[]{:S(2)}) copy-start(bf16[2,12,24,512]{3,2,1,0:T(8,128)(2,1)} %param.19) | copy-start | bytes 1769476
  139.5 14.2 %copy-start.6 = (s32[4,144,1]{2,1,0:T(8,128)S(1)}, s32[4,144,1]{2,1,0:T(8,128)}, u32[]{:S(2)}) copy-start(s32[4,144,1]{2,1,0:T(8,128)} %constant.183.clone.places) | copy-start | bytes 6916
  139.5 14.2 %copy-start.12 = (f32[2048]{0:T(1024)S(1)}, f32[2048]{0:T(1024)}, u32[]{:S(2)}) copy-start(f32[2048]{0:T(1024)} %param.23) | copy-start | bytes 24580
  155.0 2.6 %copy-start.13 = (f32[1024]{0:T(1024)S(1)}, f32[1024]{0:T(1024)}, u32[]{:S(2)}) copy-start(f32[1024]{0:T(1024)} %param.25) | copy-start | bytes 12292
  157.6 5.3 %copy-start.23 = (bf16[1024,1536]{1,0:T(8,128)(2,1)S(1)}, bf16[1024,1536]{1,0:T(8,128)(2,1)}, u32[]{:S(2)}) copy-start(bf16[1024,1536]{1,0:T(8,128)(2,1)} %all-gather.6.cloned.1.call-done) | copy-start | bytes 9437188
  165.8 3.4 %copy-start.14 = (s32[4,1,144]{2,1,0:T(1,128)S(1)}, s32[4,1,144]{2,1,0:T(1,128)}, u32[]{:S(2)}) copy-start(s32[4,1,144]{2,1,0:T(1,128)} %constant.184.clone.places) | copy-start | bytes 6916
  165.8 3.4 %copy-start.16 = (f32[512]{0:T(512)S(1)}, f32[512]{0:T(512)}, u32[]{:S(2)}) copy-start(f32[512]{0:T(512)} %param.29) | copy-start | bytes 6148
Sparse Core Ops, SparseCore 0:
  14.3 34.2 all-gather.7
  50.7 86.6 all-gather.5

commit v7 on v6

--- a/solution.py
+++ b/solution.py
@@ -329,13 +329,12 @@
     perm = [(2 * i + 1, (2 * i + 2) % 8) for i in range(4)]
     perm += [(there, here) for here, there in perm]
     next_row = lax.ppermute(jnp.where(even, first_cols, last_cols), ("y", "zh"), perm)
-    depth, late, same_row = lax.optimization_barrier((depth, late, same_row))
+    depth, same_row = lax.optimization_barrier((depth, same_row))
+    merge_side = sent_to_all(depth[..., :1664], "x")
+    depth, late = lax.optimization_barrier((depth, late))
     late = lax.all_gather(late, ("za", "zq"), axis=0, tiled=True)
-    merge_side = sent_to_all(depth[..., :1664], "x")
     qkv_quad = jnp.stack(from_others(depth[..., 1664:], "y")).reshape(4, 64, 1536)
-    merge_side, qkv_quad, same_row, next_row = lax.optimization_barrier(
-        (merge_side, qkv_quad, same_row, next_row)
-    )
+    merge_side, qkv_quad = lax.optimization_barrier((merge_side, qkv_quad))
     east = jnp.where(even, same_row, next_row)
     west = jnp.where(even, next_row, same_row)
     qkv_pieces = from_others(qkv_quad, "x")
@@ -390,6 +389,7 @@
         scratch_shapes=[pltpu.VMEM((OWN, 256), jnp.float32)],
     )
     all_heads = lax.all_gather(window_out, "core", axis=1, tiled=True)
+    all_heads, qkv_pieces = lax.optimization_barrier((all_heads, qkv_pieces))
     residual, merged_in = call(
         merge_kernel,
         (shape(OWN, 512), shape(COARSE, 2048)),

time: 179 us -> 205 us (1.15)
  the two profiles are of different devices: /device:TPU:195 before, /device:TPU:1 now
where the time goes in v7:
time: 205 us; the launch traced here: 203 us
  starting transfers between devices  87.9 us (43%)
  waiting for transfers between devices  39.5 us (19%)
  Pallas kernels  23.9 us (12%)
  blocking collectives  17.1 us (8%)
  local copies, waits for them, and re-layouts  15.8 us (8%)
  between operations  14 us (7%)
  other arithmetic  3.63 us (2%)
    pallas_call x8, Pallas kernels, call(): pl.pallas_call(kernel, out_shape=out_shape, compiler_params=pltpu.Compile...  23.9 us
    ppermute x6, starting transfers between devices, from_others(): lax.ppermute(block, axis, [((i + by) % 4, i) for i in range(4)])  23.4 us
    ppermute x6, waiting for transfers between devices, from_others(): lax.ppermute(block, axis, [((i + by) % 4, i) for i in range(4)])  22.5 us
    all_to_all x3, starting transfers between devices, sent_to_all(): return lax.all_to_all(copies, axes, split_axis=0, concat_axis=0, tiled=True)  15.6 us
    ppermute x1, starting transfers between devices, body(): lax.ppermute(jnp.where(even, first_cols, last_cols), ('y', 'zh'), perm)  15.1 us
    ppermute x2, starting transfers between devices, lat_shift(): return lax.ppermute(value, ('za', 'zq', 'x'), perm)  14.1 us
    ppermute x1, starting transfers between devices, body(): lax.ppermute(jnp.where(even, last_cols, first_cols), 'zh', [(0, 1), (1, 0)])  10 us
    ppermute x1, starting transfers between devices, depth_pair(): other = lax.ppermute(block, 'za', [(0, 1), (1, 0)])  9.63 us
  transfers between devices with their start and end apart: 16, of which 9 were waited for; matrix products, arithmetic and copies ran while one was open for 6% of the time, Pallas kernels for 8%

profile of v7, /device:TPU:1, one launch (start us, length us, event | category | flops | bytes accessed | tf_op | source)
XLA Modules:
  0.0 203.3 jit_solution(10049756000073717626)
XLA Ops:
  6.6 0.9 copy-done.17
  7.6 0.8 copy-done.18
  8.4 0.8 copy-done.19
  9.2 0.8 copy-done.20
  10.0 0.7 copy-done.21
  11.4 0.8 shard_map.181
  12.3 9.6 %collective-permute-start.1 = (bf16[8,3200]{1,0:T(8,128)(2,1)S(1)}, bf16[8,3200]{1,0:T(8,128)(2,1)S(1)}, u32[]{:S(2)}, u32[]{:S(2)}) collective-permute-start(bf16[8,3200]{1,0:T(8,128)(2,1)S(1)} %get-tuple-element.39), channel_id=1, source_target_pairs={{0,256},{256,0},{1,257},{257,1},{2,258},{258,2},{3,259},{259,3},{4... | collective-permute-start | bytes 153608 | tf_op jit(solution)/shard_map/ppermute | solution.py:268
  21.9 1.5 collective-permute-done.1
  23.4 0.8 broadcast_in_dim.64
  24.2 7.4 %all-to-all-start = ((bf16[4,2,8,3200]{3,2,1,0:T(8,128)(2,1)}), bf16[4,2,8,3200]{3,2,1,0:T(8,128)(2,1)S(1)}, u32[]{:S(2)}, u32[]{:S(2)}) async-start(bf16[4,2,8,3200]{3,2,1,0:T(8,128)(2,1)} %broadcast_in_dim.64), calls=%async_computation | async-start | bytes 819200 | tf_op jit(solution)/shard_map/all_to_all | solution.py:264
  32.4 10.0 %collective-permute-start.2 = (bf16[144,256]{1,0:T(8,128)(2,1)S(1)}, bf16[144,256]{1,0:T(8,128)(2,1)S(1)}, u32[]{:S(2)}, u32[]{:S(2)}) collective-permute-start(bf16[144,256]{1,0:T(8,128)(2,1)S(1)} %get-tuple-element.69), channel_id=1, source_target_pairs={{0,2},{2,0},{1,3},{3,1},{4,6},{6,4},{5,7},{7,5},{8,10},{10,8},{9,1... | collective-permute-start | bytes 221192 | tf_op jit(solution)/shard_map/ppermute | solution.py:328
  42.4 4.4 %collective-permute-done.2 = bf16[144,256]{1,0:T(8,128)(2,1)S(1)} collective-permute-done((bf16[144,256]{1,0:T(8,128)(2,1)S(1)}, bf16[144,256]{1,0:T(8,128)(2,1)S(1)}, u32[]{:S(2)}, u32[]{:S(2)}) %collective-permute-start.2) | collective-permute-done | bytes 73760 | tf_op jit(solution)/shard_map/ppermute | solution.py:328
  46.8 6.0 %all-gather.8.cloned.1.call-done = bf16[352,1536]{1,0:T(8,128)(2,1)} async-done(((bf16[88,1536]{1,0:T(8,128)(2,1)}), bf16[352,1536]{1,0:T(8,128)(2,1)}) %all-gather.8.cloned.1.call-update) | async-done | bytes 1081360 | tf_op jit(solution)/shard_map/all_gather | solution.py:324
  52.8 1.8 slice.50
  54.7 1.0 broadcast_in_dim.65
  55.6 3.5 %all-to-all-start.1 = ((bf16[4,4,2,8,1664]{4,3,2,1,0:T(8,128)(2,1)}), bf16[4,4,2,8,1664]{4,3,2,1,0:T(8,128)(2,1)S(1)}, u32[]{:S(2)}, u32[]{:S(2)}) async-start(bf16[4,4,2,8,1664]{4,3,2,1,0:T(8,128)(2,1)} %broadcast_in_dim.65), calls=%async_computation.1 | async-start | bytes 1703936 | tf_op jit(solution)/shard_map/all_to_all | solution.py:264
  59.2 4.4 %collective-permute-start.5 = (bf16[4,2,8,1536]{3,2,1,0:T(8,128)(2,1)S(1)}, bf16[4,2,8,1536]{3,2,1,0:T(8,128)(2,1)S(1)}, u32[]{:S(2)}, u32[]{:S(2)}) collective-permute-start(bf16[4,2,8,1536]{3,2,1,0:T(8,128)(2,1)S(1)} %slice.38), channel_id=1, source_target_pairs={{4,0},{8,4},{12,8},{0,12},{5,1},{9,5},{13,9},{1,13},{6,2},{10,6},{... | collective-permute-start | bytes 589832 | tf_op jit(solution)/shard_map/ppermute | solution.py:275
  63.5 2.4 %collective-permute-start.6 = (bf16[4,2,8,1536]{3,2,1,0:T(8,128)(2,1)S(1)}, bf16[4,2,8,1536]{3,2,1,0:T(8,128)(2,1)S(1)}, u32[]{:S(2)}, u32[]{:S(2)}) collective-permute-start(bf16[4,2,8,1536]{3,2,1,0:T(8,128)(2,1)S(1)} %slice.38), channel_id=1, source_target_pairs={{8,0},{12,4},{0,8},{4,12},{9,1},{13,5},{1,9},{5,13},{10,2},{14,6},... | collective-permute-start | bytes 589832 | tf_op jit(solution)/shard_map/ppermute | solution.py:275
  66.0 2.5 %collective-permute-start.7 = (bf16[4,2,8,1536]{3,2,1,0:T(8,128)(2,1)S(1)}, bf16[4,2,8,1536]{3,2,1,0:T(8,128)(2,1)S(1)}, u32[]{:S(2)}, u32[]{:S(2)}) collective-permute-start(bf16[4,2,8,1536]{3,2,1,0:T(8,128)(2,1)S(1)} %slice.38), channel_id=1, source_target_pairs={{12,0},{0,4},{4,8},{8,12},{13,1},{1,5},{5,9},{9,13},{14,2},{2,6},{... | collective-permute-start | bytes 589832 | tf_op jit(solution)/shard_map/ppermute | solution.py:275
  68.5 3.2 %collective-permute-done.6 = bf16[4,2,8,1536]{3,2,1,0:T(8,128)(2,1)S(1)} collective-permute-done((bf16[4,2,8,1536]{3,2,1,0:T(8,128)(2,1)S(1)}, bf16[4,2,8,1536]{3,2,1,0:T(8,128)(2,1)S(1)}, u32[]{:S(2)}, u32[]{:S(2)}) %collective-permute-start.6) | collective-permute-done | bytes 196640 | tf_op jit(solution)/shard_map/ppermute | solution.py:275
  71.8 4.9 %collective-permute-done.7 = bf16[4,2,8,1536]{3,2,1,0:T(8,128)(2,1)S(1)} collective-permute-done((bf16[4,2,8,1536]{3,2,1,0:T(8,128)(2,1)S(1)}, bf16[4,2,8,1536]{3,2,1,0:T(8,128)(2,1)S(1)}, u32[]{:S(2)}, u32[]{:S(2)}) %collective-permute-start.7) | collective-permute-done | bytes 196640 | tf_op jit(solution)/shard_map/ppermute | solution.py:275
  76.6 1.0 pad_maximum_fusion.first
  77.6 2.1 %broadcast_in_dim.66 = bf16[4,4,4,2,8,1664]{5,4,3,2,1,0:T(8,128)(2,1)} broadcast(bf16[4,4,2,8,1664]{4,3,2,1,0:T(8,128)(2,1)S(1)} %all-to-all-done.1), dimensions={1,2,3,4,5} | broadcast | bytes 4259840 | tf_op jit(solution)/shard_map/broadcast_in_dim | solution.py:263
  79.8 4.7 %all-to-all-start.2 = ((bf16[4,4,4,2,8,1664]{5,4,3,2,1,0:T(8,128)(2,1)}), bf16[4,4,4,2,8,1664]{5,4,3,2,1,0:T(8,128)(2,1)}, u32[]{:S(2)}, u32[]{:S(2)}) async-start(bf16[4,4,4,2,8,1664]{5,4,3,2,1,0:T(8,128)(2,1)} %broadcast_in_dim.66), calls=%async_computation.2 | async-start | bytes 6815744 | tf_op jit(solution)/shard_map/all_to_all | solution.py:264
  84.5 15.1 %collective-permute-start = (bf16[144,256]{1,0:T(8,128)(2,1)S(1)}, bf16[144,256]{1,0:T(8,128)(2,1)S(1)}, u32[]{:S(2)}, u32[]{:S(2)}) collective-permute-start(bf16[144,256]{1,0:T(8,128)(2,1)S(1)} %get-tuple-element.70), channel_id=1, source_target_pairs={{2,4},{6,8},{10,12},{14,0},{4,2},{8,6},{12,10},{0,14},{3,5},{7,9},... | collective-permute-start | bytes 221192 | tf_op jit(solution)/shard_map/ppermute | solution.py:331
  99.8 0.9 fusion.row_order
  100.7 0.9 compare_select_fusion.bias
  101.6 1.6 collective-permute-done
  103.9 2.9 %collective-permute-start.3 = (bf16[216,256]{1,0:T(8,128)(2,1)S(1)}, bf16[216,256]{1,0:T(8,128)(2,1)S(1)}, u32[]{:S(2)}, u32[]{:S(2)}) collective-permute-start(bf16[216,256]{1,0:T(8,128)(2,1)S(1)} %get-tuple-element.41), channel_id=1, source_target_pairs={{0,16},{16,32},{32,48},{48,64},{64,80},{80,96},{96,112},{112,128},... | collective-permute-start | bytes 331784 | tf_op jit(solution)/shard_map/ppermute | solution.py:281
  106.8 11.3 %collective-permute-start.4 = (bf16[216,256]{1,0:T(8,128)(2,1)S(1)}, bf16[216,256]{1,0:T(8,128)(2,1)S(1)}, u32[]{:S(2)}, u32[]{:S(2)}) collective-permute-start(bf16[216,256]{1,0:T(8,128)(2,1)S(1)} %get-tuple-element.42), channel_id=1, source_target_pairs={{0,496},{16,0},{32,16},{48,32},{64,48},{80,64},{96,80},{112,96},{1... | collective-permute-start | bytes 331784 | tf_op jit(solution)/shard_map/ppermute | solution.py:281
  118.1 2.5 %collective-permute-done.3 = bf16[216,256]{1,0:T(8,128)(2,1)S(1)} collective-permute-done((bf16[216,256]{1,0:T(8,128)(2,1)S(1)}, bf16[216,256]{1,0:T(8,128)(2,1)S(1)}, u32[]{:S(2)}, u32[]{:S(2)}) %collective-permute-start.3) | collective-permute-done | bytes 110624 | tf_op jit(solution)/shard_map/ppermute | solution.py:281
  120.6 0.9 collective-permute-done.4
  121.6 7.4 %all_gather.27.rims = bf16[720,512]{1,0:T(8,128)(2,1)S(1)} all-gather(bf16[720,256]{1,0:T(8,128)(2,1)S(1)} %pad_maximum_fusion.1), channel_id=1, replica_groups=mesh['za'=2,'zq'=4,'x'=4,'y'=4,'zh'=2,'core'=2] {'core'}, dimensions={1}, use_global_device_ids=true | all-gather | bytes 1105920 | tf_op jit(solution)/shard_map/all_gather | solution.py:351
  129.0 4.7 %shard_map.184.windows = bf16[9,144,512]{2,1,0:T(8,128)(2,1)S(1)} custom-call(bf16[576,512]{1,0:T(8,128)(2,1)S(1)} %copy-done.1, bf16[720,512]{1,0:T(8,128)(2,1)S(1)} %all_gather.27.rims, s32[9,144,1]{2,1,0:T(8,128)S(1)} %copy-done.5), custom_call_target="tpu_custom_call" | custom-call | flops 100000000 | bytes 1048576 | tf_op jit(solution)/shard_map/pallas_call | solution.py:112
  133.7 1.9 collective-permute-start.10
  135.6 9.1 %collective-permute-start.8 = (bf16[4,64,1536]{2,1,0:T(8,128)(2,1)}, bf16[4,64,1536]{2,1,0:T(8,128)(2,1)}, u32[]{:S(2)}, u32[]{:S(2)}) collective-permute-start(bf16[4,64,1536]{2,1,0:T(8,128)(2,1)} %pad_maximum_fusion.first), channel_id=1, source_target_pairs={{16,0},{32,16},{48,32},{0,48},{17,1},{33,17},{49,33},{1,49},{18,2}... | collective-permute-start | bytes 2359304 | tf_op jit(solution)/shard_map/ppermute | solution.py:275
  144.7 3.1 %collective-permute-start.9 = (bf16[4,64,1536]{2,1,0:T(8,128)(2,1)}, bf16[4,64,1536]{2,1,0:T(8,128)(2,1)}, u32[]{:S(2)}, u32[]{:S(2)}) collective-permute-start(bf16[4,64,1536]{2,1,0:T(8,128)(2,1)} %pad_maximum_fusion.first), channel_id=1, source_target_pairs={{32,0},{48,16},{0,32},{16,48},{33,1},{49,17},{1,33},{17,49},{34,2}... | collective-permute-start | bytes 2359304 | tf_op jit(solution)/shard_map/ppermute | solution.py:275
  147.8 1.8 slice_bitcast_fusion.1
  150.0 1.4 slice.51
  152.5 8.7 %shard_map.185 = bf16[576,256]{1,0:T(8,128)(2,1)S(1)} custom-call(bf16[9,144,512]{2,1,0:T(8,128)(2,1)S(1)} %shard_map.184.windows, bf16[512,640]{1,0:T(8,128)(2,1)S(1)} %bitcast.55, bf16[512,640]{1,0:T(8,128)(2,1)S(1)} %bitcast.53, f32[3,144,144]{2,1,0:T(8,128)S(1)} %copy-done.4, s32[9,1,144]{2,1,0:T(1,128)S(1)} %copy-done.11), custom_call_target="tpu_custom_call" | custom-call | flops 100000000 | bytes 1048576 | tf_op jit(solution)/shard_map/pallas_call | solution.py:112
  161.2 2.8 %all_gather.30.heads = bf16[576,512]{1,0:T(8,128)(2,1)S(1)} all-gather(bf16[576,256]{1,0:T(8,128)(2,1)S(1)} %shard_map.185), channel_id=1, replica_groups=mesh['za'=2,'zq'=4,'x'=4,'y'=4,'zh'=2,'core'=2] {'core'}, dimensions={1}, use_global_device_ids=true | all-gather | bytes 884736 | tf_op jit(solution)/shard_map/all_gather | solution.py:391
  164.0 14.4 %collective-permute-done.8.second = bf16[4,64,1536]{2,1,0:T(8,128)(2,1)} collective-permute-done((bf16[4,64,1536]{2,1,0:T(8,128)(2,1)}, bf16[4,64,1536]{2,1,0:T(8,128)(2,1)}, u32[]{:S(2)}, u32[]{:S(2)}) %collective-permute-start.8) | collective-permute-done | bytes 786464 | tf_op jit(solution)/shard_map/ppermute | solution.py:275
  178.4 1.4 shard_map.186
  180.3 2.8 %all_gather.31.coarse = bf16[144,1024]{1,0:T(8,128)(2,1)S(1)} all-gather(bf16[144,512]{1,0:T(8,128)(2,1)S(1)} %convolution_convert_fusion.1), channel_id=1, replica_groups=mesh['za'=2,'zq'=4,'x'=4,'y'=4,'zh'=2,'core'=2] {'core'}, dimensions={1}, use_global_device_ids=true | all-gather | bytes 442368 | tf_op jit(solution)/shard_map/all_gather | solution.py:401
  183.2 5.3 %shard_map.187 = bf16[4,144,128]{2,1,0:T(8,128)(2,1)S(1)} custom-call(s32[4]{0:T(128)S(1)} %and_select_fusion.order, bf16[144,1024]{1,0:T(8,128)(2,1)S(1)} %all_gather.31.coarse, f32[1,1024]{1,0:T(1,128)S(1)} %bitcast.60, bf16[1024,1024]{1,0:T(8,128)(2,1)S(1)} %fusion.row_order, bf16[4,64,1536]{2,1,0:T(8,128)(2,1)} %pad_maximum_fusion.first, ...), custom_call_target="tpu_custom_call" | custom-call | flops 100000000 | bytes 1048576 | tf_op jit(solution)/shard_map/pallas_call | solution.py:112
  188.9 2.2 %all-gather.1 = bf16[288,1024]{1,0:T(8,128)(2,1)S(1)} all-gather(bf16[144,1024]{1,0:T(8,128)(2,1)S(1)} %convolution_convert_fusion), channel_id=3, replica_groups=mesh['za'=2,'zq'=4,'x'=4,'y'=4,'zh'=2,'core'=2] {'core'}, dimensions={0}, use_global_device_ids=true | all-gather | bytes 884736 | tf_op jit(solution)/shard_map/all_gather | solution.py:423
  192.7 1.9 all-gather.2
  194.7 1.7 shard_map.188
  (83 shorter events, 6.5 us)
Async XLA Ops:
  6.5 25.1 %copy-start.9 = (s32[144,1]{1,0:T(8,128)S(1)}, s32[144,1]{1,0:T(8,128)}, u32[]{:S(2)}) copy-start(s32[144,1]{1,0:T(8,128)} %constant.177.clone.first_place) | copy-start | bytes 1732
  6.5 25.1 %copy-start.10 = (s32[144,1]{1,0:T(8,128)S(1)}, s32[144,1]{1,0:T(8,128)}, u32[]{:S(2)}) copy-start(s32[144,1]{1,0:T(8,128)} %constant.178.clone.last_place) | copy-start | bytes 1732
  6.5 25.1 %copy-start.2 = (bf16[2,12,24,512]{3,2,1,0:T(8,128)(2,1)S(1)}, bf16[2,12,24,512]{3,2,1,0:T(8,128)(2,1)}, u32[]{:S(2)}) copy-start(bf16[2,12,24,512]{3,2,1,0:T(8,128)(2,1)} %param.19) | copy-start | bytes 1769476
  6.5 25.1 %copy-start.15 = (f32[512]{0:T(512)S(1)}, f32[512]{0:T(512)}, u32[]{:S(2)}) copy-start(f32[512]{0:T(512)} %param.20) | copy-start | bytes 6148
  6.5 46.3 %all-gather.8.cloned.1.call-start = ((), (), s32[]{:S(2)}) async-start(), calls=%async_computation.4 | async-start | bytes 1351680 | tf_op jit(solution)/shard_map/all_gather | solution.py:324
  6.6 1.0 copy-start.17
  7.5 0.8 copy-start.18
  8.4 0.8 copy-start.19
  9.2 0.8 copy-start.20
  10.0 0.7 copy-start.21
  10.7 0.7 copy-start.22
  12.3 11.1 %collective-permute-start.1 = (bf16[8,3200]{1,0:T(8,128)(2,1)S(1)}, bf16[8,3200]{1,0:T(8,128)(2,1)S(1)}, u32[]{:S(2)}, u32[]{:S(2)}) collective-permute-start(bf16[8,3200]{1,0:T(8,128)(2,1)S(1)} %get-tuple-element.39), channel_id=1, source_target_pairs={{0,256},{256,0},{1,257},{257,1},{2,258},{258,2},{3,259},{259,3},{4... | collective-permute-start | bytes 153608 | tf_op jit(solution)/shard_map/ppermute | solution.py:268
  24.2 22.6 %all-to-all-start = ((bf16[4,2,8,3200]{3,2,1,0:T(8,128)(2,1)}), bf16[4,2,8,3200]{3,2,1,0:T(8,128)(2,1)S(1)}, u32[]{:S(2)}, u32[]{:S(2)}) async-start(bf16[4,2,8,3200]{3,2,1,0:T(8,128)(2,1)} %broadcast_in_dim.64), calls=%async_computation | async-start | bytes 819200 | tf_op jit(solution)/shard_map/all_to_all | solution.py:264
  31.6 151.5 %all-gather.6.cloned.1.call-start = ((), (), s32[]{:S(2)}) async-start(), calls=%async_computation.3 | async-start | bytes 3538944 | tf_op jit(solution)/shard_map/all_gather | solution.py:335
  32.3 70.9 %copy-start = (bf16[576,512]{1,0:T(8,128)(2,1)}, bf16[576,512]{1,0:T(8,128)(2,1)S(1)}, u32[]{:S(2)}) copy-start(bf16[576,512]{1,0:T(8,128)(2,1)S(1)} %get-tuple-element.36.normed) | copy-start | bytes 1769476
  32.4 14.5 %collective-permute-start.2 = (bf16[144,256]{1,0:T(8,128)(2,1)S(1)}, bf16[144,256]{1,0:T(8,128)(2,1)S(1)}, u32[]{:S(2)}, u32[]{:S(2)}) collective-permute-start(bf16[144,256]{1,0:T(8,128)(2,1)S(1)} %get-tuple-element.69), channel_id=1, source_target_pairs={{0,2},{2,0},{1,3},{3,1},{4,6},{6,4},{5,7},{7,5},{8,10},{10,8},{9,1... | collective-permute-start | bytes 221192 | tf_op jit(solution)/shard_map/ppermute | solution.py:328
  55.6 22.0 %all-to-all-start.1 = ((bf16[4,4,2,8,1664]{4,3,2,1,0:T(8,128)(2,1)}), bf16[4,4,2,8,1664]{4,3,2,1,0:T(8,128)(2,1)S(1)}, u32[]{:S(2)}, u32[]{:S(2)}) async-start(bf16[4,4,2,8,1664]{4,3,2,1,0:T(8,128)(2,1)} %broadcast_in_dim.65), calls=%async_computation.1 | async-start | bytes 1703936 | tf_op jit(solution)/shard_map/all_to_all | solution.py:264
  59.2 9.3 %collective-permute-start.5 = (bf16[4,2,8,1536]{3,2,1,0:T(8,128)(2,1)S(1)}, bf16[4,2,8,1536]{3,2,1,0:T(8,128)(2,1)S(1)}, u32[]{:S(2)}, u32[]{:S(2)}) collective-permute-start(bf16[4,2,8,1536]{3,2,1,0:T(8,128)(2,1)S(1)} %slice.38), channel_id=1, source_target_pairs={{4,0},{8,4},{12,8},{0,12},{5,1},{9,5},{13,9},{1,13},{6,2},{10,6},{... | collective-permute-start | bytes 589832 | tf_op jit(solution)/shard_map/ppermute | solution.py:275
  63.5 8.2 %collective-permute-start.6 = (bf16[4,2,8,1536]{3,2,1,0:T(8,128)(2,1)S(1)}, bf16[4,2,8,1536]{3,2,1,0:T(8,128)(2,1)S(1)}, u32[]{:S(2)}, u32[]{:S(2)}) collective-permute-start(bf16[4,2,8,1536]{3,2,1,0:T(8,128)(2,1)S(1)} %slice.38), channel_id=1, source_target_pairs={{8,0},{12,4},{0,8},{4,12},{9,1},{13,5},{1,9},{5,13},{10,2},{14,6},... | collective-permute-start | bytes 589832 | tf_op jit(solution)/shard_map/ppermute | solution.py:275
  66.0 10.6 %collective-permute-start.7 = (bf16[4,2,8,1536]{3,2,1,0:T(8,128)(2,1)S(1)}, bf16[4,2,8,1536]{3,2,1,0:T(8,128)(2,1)S(1)}, u32[]{:S(2)}, u32[]{:S(2)}) collective-permute-start(bf16[4,2,8,1536]{3,2,1,0:T(8,128)(2,1)S(1)} %slice.38), channel_id=1, source_target_pairs={{12,0},{0,4},{4,8},{8,12},{13,1},{1,5},{5,9},{9,13},{14,2},{2,6},{... | collective-permute-start | bytes 589832 | tf_op jit(solution)/shard_map/ppermute | solution.py:275
  79.8 68.0 %all-to-all-start.2 = ((bf16[4,4,4,2,8,1664]{5,4,3,2,1,0:T(8,128)(2,1)}), bf16[4,4,4,2,8,1664]{5,4,3,2,1,0:T(8,128)(2,1)}, u32[]{:S(2)}, u32[]{:S(2)}) async-start(bf16[4,4,4,2,8,1664]{5,4,3,2,1,0:T(8,128)(2,1)} %broadcast_in_dim.66), calls=%async_computation.2 | async-start | bytes 6815744 | tf_op jit(solution)/shard_map/all_to_all | solution.py:264
  84.5 18.8 %copy-start.7 = (s32[216,1]{1,0:T(8,128)S(1)}, s32[216,1]{1,0:T(8,128)}, u32[]{:S(2)}) copy-start(s32[216,1]{1,0:T(8,128)} %constant.179.clone.first_place) | copy-start | bytes 2596
  84.5 18.8 %copy-start.8 = (s32[216,1]{1,0:T(8,128)S(1)}, s32[216,1]{1,0:T(8,128)}, u32[]{:S(2)}) copy-start(s32[216,1]{1,0:T(8,128)} %constant.180.clone.last_place) | copy-start | bytes 2596
  84.5 18.7 %collective-permute-start = (bf16[144,256]{1,0:T(8,128)(2,1)S(1)}, bf16[144,256]{1,0:T(8,128)(2,1)S(1)}, u32[]{:S(2)}, u32[]{:S(2)}) collective-permute-start(bf16[144,256]{1,0:T(8,128)(2,1)S(1)} %get-tuple-element.70), channel_id=1, source_target_pairs={{2,4},{6,8},{10,12},{14,0},{4,2},{8,6},{12,10},{0,14},{3,5},{7,9},... | collective-permute-start | bytes 221192 | tf_op jit(solution)/shard_map/ppermute | solution.py:331
  100.7 28.3 %copy-start.5 = (s32[9,144,1]{2,1,0:T(8,128)S(1)}, s32[9,144,1]{2,1,0:T(8,128)}, u32[]{:S(2)}) copy-start(s32[9,144,1]{2,1,0:T(8,128)} %constant.181.clone.column) | copy-start | bytes 15556
  103.9 25.1 %copy-start.1 = (bf16[576,512]{1,0:T(8,128)(2,1)S(1)}, bf16[576,512]{1,0:T(8,128)(2,1)}, u32[]{:S(2)}) copy-start(bf16[576,512]{1,0:T(8,128)(2,1)} %copy-done) | copy-start | bytes 1769476
  103.9 16.7 %collective-permute-start.3 = (bf16[216,256]{1,0:T(8,128)(2,1)S(1)}, bf16[216,256]{1,0:T(8,128)(2,1)S(1)}, u32[]{:S(2)}, u32[]{:S(2)}) collective-permute-start(bf16[216,256]{1,0:T(8,128)(2,1)S(1)} %get-tuple-element.41), channel_id=1, source_target_pairs={{0,16},{16,32},{32,48},{48,64},{64,80},{80,96},{96,112},{112,128},... | collective-permute-start | bytes 331784 | tf_op jit(solution)/shard_map/ppermute | solution.py:281
  106.8 14.8 %collective-permute-start.4 = (bf16[216,256]{1,0:T(8,128)(2,1)S(1)}, bf16[216,256]{1,0:T(8,128)(2,1)S(1)}, u32[]{:S(2)}, u32[]{:S(2)}) collective-permute-start(bf16[216,256]{1,0:T(8,128)(2,1)S(1)} %get-tuple-element.42), channel_id=1, source_target_pairs={{0,496},{16,0},{32,16},{48,32},{64,48},{80,64},{96,80},{112,96},{1... | collective-permute-start | bytes 331784 | tf_op jit(solution)/shard_map/ppermute | solution.py:281
  133.7 30.3 %collective-permute-start.10 = (bf16[4,64,1536]{2,1,0:T(8,128)(2,1)}, bf16[4,64,1536]{2,1,0:T(8,128)(2,1)}, u32[]{:S(2)}, u32[]{:S(2)}) collective-permute-start(bf16[4,64,1536]{2,1,0:T(8,128)(2,1)} %pad_maximum_fusion.first), channel_id=1, source_target_pairs={{48,0},{0,16},{16,32},{32,48},{49,1},{1,17},{17,33},{33,49},{50,2}... | collective-permute-start | bytes 2359304 | tf_op jit(solution)/shard_map/ppermute | solution.py:275
  135.6 42.8 %collective-permute-start.8 = (bf16[4,64,1536]{2,1,0:T(8,128)(2,1)}, bf16[4,64,1536]{2,1,0:T(8,128)(2,1)}, u32[]{:S(2)}, u32[]{:S(2)}) collective-permute-start(bf16[4,64,1536]{2,1,0:T(8,128)(2,1)} %pad_maximum_fusion.first), channel_id=1, source_target_pairs={{16,0},{32,16},{48,32},{0,48},{17,1},{33,17},{49,33},{1,49},{18,2}... | collective-permute-start | bytes 2359304 | tf_op jit(solution)/shard_map/ppermute | solution.py:275
  144.7 33.7 %collective-permute-start.9 = (bf16[4,64,1536]{2,1,0:T(8,128)(2,1)}, bf16[4,64,1536]{2,1,0:T(8,128)(2,1)}, u32[]{:S(2)}, u32[]{:S(2)}) collective-permute-start(bf16[4,64,1536]{2,1,0:T(8,128)(2,1)} %pad_maximum_fusion.first), channel_id=1, source_target_pairs={{32,0},{48,16},{0,32},{16,48},{33,1},{49,17},{1,33},{17,49},{34,2}... | collective-permute-start | bytes 2359304 | tf_op jit(solution)/shard_map/ppermute | solution.py:275
  151.5 1.0 copy-start.4
  151.5 1.0 copy-start.11
  152.5 25.9 %copy-start.3 = (bf16[2,12,24,512]{3,2,1,0:T(8,128)(2,1)S(1)}, bf16[2,12,24,512]{3,2,1,0:T(8,128)(2,1)}, u32[]{:S(2)}) copy-start(bf16[2,12,24,512]{3,2,1,0:T(8,128)(2,1)} %param.19) | copy-start | bytes 1769476
  152.5 25.9 %copy-start.6 = (s32[4,144,1]{2,1,0:T(8,128)S(1)}, s32[4,144,1]{2,1,0:T(8,128)}, u32[]{:S(2)}) copy-start(s32[4,144,1]{2,1,0:T(8,128)} %constant.183.clone.places) | copy-start | bytes 6916
  152.5 25.9 %copy-start.12 = (f32[2048]{0:T(1024)S(1)}, f32[2048]{0:T(1024)}, u32[]{:S(2)}) copy-start(f32[2048]{0:T(1024)} %param.23) | copy-start | bytes 24580
  179.8 3.3 %copy-start.13 = (f32[1024]{0:T(1024)S(1)}, f32[1024]{0:T(1024)}, u32[]{:S(2)}) copy-start(f32[1024]{0:T(1024)} %param.25) | copy-start | bytes 12292
  183.2 5.3 %copy-start.23 = (bf16[1024,1536]{1,0:T(8,128)(2,1)S(1)}, bf16[1024,1536]{1,0:T(8,128)(2,1)}, u32[]{:S(2)}) copy-start(bf16[1024,1536]{1,0:T(8,128)(2,1)} %all-gather.6.cloned.1.call-done) | copy-start | bytes 9437188
  191.3 3.4 %copy-start.14 = (s32[4,1,144]{2,1,0:T(1,128)S(1)}, s32[4,1,144]{2,1,0:T(1,128)}, u32[]{:S(2)}) copy-start(s32[4,1,144]{2,1,0:T(1,128)} %constant.184.clone.places) | copy-start | bytes 6916
  191.3 3.4 %copy-start.16 = (f32[512]{0:T(512)S(1)}, f32[512]{0:T(512)}, u32[]{:S(2)}) copy-start(f32[512]{0:T(512)} %param.29) | copy-start | bytes 6148
Sparse Core Ops, SparseCore 0:
  22.1 30.7 all-gather.7
  54.9 93.9 all-gather.5

commit v8 on v7

--- a/solution.py
+++ b/solution.py
@@ -334,7 +334,9 @@
     depth, late = lax.optimization_barrier((depth, late))
     late = lax.all_gather(late, ("za", "zq"), axis=0, tiled=True)
     qkv_quad = jnp.stack(from_others(depth[..., 1664:], "y")).reshape(4, 64, 1536)
-    merge_side, qkv_quad = lax.optimization_barrier((merge_side, qkv_quad))
+    merge_side, qkv_quad, same_row, next_row = lax.optimization_barrier(
+        (merge_side, qkv_quad, same_row, next_row)
+    )
     east = jnp.where(even, same_row, next_row)
     west = jnp.where(even, next_row, same_row)
     qkv_pieces = from_others(qkv_quad, "x")
@@ -389,7 +391,6 @@
         scratch_shapes=[pltpu.VMEM((OWN, 256), jnp.float32)],
     )
     all_heads = lax.all_gather(window_out, "core", axis=1, tiled=True)
-    all_heads, qkv_pieces = lax.optimization_barrier((all_heads, qkv_pieces))
     residual, merged_in = call(
         merge_kernel,
         (shape(OWN, 512), shape(COARSE, 2048)),

time: 205 us -> 180 us (0.88)
  the two profiles are of different devices: /device:TPU:1 before, /device:TPU:195 now
where the time goes in v8:
time: 180 us; the launch traced here: 179 us
  starting transfers between devices  58.1 us (32%)
  waiting for transfers between devices  46.4 us (26%)
  Pallas kernels  23.9 us (13%)
  local copies, waits for them, and re-layouts  15.8 us (9%)
  blocking collectives  15.7 us (9%)
  between operations  14 us (8%)
  other arithmetic  3.64 us (2%)
    pallas_call x8, Pallas kernels, call(): pl.pallas_call(kernel, out_shape=out_shape, compiler_params=pltpu.Compile...  23.9 us
    ppermute x6, starting transfers between devices, from_others(): lax.ppermute(block, axis, [((i + by) % 4, i) for i in range(4)])  18.5 us
    ppermute x1, waiting for transfers between devices, body(): lax.ppermute(jnp.where(even, first_cols, last_cols), ('y', 'zh'), perm)  15.5 us
    all_to_all x3, starting transfers between devices, sent_to_all(): return lax.all_to_all(copies, axes, split_axis=0, concat_axis=0, tiled=True)  14.7 us
    all_to_all x3, waiting for transfers between devices, sent_to_all(): return lax.all_to_all(copies, axes, split_axis=0, concat_axis=0, tiled=True)  11.6 us
    ppermute x1, waiting for transfers between devices, body(): lax.ppermute(jnp.where(even, last_cols, first_cols), 'zh', [(0, 1), (1, 0)])  10.4 us
    ppermute x1, starting transfers between devices, body(): lax.ppermute(jnp.where(even, first_cols, last_cols), ('y', 'zh'), perm)  8.99 us
    ppermute x1, waiting for transfers between devices, depth_pair(): other = lax.ppermute(block, 'za', [(0, 1), (1, 0)])  8.87 us
  transfers between devices with their start and end apart: 16, of which 4 were waited for; matrix products, arithmetic and copies ran while one was open for 6% of the time, Pallas kernels for 9%

profile of v8, /device:TPU:195, one launch (start us, length us, event | category | flops | bytes accessed | tf_op | source)
XLA Modules:
  0.0 178.9 jit_solution(9793149681376716573)
XLA Ops:
  6.6 0.9 copy-done.17
  7.6 0.8 copy-done.18
  8.4 0.8 copy-done.19
  9.2 0.8 copy-done.20
  10.0 0.7 copy-done.21
  10.7 0.7 copy-done.22
  11.4 0.8 shard_map.181
  12.3 1.9 %collective-permute-start = (bf16[8,3200]{1,0:T(8,128)(2,1)S(1)}, bf16[8,3200]{1,0:T(8,128)(2,1)S(1)}, u32[]{:S(2)}, u32[]{:S(2)}) collective-permute-start(bf16[8,3200]{1,0:T(8,128)(2,1)S(1)} %get-tuple-element.34), channel_id=1, source_target_pairs={{0,256},{256,0},{1,257},{257,1},{2,258},{258,2},{3,259},{259,3},{4... | collective-permute-start | bytes 153608 | tf_op jit(solution)/shard_map/ppermute | solution.py:268
  14.2 8.9 %collective-permute-done = bf16[8,3200]{1,0:T(8,128)(2,1)S(1)} collective-permute-done((bf16[8,3200]{1,0:T(8,128)(2,1)S(1)}, bf16[8,3200]{1,0:T(8,128)(2,1)S(1)}, u32[]{:S(2)}, u32[]{:S(2)}) %collective-permute-start) | collective-permute-done | bytes 51232 | tf_op jit(solution)/shard_map/ppermute | solution.py:268
  23.1 0.8 broadcast_in_dim.64
  23.9 5.6 %all-to-all-start = ((bf16[4,2,8,3200]{3,2,1,0:T(8,128)(2,1)}), bf16[4,2,8,3200]{3,2,1,0:T(8,128)(2,1)S(1)}, u32[]{:S(2)}, u32[]{:S(2)}) async-start(bf16[4,2,8,3200]{3,2,1,0:T(8,128)(2,1)} %broadcast_in_dim.64), calls=%async_computation | async-start | bytes 819200 | tf_op jit(solution)/shard_map/all_to_all | solution.py:264
  29.5 0.7 shard_map.182
  30.2 8.6 %collective-permute-start.1 = (bf16[144,256]{1,0:T(8,128)(2,1)S(1)}, bf16[144,256]{1,0:T(8,128)(2,1)S(1)}, u32[]{:S(2)}, u32[]{:S(2)}) collective-permute-start(bf16[144,256]{1,0:T(8,128)(2,1)S(1)} %get-tuple-element.64), channel_id=1, source_target_pairs={{0,2},{2,0},{1,3},{3,1},{4,6},{6,4},{5,7},{7,5},{8,10},{10,8},{9,1... | collective-permute-start | bytes 221192 | tf_op jit(solution)/shard_map/ppermute | solution.py:328
  38.8 10.4 %collective-permute-done.1 = bf16[144,256]{1,0:T(8,128)(2,1)S(1)} collective-permute-done((bf16[144,256]{1,0:T(8,128)(2,1)S(1)}, bf16[144,256]{1,0:T(8,128)(2,1)S(1)}, u32[]{:S(2)}, u32[]{:S(2)}) %collective-permute-start.1) | collective-permute-done | bytes 73760 | tf_op jit(solution)/shard_map/ppermute | solution.py:328
  49.2 1.8 slice.50
  51.0 1.0 broadcast_in_dim.65
  52.0 4.4 %all-to-all-start.1 = ((bf16[4,4,2,8,1664]{4,3,2,1,0:T(8,128)(2,1)}), bf16[4,4,2,8,1664]{4,3,2,1,0:T(8,128)(2,1)S(1)}, u32[]{:S(2)}, u32[]{:S(2)}) async-start(bf16[4,4,2,8,1664]{4,3,2,1,0:T(8,128)(2,1)} %broadcast_in_dim.65), calls=%async_computation.1 | async-start | bytes 1703936 | tf_op jit(solution)/shard_map/all_to_all | solution.py:264
  56.4 4.6 %collective-permute-start.2 = (bf16[4,2,8,1536]{3,2,1,0:T(8,128)(2,1)S(1)}, bf16[4,2,8,1536]{3,2,1,0:T(8,128)(2,1)S(1)}, u32[]{:S(2)}, u32[]{:S(2)}) collective-permute-start(bf16[4,2,8,1536]{3,2,1,0:T(8,128)(2,1)S(1)} %slice.38), channel_id=1, source_target_pairs={{4,0},{8,4},{12,8},{0,12},{5,1},{9,5},{13,9},{1,13},{6,2},{10,6},{... | collective-permute-start | bytes 589832 | tf_op jit(solution)/shard_map/ppermute | solution.py:275
  60.9 2.3 %collective-permute-start.3 = (bf16[4,2,8,1536]{3,2,1,0:T(8,128)(2,1)S(1)}, bf16[4,2,8,1536]{3,2,1,0:T(8,128)(2,1)S(1)}, u32[]{:S(2)}, u32[]{:S(2)}) collective-permute-start(bf16[4,2,8,1536]{3,2,1,0:T(8,128)(2,1)S(1)} %slice.38), channel_id=1, source_target_pairs={{8,0},{12,4},{0,8},{4,12},{9,1},{13,5},{1,9},{5,13},{10,2},{14,6},... | collective-permute-start | bytes 589832 | tf_op jit(solution)/shard_map/ppermute | solution.py:275
  63.2 2.6 %collective-permute-start.4 = (bf16[4,2,8,1536]{3,2,1,0:T(8,128)(2,1)S(1)}, bf16[4,2,8,1536]{3,2,1,0:T(8,128)(2,1)S(1)}, u32[]{:S(2)}, u32[]{:S(2)}) collective-permute-start(bf16[4,2,8,1536]{3,2,1,0:T(8,128)(2,1)S(1)} %slice.38), channel_id=1, source_target_pairs={{12,0},{0,4},{4,8},{8,12},{13,1},{1,5},{5,9},{9,13},{14,2},{2,6},{... | collective-permute-start | bytes 589832 | tf_op jit(solution)/shard_map/ppermute | solution.py:275
  65.8 9.0 %collective-permute-start.5 = (bf16[144,256]{1,0:T(8,128)(2,1)S(1)}, bf16[144,256]{1,0:T(8,128)(2,1)S(1)}, u32[]{:S(2)}, u32[]{:S(2)}) collective-permute-start(bf16[144,256]{1,0:T(8,128)(2,1)S(1)} %get-tuple-element.63), channel_id=1, source_target_pairs={{2,4},{6,8},{10,12},{14,0},{4,2},{8,6},{12,10},{0,14},{3,5},{7,9},... | collective-permute-start | bytes 221192 | tf_op jit(solution)/shard_map/ppermute | solution.py:331
  74.8 1.0 pad_maximum_fusion.first
  75.8 15.5 %collective-permute-done.5 = bf16[144,256]{1,0:T(8,128)(2,1)S(1)} collective-permute-done((bf16[144,256]{1,0:T(8,128)(2,1)S(1)}, bf16[144,256]{1,0:T(8,128)(2,1)S(1)}, u32[]{:S(2)}, u32[]{:S(2)}) %collective-permute-start.5) | collective-permute-done | bytes 73760 | tf_op jit(solution)/shard_map/ppermute | solution.py:331
  91.3 2.1 %broadcast_in_dim.66 = bf16[4,4,4,2,8,1664]{5,4,3,2,1,0:T(8,128)(2,1)} broadcast(bf16[4,4,2,8,1664]{4,3,2,1,0:T(8,128)(2,1)S(1)} %all-to-all-done.1), dimensions={1,2,3,4,5} | broadcast | bytes 4259840 | tf_op jit(solution)/shard_map/broadcast_in_dim | solution.py:263
  93.5 4.7 %all-to-all-start.2 = ((bf16[4,4,4,2,8,1664]{5,4,3,2,1,0:T(8,128)(2,1)}), bf16[4,4,4,2,8,1664]{5,4,3,2,1,0:T(8,128)(2,1)}, u32[]{:S(2)}, u32[]{:S(2)}) async-start(bf16[4,4,4,2,8,1664]{5,4,3,2,1,0:T(8,128)(2,1)} %broadcast_in_dim.66), calls=%async_computation.2 | async-start | bytes 6815744 | tf_op jit(solution)/shard_map/all_to_all | solution.py:264
  98.4 0.9 compare_select_fusion.bias
  99.3 0.9 fusion.row_order
  100.3 0.6 shard_map.183
  100.9 3.2 %collective-permute-start.6 = (bf16[216,256]{1,0:T(8,128)(2,1)S(1)}, bf16[216,256]{1,0:T(8,128)(2,1)S(1)}, u32[]{:S(2)}, u32[]{:S(2)}) collective-permute-start(bf16[216,256]{1,0:T(8,128)(2,1)S(1)} %get-tuple-element.43), channel_id=1, source_target_pairs={{0,16},{16,32},{32,48},{48,64},{64,80},{80,96},{96,112},{112,128},... | collective-permute-start | bytes 331784 | tf_op jit(solution)/shard_map/ppermute | solution.py:281
  104.1 2.2 %collective-permute-start.7 = (bf16[216,256]{1,0:T(8,128)(2,1)S(1)}, bf16[216,256]{1,0:T(8,128)(2,1)S(1)}, u32[]{:S(2)}, u32[]{:S(2)}) collective-permute-start(bf16[216,256]{1,0:T(8,128)(2,1)S(1)} %get-tuple-element.44), channel_id=1, source_target_pairs={{0,496},{16,0},{32,16},{48,32},{64,48},{80,64},{96,80},{112,96},{1... | collective-permute-start | bytes 331784 | tf_op jit(solution)/shard_map/ppermute | solution.py:281
  106.4 3.1 %collective-permute-start.10 = (bf16[4,64,1536]{2,1,0:T(8,128)(2,1)}, bf16[4,64,1536]{2,1,0:T(8,128)(2,1)}, u32[]{:S(2)}, u32[]{:S(2)}) collective-permute-start(bf16[4,64,1536]{2,1,0:T(8,128)(2,1)} %pad_maximum_fusion.first), channel_id=1, source_target_pairs={{48,0},{0,16},{16,32},{32,48},{49,1},{1,17},{17,33},{33,49},{50,2}... | collective-permute-start | bytes 2359304 | tf_op jit(solution)/shard_map/ppermute | solution.py:275
  109.5 2.3 %collective-permute-start.8 = (bf16[4,64,1536]{2,1,0:T(8,128)(2,1)}, bf16[4,64,1536]{2,1,0:T(8,128)(2,1)}, u32[]{:S(2)}, u32[]{:S(2)}) collective-permute-start(bf16[4,64,1536]{2,1,0:T(8,128)(2,1)} %pad_maximum_fusion.first), channel_id=1, source_target_pairs={{16,0},{32,16},{48,32},{0,48},{17,1},{33,17},{49,33},{1,49},{18,2}... | collective-permute-start | bytes 2359304 | tf_op jit(solution)/shard_map/ppermute | solution.py:275
  111.8 3.7 %collective-permute-start.9 = (bf16[4,64,1536]{2,1,0:T(8,128)(2,1)}, bf16[4,64,1536]{2,1,0:T(8,128)(2,1)}, u32[]{:S(2)}, u32[]{:S(2)}) collective-permute-start(bf16[4,64,1536]{2,1,0:T(8,128)(2,1)} %pad_maximum_fusion.first), channel_id=1, source_target_pairs={{32,0},{48,16},{0,32},{16,48},{33,1},{49,17},{1,33},{17,49},{34,2}... | collective-permute-start | bytes 2359304 | tf_op jit(solution)/shard_map/ppermute | solution.py:275
  115.6 5.2 %all_gather.29.rims = bf16[720,512]{1,0:T(8,128)(2,1)S(1)} all-gather(bf16[720,256]{1,0:T(8,128)(2,1)S(1)} %pad_maximum_fusion.1), channel_id=1, replica_groups=mesh['za'=2,'zq'=4,'x'=4,'y'=4,'zh'=2,'core'=2] {'core'}, dimensions={1}, use_global_device_ids=true | all-gather | bytes 1105920 | tf_op jit(solution)/shard_map/all_gather | solution.py:353
  120.7 4.7 %shard_map.184.windows = bf16[9,144,512]{2,1,0:T(8,128)(2,1)S(1)} custom-call(bf16[576,512]{1,0:T(8,128)(2,1)S(1)} %copy-done.1, bf16[720,512]{1,0:T(8,128)(2,1)S(1)} %all_gather.29.rims, s32[9,144,1]{2,1,0:T(8,128)S(1)} %copy-done.5), custom_call_target="tpu_custom_call" | custom-call | flops 100000000 | bytes 1048576 | tf_op jit(solution)/shard_map/pallas_call | solution.py:112
  125.4 11.6 %all-to-all-done.2 = bf16[4,4,4,2,8,1664]{5,4,3,2,1,0:T(8,128)(2,1)} async-done(((bf16[4,4,4,2,8,1664]{5,4,3,2,1,0:T(8,128)(2,1)}), bf16[4,4,4,2,8,1664]{5,4,3,2,1,0:T(8,128)(2,1)}, u32[]{:S(2)}, u32[]{:S(2)}) %all-to-all-start.2) | async-done | bytes 3407904 | tf_op jit(solution)/shard_map/all_to_all | solution.py:264
  137.0 1.8 slice_bitcast_fusion.1
  139.3 1.4 slice.51
  141.0 0.7 copy-done.4
  141.7 8.7 %shard_map.185 = bf16[576,256]{1,0:T(8,128)(2,1)S(1)} custom-call(bf16[9,144,512]{2,1,0:T(8,128)(2,1)S(1)} %shard_map.184.windows, bf16[512,640]{1,0:T(8,128)(2,1)S(1)} %bitcast.55, bf16[512,640]{1,0:T(8,128)(2,1)S(1)} %bitcast.53, f32[3,144,144]{2,1,0:T(8,128)S(1)} %copy-done.4, s32[9,1,144]{2,1,0:T(1,128)S(1)} %copy-done.11), custom_call_target="tpu_custom_call" | custom-call | flops 100000000 | bytes 1048576 | tf_op jit(solution)/shard_map/pallas_call | solution.py:112
  150.5 4.4 %all_gather.30.heads = bf16[576,512]{1,0:T(8,128)(2,1)S(1)} all-gather(bf16[576,256]{1,0:T(8,128)(2,1)S(1)} %shard_map.185), channel_id=1, replica_groups=mesh['za'=2,'zq'=4,'x'=4,'y'=4,'zh'=2,'core'=2] {'core'}, dimensions={1}, use_global_device_ids=true | all-gather | bytes 884736 | tf_op jit(solution)/shard_map/all_gather | solution.py:393
  154.9 1.4 shard_map.186
  156.8 2.0 %all_gather.31.coarse = bf16[144,1024]{1,0:T(8,128)(2,1)S(1)} all-gather(bf16[144,512]{1,0:T(8,128)(2,1)S(1)} %convolution_convert_fusion.1), channel_id=1, replica_groups=mesh['za'=2,'zq'=4,'x'=4,'y'=4,'zh'=2,'core'=2] {'core'}, dimensions={1}, use_global_device_ids=true | all-gather | bytes 442368 | tf_op jit(solution)/shard_map/all_gather | solution.py:402
  158.8 5.3 %shard_map.187 = bf16[4,144,128]{2,1,0:T(8,128)(2,1)S(1)} custom-call(s32[4]{0:T(128)S(1)} %and_select_fusion.order, bf16[144,1024]{1,0:T(8,128)(2,1)S(1)} %all_gather.31.coarse, f32[1,1024]{1,0:T(1,128)S(1)} %bitcast.60, bf16[1024,1024]{1,0:T(8,128)(2,1)S(1)} %fusion.row_order, bf16[4,64,1536]{2,1,0:T(8,128)(2,1)} %pad_maximum_fusion.first, ...), custom_call_target="tpu_custom_call" | custom-call | flops 100000000 | bytes 1048576 | tf_op jit(solution)/shard_map/pallas_call | solution.py:112
  164.6 2.2 %all-gather.1 = bf16[288,1024]{1,0:T(8,128)(2,1)S(1)} all-gather(bf16[144,1024]{1,0:T(8,128)(2,1)S(1)} %convolution_convert_fusion), channel_id=3, replica_groups=mesh['za'=2,'zq'=4,'x'=4,'y'=4,'zh'=2,'core'=2] {'core'}, dimensions={0}, use_global_device_ids=true | all-gather | bytes 884736 | tf_op jit(solution)/shard_map/all_gather | solution.py:424
  167.0 0.5 fusion.1.expanded
  168.4 1.9 %all-gather.2 = f32[2,144,8]{1,2,0:T(8,128)S(1)} all-gather(f32[1,144,8]{1,2,0:T(8,128)S(1)} %maximum_bitcast_fusion.1), channel_id=1, replica_groups=mesh['za'=2,'zq'=4,'x'=4,'y'=4,'zh'=2,'core'=2] {'core'}, dimensions={0}, use_global_device_ids=true | all-gather | bytes 13824 | tf_op jit(solution)/shard_map/all_gather | solution.py:429
  170.4 1.7 shard_map.188
  (83 shorter events, 3.3 us)
Async XLA Ops:
  6.5 23.0 %copy-start.9 = (s32[144,1]{1,0:T(8,128)S(1)}, s32[144,1]{1,0:T(8,128)}, u32[]{:S(2)}) copy-start(s32[144,1]{1,0:T(8,128)} %constant.177.clone.first_place) | copy-start | bytes 1732
  6.5 23.0 %copy-start.10 = (s32[144,1]{1,0:T(8,128)S(1)}, s32[144,1]{1,0:T(8,128)}, u32[]{:S(2)}) copy-start(s32[144,1]{1,0:T(8,128)} %constant.178.clone.last_place) | copy-start | bytes 1732
  6.5 23.0 %copy-start.2 = (bf16[2,12,24,512]{3,2,1,0:T(8,128)(2,1)S(1)}, bf16[2,12,24,512]{3,2,1,0:T(8,128)(2,1)}, u32[]{:S(2)}) copy-start(bf16[2,12,24,512]{3,2,1,0:T(8,128)(2,1)} %param.19) | copy-start | bytes 1769476
  6.5 23.0 %copy-start.15 = (f32[512]{0:T(512)S(1)}, f32[512]{0:T(512)}, u32[]{:S(2)}) copy-start(f32[512]{0:T(512)} %param.20) | copy-start | bytes 6148
  6.5 42.7 %all-gather.8.cloned.1.call-start = ((), (), s32[]{:S(2)}) async-start(), calls=%async_computation.4 | async-start | bytes 1351680 | tf_op jit(solution)/shard_map/all_gather | solution.py:324
  6.6 1.0 copy-start.17
  7.5 0.8 copy-start.18
  8.4 0.8 copy-start.19
  9.2 0.8 copy-start.20
  10.0 0.7 copy-start.21
  10.7 0.7 copy-start.22
  12.3 10.8 %collective-permute-start = (bf16[8,3200]{1,0:T(8,128)(2,1)S(1)}, bf16[8,3200]{1,0:T(8,128)(2,1)S(1)}, u32[]{:S(2)}, u32[]{:S(2)}) collective-permute-start(bf16[8,3200]{1,0:T(8,128)(2,1)S(1)} %get-tuple-element.34), channel_id=1, source_target_pairs={{0,256},{256,0},{1,257},{257,1},{2,258},{258,2},{3,259},{259,3},{4... | collective-permute-start | bytes 153608 | tf_op jit(solution)/shard_map/ppermute | solution.py:268
  23.9 25.3 %all-to-all-start = ((bf16[4,2,8,3200]{3,2,1,0:T(8,128)(2,1)}), bf16[4,2,8,3200]{3,2,1,0:T(8,128)(2,1)S(1)}, u32[]{:S(2)}, u32[]{:S(2)}) async-start(bf16[4,2,8,3200]{3,2,1,0:T(8,128)(2,1)} %broadcast_in_dim.64), calls=%async_computation | async-start | bytes 819200 | tf_op jit(solution)/shard_map/all_to_all | solution.py:264
  29.5 129.3 %all-gather.6.cloned.1.call-start = ((), (), s32[]{:S(2)}) async-start(), calls=%async_computation.3 | async-start | bytes 3538944 | tf_op jit(solution)/shard_map/all_gather | solution.py:335
  30.2 70.0 %copy-start = (bf16[576,512]{1,0:T(8,128)(2,1)}, bf16[576,512]{1,0:T(8,128)(2,1)S(1)}, u32[]{:S(2)}) copy-start(bf16[576,512]{1,0:T(8,128)(2,1)S(1)} %get-tuple-element.33.normed) | copy-start | bytes 1769476
  30.2 18.9 %collective-permute-start.1 = (bf16[144,256]{1,0:T(8,128)(2,1)S(1)}, bf16[144,256]{1,0:T(8,128)(2,1)S(1)}, u32[]{:S(2)}, u32[]{:S(2)}) collective-permute-start(bf16[144,256]{1,0:T(8,128)(2,1)S(1)} %get-tuple-element.64), channel_id=1, source_target_pairs={{0,2},{2,0},{1,3},{3,1},{4,6},{6,4},{5,7},{7,5},{8,10},{10,8},{9,1... | collective-permute-start | bytes 221192 | tf_op jit(solution)/shard_map/ppermute | solution.py:328
  52.0 39.3 %all-to-all-start.1 = ((bf16[4,4,2,8,1664]{4,3,2,1,0:T(8,128)(2,1)}), bf16[4,4,2,8,1664]{4,3,2,1,0:T(8,128)(2,1)S(1)}, u32[]{:S(2)}, u32[]{:S(2)}) async-start(bf16[4,4,2,8,1664]{4,3,2,1,0:T(8,128)(2,1)} %broadcast_in_dim.65), calls=%async_computation.1 | async-start | bytes 1703936 | tf_op jit(solution)/shard_map/all_to_all | solution.py:264
  56.4 18.4 %collective-permute-start.2 = (bf16[4,2,8,1536]{3,2,1,0:T(8,128)(2,1)S(1)}, bf16[4,2,8,1536]{3,2,1,0:T(8,128)(2,1)S(1)}, u32[]{:S(2)}, u32[]{:S(2)}) collective-permute-start(bf16[4,2,8,1536]{3,2,1,0:T(8,128)(2,1)S(1)} %slice.38), channel_id=1, source_target_pairs={{4,0},{8,4},{12,8},{0,12},{5,1},{9,5},{13,9},{1,13},{6,2},{10,6},{... | collective-permute-start | bytes 589832 | tf_op jit(solution)/shard_map/ppermute | solution.py:275
  60.9 13.9 %collective-permute-start.3 = (bf16[4,2,8,1536]{3,2,1,0:T(8,128)(2,1)S(1)}, bf16[4,2,8,1536]{3,2,1,0:T(8,128)(2,1)S(1)}, u32[]{:S(2)}, u32[]{:S(2)}) collective-permute-start(bf16[4,2,8,1536]{3,2,1,0:T(8,128)(2,1)S(1)} %slice.38), channel_id=1, source_target_pairs={{8,0},{12,4},{0,8},{4,12},{9,1},{13,5},{1,9},{5,13},{10,2},{14,6},... | collective-permute-start | bytes 589832 | tf_op jit(solution)/shard_map/ppermute | solution.py:275
  63.2 11.6 %collective-permute-start.4 = (bf16[4,2,8,1536]{3,2,1,0:T(8,128)(2,1)S(1)}, bf16[4,2,8,1536]{3,2,1,0:T(8,128)(2,1)S(1)}, u32[]{:S(2)}, u32[]{:S(2)}) collective-permute-start(bf16[4,2,8,1536]{3,2,1,0:T(8,128)(2,1)S(1)} %slice.38), channel_id=1, source_target_pairs={{12,0},{0,4},{4,8},{8,12},{13,1},{1,5},{5,9},{9,13},{14,2},{2,6},{... | collective-permute-start | bytes 589832 | tf_op jit(solution)/shard_map/ppermute | solution.py:275
  65.8 25.5 %collective-permute-start.5 = (bf16[144,256]{1,0:T(8,128)(2,1)S(1)}, bf16[144,256]{1,0:T(8,128)(2,1)S(1)}, u32[]{:S(2)}, u32[]{:S(2)}) collective-permute-start(bf16[144,256]{1,0:T(8,128)(2,1)S(1)} %get-tuple-element.63), channel_id=1, source_target_pairs={{2,4},{6,8},{10,12},{14,0},{4,2},{8,6},{12,10},{0,14},{3,5},{7,9},... | collective-permute-start | bytes 221192 | tf_op jit(solution)/shard_map/ppermute | solution.py:331
  93.5 43.6 %all-to-all-start.2 = ((bf16[4,4,4,2,8,1664]{5,4,3,2,1,0:T(8,128)(2,1)}), bf16[4,4,4,2,8,1664]{5,4,3,2,1,0:T(8,128)(2,1)}, u32[]{:S(2)}, u32[]{:S(2)}) async-start(bf16[4,4,4,2,8,1664]{5,4,3,2,1,0:T(8,128)(2,1)} %broadcast_in_dim.66), calls=%async_computation.2 | async-start | bytes 6815744 | tf_op jit(solution)/shard_map/all_to_all | solution.py:264
  98.2 2.1 %copy-start.7 = (s32[216,1]{1,0:T(8,128)S(1)}, s32[216,1]{1,0:T(8,128)}, u32[]{:S(2)}) copy-start(s32[216,1]{1,0:T(8,128)} %constant.179.clone.first_place) | copy-start | bytes 2596
  98.2 2.1 %copy-start.8 = (s32[216,1]{1,0:T(8,128)S(1)}, s32[216,1]{1,0:T(8,128)}, u32[]{:S(2)}) copy-start(s32[216,1]{1,0:T(8,128)} %constant.180.clone.last_place) | copy-start | bytes 2596
  99.3 21.4 %copy-start.5 = (s32[9,144,1]{2,1,0:T(8,128)S(1)}, s32[9,144,1]{2,1,0:T(8,128)}, u32[]{:S(2)}) copy-start(s32[9,144,1]{2,1,0:T(8,128)} %constant.181.clone.column) | copy-start | bytes 15556
  100.9 19.8 %copy-start.1 = (bf16[576,512]{1,0:T(8,128)(2,1)S(1)}, bf16[576,512]{1,0:T(8,128)(2,1)}, u32[]{:S(2)}) copy-start(bf16[576,512]{1,0:T(8,128)(2,1)} %copy-done) | copy-start | bytes 1769476
  100.9 14.6 %collective-permute-start.6 = (bf16[216,256]{1,0:T(8,128)(2,1)S(1)}, bf16[216,256]{1,0:T(8,128)(2,1)S(1)}, u32[]{:S(2)}, u32[]{:S(2)}) collective-permute-start(bf16[216,256]{1,0:T(8,128)(2,1)S(1)} %get-tuple-element.43), channel_id=1, source_target_pairs={{0,16},{16,32},{32,48},{48,64},{64,80},{80,96},{96,112},{112,128},... | collective-permute-start | bytes 331784 | tf_op jit(solution)/shard_map/ppermute | solution.py:281
  104.1 11.4 %collective-permute-start.7 = (bf16[216,256]{1,0:T(8,128)(2,1)S(1)}, bf16[216,256]{1,0:T(8,128)(2,1)S(1)}, u32[]{:S(2)}, u32[]{:S(2)}) collective-permute-start(bf16[216,256]{1,0:T(8,128)(2,1)S(1)} %get-tuple-element.44), channel_id=1, source_target_pairs={{0,496},{16,0},{32,16},{48,32},{64,48},{80,64},{96,80},{112,96},{1... | collective-permute-start | bytes 331784 | tf_op jit(solution)/shard_map/ppermute | solution.py:281
  106.4 52.4 %collective-permute-start.10 = (bf16[4,64,1536]{2,1,0:T(8,128)(2,1)}, bf16[4,64,1536]{2,1,0:T(8,128)(2,1)}, u32[]{:S(2)}, u32[]{:S(2)}) collective-permute-start(bf16[4,64,1536]{2,1,0:T(8,128)(2,1)} %pad_maximum_fusion.first), channel_id=1, source_target_pairs={{48,0},{0,16},{16,32},{32,48},{49,1},{1,17},{17,33},{33,49},{50,2}... | collective-permute-start | bytes 2359304 | tf_op jit(solution)/shard_map/ppermute | solution.py:275
  109.5 49.3 %collective-permute-start.8 = (bf16[4,64,1536]{2,1,0:T(8,128)(2,1)}, bf16[4,64,1536]{2,1,0:T(8,128)(2,1)}, u32[]{:S(2)}, u32[]{:S(2)}) collective-permute-start(bf16[4,64,1536]{2,1,0:T(8,128)(2,1)} %pad_maximum_fusion.first), channel_id=1, source_target_pairs={{16,0},{32,16},{48,32},{0,48},{17,1},{33,17},{49,33},{1,49},{18,2}... | collective-permute-start | bytes 2359304 | tf_op jit(solution)/shard_map/ppermute | solution.py:275
  111.8 47.0 %collective-permute-start.9 = (bf16[4,64,1536]{2,1,0:T(8,128)(2,1)}, bf16[4,64,1536]{2,1,0:T(8,128)(2,1)}, u32[]{:S(2)}, u32[]{:S(2)}) collective-permute-start(bf16[4,64,1536]{2,1,0:T(8,128)(2,1)} %pad_maximum_fusion.first), channel_id=1, source_target_pairs={{32,0},{48,16},{0,32},{16,48},{33,1},{49,17},{1,33},{17,49},{34,2}... | collective-permute-start | bytes 2359304 | tf_op jit(solution)/shard_map/ppermute | solution.py:275
  140.7 1.0 copy-start.4
  140.7 1.0 copy-start.11
  141.7 13.1 %copy-start.3 = (bf16[2,12,24,512]{3,2,1,0:T(8,128)(2,1)S(1)}, bf16[2,12,24,512]{3,2,1,0:T(8,128)(2,1)}, u32[]{:S(2)}) copy-start(bf16[2,12,24,512]{3,2,1,0:T(8,128)(2,1)} %param.19) | copy-start | bytes 1769476
  141.7 13.1 %copy-start.6 = (s32[4,144,1]{2,1,0:T(8,128)S(1)}, s32[4,144,1]{2,1,0:T(8,128)}, u32[]{:S(2)}) copy-start(s32[4,144,1]{2,1,0:T(8,128)} %constant.183.clone.places) | copy-start | bytes 6916
  141.7 13.1 %copy-start.12 = (f32[2048]{0:T(1024)S(1)}, f32[2048]{0:T(1024)}, u32[]{:S(2)}) copy-start(f32[2048]{0:T(1024)} %param.23) | copy-start | bytes 24580
  156.3 2.6 %copy-start.13 = (f32[1024]{0:T(1024)S(1)}, f32[1024]{0:T(1024)}, u32[]{:S(2)}) copy-start(f32[1024]{0:T(1024)} %param.25) | copy-start | bytes 12292
  158.8 5.3 %copy-start.23 = (bf16[1024,1536]{1,0:T(8,128)(2,1)S(1)}, bf16[1024,1536]{1,0:T(8,128)(2,1)}, u32[]{:S(2)}) copy-start(bf16[1024,1536]{1,0:T(8,128)(2,1)} %all-gather.6.cloned.1.call-done) | copy-start | bytes 9437188
  167.0 3.4 %copy-start.14 = (s32[4,1,144]{2,1,0:T(1,128)S(1)}, s32[4,1,144]{2,1,0:T(1,128)}, u32[]{:S(2)}) copy-start(s32[4,1,144]{2,1,0:T(1,128)} %constant.184.clone.places) | copy-start | bytes 6916
  167.0 3.4 %copy-start.16 = (f32[512]{0:T(512)S(1)}, f32[512]{0:T(512)}, u32[]{:S(2)}) copy-start(f32[512]{0:T(512)} %param.29) | copy-start | bytes 6148
Sparse Core Ops, SparseCore 0:
  14.3 34.2 all-gather.7
  51.1 86.2 all-gather.5
